TPU v7x, 128 devices: a whole 4x4x4 slice. The times are simulated.
128 devices in a mesh: graph: 32 (over z, y, core), mp: 4 (over x).
Axes of the slice: x: 4, y: 4, z: 4, core: 2. Of those that a mesh axis runs over, the one named last changes fastest.
Arguments:
- node_features: bfloat16 [65536, 512], P('graph'), may hold values from -6 to 6
- w_qkv: bfloat16 [3, 512, 512], P(None, None, 'mp'), may hold values from -0.25 to 0.25
- w_out: bfloat16 [512, 512], P('mp'), may hold values from -0.25 to 0.25
- head_scale: float32 [8], P('mp'), may hold values from 1 to 100
- norm_gain: float32 [512], replicated, may hold values from 0.1 to 1.9
- router: bfloat16 [512, 64], replicated, may hold values from -0.5 to 0.5
- w_gate: bfloat16 [64, 512, 2048], P('graph', None, 'mp'), may hold values from -0.25 to 0.25
- w_up: bfloat16 [64, 512, 2048], P('graph', None, 'mp'), may hold values from -0.25 to 0.25
- w_down: bfloat16 [64, 2048, 512], P('graph', 'mp'), may hold values from -0.25 to 0.25
- neighbor_blocks: int32 [512, 12], P('graph'), may hold values from 0 to 511, as said below
- expert_ids: int32 [65536, 1], P('graph'), may hold values from 0 to 63; in each aligned block of 2048 rows (0 to 2047, 2048 to 4095, ...) at most 96 rows name the same one
Outputs:
- attn_out: bfloat16 [65536, 512], P('graph', 'mp')
- layer_out: bfloat16 [65536, 512], P('graph', 'mp')
Inputs may be any that keep to these rules, and one draw needn't show every extreme that they name: `neighbor_blocks`: row b lists distinct blocks: b itself, 3 other blocks of the same index of graph (blocks of part p are p * 16 to p * 16 + 15), then 8 blocks of other parts. Among all rows of one part, at most 2 distinct blocks come from any one other part, and every part reaches 2 from some other part. `expert_ids`: among the rows of one index of graph, at most 96 name one expert, a bound that some block reaches.
All inputs are finite; a program needn't handle non-finite values.
Results may differ from a plain program's by a relative error of at most 0.012.
The roundings to bfloat16 on the way count: a program that leaves them out, or rounds other values in their place, can miss the bound.
Values may be sent and summed in bfloat16 or wider, within the bound.
No kernel may reach another device: no remote copies, remote signals or barrier semaphores. Data moves between devices by JAX's collectives and lax.ppermute only.
A program may use at most 128 MiB of HBM per device.

v0:
```python
import math

import jax
import jax.numpy as jnp
from jax import lax
from jax.sharding import PartitionSpec as P

HEAD_DIM = 64
ROWS_BLK = 128
CAP_H = 2


def unit_rms(values):
    return values * lax.rsqrt(jnp.mean(values * values, axis=-1, keepdims=True) + 1e-06)


def make_work(gate_weights, up_weights, down_weights, tokens):
    gate_part = jnp.einsum(
        "gesd,edf->gesf", tokens, gate_weights, preferred_element_type=jnp.float32
    )
    up_part = jnp.einsum("gesd,edf->gesf", tokens, up_weights, preferred_element_type=jnp.float32)
    hidden = (jax.nn.silu(gate_part) * up_part).astype(jnp.bfloat16)
    return jnp.einsum("gesf,efd->gesd", hidden, down_weights, preferred_element_type=jnp.float32)


def on_device(
    node_features,
    w_qkv,
    w_out,
    head_scale,
    norm_gain,
    router,
    w_gate,
    w_up,
    w_down,
    neighbor_blocks,
    expert_ids,
):
    graph_count = lax.axis_size("graph")
    own_part = lax.axis_index("graph")
    column_start = lax.axis_index("mp") * w_qkv.shape[2]
    rows = node_features.shape[0]
    width = node_features.shape[1]
    local_width = w_qkv.shape[2]
    local_heads = local_width // HEAD_DIM
    blocks = rows // ROWS_BLK
    query = jnp.dot(node_features, w_qkv[0], preferred_element_type=jnp.float32).reshape(
        rows, local_heads, HEAD_DIM
    )
    keys = jnp.dot(node_features, w_qkv[1], preferred_element_type=jnp.float32).reshape(
        rows, local_heads, HEAD_DIM
    )
    values = jnp.dot(node_features, w_qkv[2], preferred_element_type=jnp.float32)
    scaled = (unit_rms(query) * (head_scale / math.sqrt(HEAD_DIM))[None, :, None]).astype(
        jnp.bfloat16
    )
    key_unit = unit_rms(keys).astype(jnp.bfloat16).reshape(blocks, ROWS_BLK, local_width)
    value_rows = values.astype(jnp.bfloat16).reshape(blocks, ROWS_BLK, local_width)
    key_value = jnp.concatenate([key_unit, value_rows], axis=2)
    entries = neighbor_blocks.reshape(-1)
    owner = entries // blocks
    local_index = entries % blocks
    listed = jnp.arange(entries.shape[0], dtype=jnp.int32)
    repeated = jnp.any(
        (entries[:, None] == entries[None, :]) & (listed[None, :] < listed[:, None]), axis=1
    )
    wanted = (owner != own_part) & jnp.logical_not(repeated)
    part_ids = jnp.arange(graph_count, dtype=jnp.int32)
    owner_hit = ((owner[:, None] == part_ids[None, :]) & wanted[:, None]).astype(jnp.int32)
    position = jnp.sum((jnp.cumsum(owner_hit, axis=0) - owner_hit) * owner_hit, axis=1)
    slot_hit = (position[:, None] == jnp.arange(CAP_H, dtype=jnp.int32)[None, :]).astype(jnp.int32)
    requests = (
        jnp.sum(
            owner_hit[:, :, None] * slot_hit[:, None, :] * (local_index + 1)[:, None, None], axis=0
        )
        - 1
    )
    incoming = lax.all_to_all(requests, "graph", split_axis=0, concat_axis=0, tiled=True)
    outgoing = key_value[jnp.maximum(incoming, 0)]
    halo_rows = lax.all_to_all(outgoing, "graph", split_axis=0, concat_axis=0, tiled=True)
    halo_ids = jnp.where(requests >= 0, part_ids[:, None] * blocks + requests, -1).reshape(-1)
    pool_ids = jnp.concatenate([own_part * blocks + jnp.arange(blocks, dtype=jnp.int32), halo_ids])
    key_pool = jnp.concatenate(
        [key_value, halo_rows.reshape(-1, ROWS_BLK, 2 * local_width)], axis=0
    )
    pool_slots = jnp.arange(pool_ids.shape[0], dtype=jnp.int32)
    slot_index = jnp.sum(
        jnp.where(
            neighbor_blocks[:, :, None] == pool_ids[None, None, :], pool_slots[None, None, :], 0
        ),
        axis=2,
    )
    gathered = key_pool[slot_index].reshape(blocks, -1, 2 * local_width)
    key_part = gathered[:, :, :local_width].reshape(blocks, -1, local_heads, HEAD_DIM)
    value_part = gathered[:, :, local_width:].reshape(blocks, -1, local_heads, HEAD_DIM)
    query_blocks = scaled.reshape(blocks, ROWS_BLK, local_heads, HEAD_DIM)
    scores = jnp.einsum(
        "bqhd,bkhd->bhqk", query_blocks, key_part, preferred_element_type=jnp.float32
    )
    largest = jnp.max(scores, axis=-1, keepdims=True)
    expo = jnp.exp(scores - largest)
    weights = (expo / jnp.sum(expo, axis=-1, keepdims=True)).astype(jnp.bfloat16)
    attended = jnp.einsum(
        "bhqk,bkhd->bqhd", weights, value_part, preferred_element_type=jnp.float32
    )
    attended = attended.astype(jnp.bfloat16).reshape(rows, local_width)
    partial_value = jnp.dot(attended, w_out, preferred_element_type=jnp.float32)
    total = lax.psum(partial_value, "mp")
    mixed = node_features.astype(jnp.float32) + total
    normed = (unit_rms(mixed) * norm_gain).astype(jnp.bfloat16)
    attn_cols = lax.dynamic_slice_in_dim(total, column_start, local_width, 1)
    mixed_cols = lax.dynamic_slice_in_dim(mixed, column_start, local_width, 1)
    experts = router.shape[1]
    capacity = 3 * rows // experts
    routed = expert_ids[:, 0]
    chosen = routed[:, None] == jnp.arange(experts, dtype=jnp.int32)[None, :]
    logits = jnp.dot(normed, router, preferred_element_type=jnp.float32)
    gate = jax.nn.sigmoid(jnp.sum(jnp.where(chosen, logits, 0.0), axis=1))
    row_ids = jnp.arange(rows, dtype=jnp.int32)
    earlier = (row_ids[:, None] > row_ids[None, :]).astype(jnp.bfloat16)
    before = jnp.dot(earlier, chosen.astype(jnp.bfloat16), preferred_element_type=jnp.float32)
    rank_in = jnp.sum(jnp.where(chosen, before, 0.0), axis=1).astype(jnp.int32)
    target = routed * capacity + rank_in
    buffer = jnp.zeros((experts * capacity, width), jnp.bfloat16).at[target].set(normed)
    buffer = buffer.reshape(graph_count, w_gate.shape[0], capacity, width)
    produced = make_work(
        w_gate,
        w_up,
        w_down,
        lax.all_to_all(buffer, "graph", split_axis=0, concat_axis=0, tiled=True),
    )
    back = lax.all_to_all(
        produced.astype(jnp.bfloat16), "graph", split_axis=0, concat_axis=0, tiled=True
    ).astype(produced.dtype)
    mine = back.reshape(-1, width)[target]
    expert_cols = lax.psum_scatter(
        mine.astype(jnp.bfloat16), "mp", scatter_dimension=1, tiled=True
    ).astype(jnp.float32)
    layer_out = (mixed_cols + gate[:, None] * expert_cols).astype(jnp.bfloat16)
    return (attn_cols.astype(jnp.bfloat16), layer_out)


def solution(mesh):
    placed = (
        P("graph", None),
        P(None, None, "mp"),
        P("mp", None),
        P("mp"),
        P(),
        P(),
        P("graph", None, "mp"),
        P("graph", None, "mp"),
        P("graph", "mp", None),
        P("graph", None),
        P("graph", None),
    )
    return jax.shard_map(
        on_device,
        mesh=mesh,
        in_specs=placed,
        out_specs=(P("graph", "mp"), P("graph", "mp")),
        check_vma=False,
    )
```

profile of v0, /device:TPU:1, one launch (start us, length us, event | category | flops | bytes accessed | tf_op | source)
XLA Modules:
  0.0 512.2 jit_solution(45271411930314655)
XLA Ops:
  7.2 0.0 copy-start
  7.2 0.9 reshape.272
  8.1 0.2 fusion.52
  8.3 0.6 reduce-window.6
  8.9 0.2 slice_reduce_fusion
  9.2 0.1 bitcast_bitcast_fusion
  9.3 0.1 multiply_reduce_fusion.3
  9.4 0.7 copy.52
  10.1 9.6 %all-to-all-start = ((s32[32,1,2]{2,1,0:T(1,128)}), s32[32,1,2]{2,1,0:T(1,128)S(1)}, u32[]{:S(2)}, u32[]{:S(2)}) async-start(s32[32,1,2]{2,1,0:T(1,128)} %copy.52), calls=%async_computation | async-start | bytes 32768 | tf_op jit(solution)/shard_map/all_to_all | solution.py:78
  19.7 1.0 slice_bitcast_fusion
  20.7 0.1 copy.48
  20.8 2.3 convolution_convert_fusion
  23.2 2.6 multiply_reduce_fusion.2
  25.8 0.1 multiply_convert_fusion.2
  25.9 0.1 copy.72
  26.0 0.5 copy.49
  26.5 0.1 pad_maximum_fusion.1
  26.6 0.0 all-to-all-done
  26.7 0.1 maximum_reduce_fusion
  26.7 0.1 reshape.289
  26.8 0.4 copy-done.3
  27.3 2.8 gather_fusion
  30.1 7.6 %all-to-all-start.1 = ((bf16[32,2,128,256]{3,2,1,0:T(8,128)(2,1)}), bf16[32,2,128,256]{3,2,1,0:T(8,128)(2,1)}, u32[]{:S(2)}, u32[]{:S(2)}) async-start(bf16[32,2,128,256]{3,2,1,0:T(8,128)(2,1)} %bitcast.145), calls=%async_computation.1 | async-start | bytes 8388608 | tf_op jit(solution)/shard_map/all_to_all | solution.py:80
  37.6 0.2 all-reduce.3.cloned.1.call-start
  37.9 0.1 copy.53
  38.0 0.1 copy.54
  38.0 0.1 select_n.65
  38.2 0.1 pad_add_fusion
  38.2 0.4 select_reduce_fusion
  38.6 0.1 copy.55
  38.7 0.1 reshape.297
  38.8 0.1 copy.57
  39.0 1.9 multiply_reduce_fusion.1
  40.9 47.0 %all-to-all-done.1 = bf16[32,2,128,256]{3,2,1,0:T(8,128)(2,1)} async-done(((bf16[32,2,128,256]{3,2,1,0:T(8,128)(2,1)}), bf16[32,2,128,256]{3,2,1,0:T(8,128)(2,1)}, u32[]{:S(2)}, u32[]{:S(2)}) %all-to-all-start.1) | async-done | bytes 4194336 | tf_op jit(solution)/shard_map/all_to_all | solution.py:80
  87.9 5.5 %pad_maximum_fusion = bf16[80,128,256]{2,1,0:T(8,128)(2,1)} fusion(bf16[64,128,256]{2,1,0:T(8,128)(2,1)} %bitcast.9, bf16[16,128,128]{2,1,0:T(8,128)(2,1)} %bitcast.151, bf16[16,128,128]{2,1,0:T(8,128)(2,1)} %copy-done.3), kind=kLoop, calls=%fused_computation.24 | loop fusion | flops 15728640 | bytes 10485760 | tf_op jit(solution)/shard_map/concatenate | solution.py:83
  93.4 10.7 %gather_fusion.1 = bf16[192,128,256]{2,1,0:T(8,128)(2,1)} fusion(bf16[80,128,256]{2,1,0:T(8,128)(2,1)} %pad_maximum_fusion, s32[1024]{0:T(1024)S(1)} %pad_clamp_fusion), kind=kCustom, calls=%fused_computation.1 | custom fusion | bytes 25166592 | tf_op jit(solution)/shard_map/gather | solution.py:93
  104.2 11.7 %fusion.71 = (bf16[16,1536,128]{2,1,0:T(8,128)(2,1)}, bf16[16,1536,128]{2,1,0:T(8,128)(2,1)}) fusion(bf16[16,1536,256]{2,1,0:T(8,128)(2,1)} %bitcast.143), kind=kLoop, calls=%fused_computation.114 | loop fusion | bytes 25165824 | tf_op jit(solution)/shard_map/slice | solution.py:94
  115.9 8.7 %copy.58 = bf16[16,1536,128]{1,2,0:T(8,128)(2,1)} copy(bf16[16,1536,128]{2,1,0:T(8,128)(2,1)} %get-tuple-element.6) | data formatting | bytes 12582912 | tf_op jit(solution)/shard_map/slice | solution.py:94
  124.5 8.6 %copy.56 = bf16[16,1536,128]{1,2,0:T(8,128)(2,1)} copy(bf16[16,1536,128]{2,1,0:T(8,128)(2,1)} %get-tuple-element.7) | data formatting | bytes 12582912 | tf_op jit(solution)/shard_map/slice | solution.py:95
  133.2 7.8 %fusion.72 = f32[16,2,128]{2,1,0:T(2,128)S(1)} fusion(bf16[16,1536,2,64]{1,3,2,0:T(8,128)(2,1)} %bitcast.147, f32[2048,2,64]{0,2,1:T(8,128)} %get-tuple-element.15, f32[2]{0:T(128)S(1)} %broadcast_multiply_fusion, f32[2048,2]{0,1:T(2,128)S(1)} %add_rsqrt_fusion), kind=kOutput, calls=%fused_computation.115 | convolution fusion | flops 818677248 | bytes 7372808 | tf_op jit(solution)/shard_map/sub | solution.py:101
  141.0 12.9 %fusion.29 = bf16[16,128,2,64]{1,3,2,0:T(8,128)(2,1)} fusion(bf16[16,1536,2,64]{1,3,2,0:T(8,128)(2,1)} %bitcast.149, f32[16,2,128]{2,1,0:T(2,128)S(1)} %fusion.72, bf16[16,1536,2,64]{1,3,2,0:T(8,128)(2,1)} %bitcast.148, f32[2048,2,64]{0,2,1:T(8,128)} %get-tuple-element.15, f32[2]{0:T(128)S(1)} %broadcast_multiply_fusion, f32[2048,2]{0,1:T(2,128)S(1)} %add_rsqrt_fusion), kind=kOutput, calls=%fused_computation.39 | convolution fusion | flops 1630541312 | bytes 14188552 | tf_op jit(solution)/shard_map/bhqk,bkhd->bqhd/dot_general | solution.py:103
  153.9 1.4 copy.60
  155.3 2.7 fusion.37
  157.9 0.0 all-reduce.3.cloned.1.call-update
  158.0 1.7 fusion.31
  159.7 90.8 %all-reduce.3.cloned.1.call-done = f32[2048,512]{1,0:T(8,128)} async-done(((f32[2048,512]{1,0:T(8,128)}), f32[2048,512]{1,0:T(8,128)}) %all-reduce.3.cloned.1.call-update) | async-done | bytes 4194320 | tf_op jit(solution)/shard_map/psum | solution.py:108
  250.5 4.7 multiply_reduce_fusion
  255.2 14.8 %scatter_custom_fusion = bf16[6144,512]{1,0:T(8,128)(2,1)} fusion(s32[2048]{0:T(1024)S(1)} %bitcast.160, bf16[]{:T(256)} %constant.85.clone.1, f32[2048,512]{1,0:T(8,128)} %get-tuple-element.3, f32[512]{0:T(512)S(1)} %copy-done.9, f32[2048]{0:T(1024)S(1)} %add_rsqrt_fusion.2), kind=kCustom, calls=%fused_computation.28 | custom fusion | flops 3145728 | bytes 10496002 | tf_op jit(solution)/shard_map/scatter | solution.py:124
  270.0 81.1 %all_to_all.21 = bf16[32,2,96,512]{3,2,1,0:T(8,128)(2,1)S(1)} all-to-all(bf16[32,2,96,512]{3,2,1,0:T(8,128)(2,1)} %bitcast.144), channel_id=1, replica_groups=mesh['graph'=32,'mp'=4] {'graph'}, dimensions={0} | all-to-all | bytes 12582912 | tf_op jit(solution)/shard_map/all_to_all | solution.py:130
  351.0 2.6 copy-done.2
  353.6 6.5 %fusion.9 = f32[2,32,96,512]{3,2,1,0:T(8,128)} fusion(bf16[32,2,96,512]{3,2,1,0:T(8,128)(2,1)S(1)} %all_to_all.21, bf16[2,512,512]{2,1,0:T(8,128)(2,1)S(1)} %copy-done), kind=kOutput, calls=%fused_computation.20 | convolution fusion | flops 3221225472 | bytes 19922944 | tf_op jit(solution)/shard_map/gesd,edf->gesf/dot_general | solution.py:21
  360.1 14.0 %convert_bitcast_fusion = bf16[32,2,96,512]{3,2,0,1:T(8,128)(2,1)} fusion(f32[2,32,96,512]{3,2,1,0:T(8,128)} %fusion.9, bf16[32,2,96,512]{3,2,1,0:T(8,128)(2,1)} %copy-done.2, bf16[2,512,512]{2,1,0:T(8,128)(2,1)S(1)} %copy-done.10, bf16[2,512,512]{2,1,0:T(8,128)(2,1)S(1)} %copy-done.11), kind=kOutput, calls=%fused_computation.18 | convolution fusion | flops 6464471040 | bytes 27262976 | tf_op jit(solution)/shard_map/gesf,efd->gesd/dot_general | solution.py:23
  374.1 6.2 %copy.63 = bf16[32,2,96,512]{3,2,1,0:T(8,128)(2,1)} copy(bf16[32,2,96,512]{3,2,0,1:T(8,128)(2,1)} %convert_bitcast_fusion) | data formatting | bytes 12582912 | tf_op jit(solution)/shard_map/convert_element_type | solution.py:133
  380.2 4.9 all-to-all-start.3
  385.1 0.0 reduce-scatter.4.cloned.1.call-start
  385.2 73.0 %all-to-all-done.3 = bf16[32,2,96,512]{3,2,1,0:T(8,128)(2,1)} async-done(((bf16[32,2,96,512]{3,2,1,0:T(8,128)(2,1)}), bf16[32,2,96,512]{3,2,1,0:T(8,128)(2,1)}, u32[]{:S(2)}, u32[]{:S(2)}) %all-to-all-start.3) | async-done | bytes 6291488 | tf_op jit(solution)/shard_map/all_to_all | solution.py:132
  458.2 11.2 %gather_fusion.2 = bf16[2048,512]{1,0:T(8,128)(2,1)S(1)} fusion(bf16[6144,512]{1,0:T(8,128)(2,1)} %bitcast.118, s32[2048]{0:T(1024)S(1)} %broadcast_clamp_fusion), kind=kCustom, calls=%fused_computation.2 | custom fusion | bytes 4202496 | tf_op jit(solution)/shard_map/gather | solution.py:135
  469.4 2.5 copy.67
  471.9 0.0 reduce-scatter.4.cloned.1.call-update
  471.9 3.1 fusion.30
  475.0 2.1 dynamic-slice_convert_fusion
  477.1 24.6 %reduce-scatter.4.cloned.1.call-done = bf16[128,2048]{1,0:T(8,128)(2,1)} async-done(((bf16[512,2048]{1,0:T(8,128)(2,1)}), bf16[128,2048]{1,0:T(8,128)(2,1)}) %reduce-scatter.4.cloned.1.call-update) | async-done | bytes 524304
  501.6 1.3 copy.68
  502.9 2.4 add_convert_fusion
  (46 shorter events, 0.3 us)
Async XLA Ops:
  7.2 346.5 %copy-start = (bf16[2,512,512]{2,1,0:T(8,128)(2,1)S(1)}, bf16[2,512,512]{2,1,0:T(8,128)(2,1)}, u32[]{:S(2)}) copy-start(bf16[2,512,512]{2,1,0:T(8,128)(2,1)} %param.18) | copy-start | bytes 3145732
  10.1 16.6 %all-to-all-start = ((s32[32,1,2]{2,1,0:T(1,128)}), s32[32,1,2]{2,1,0:T(1,128)S(1)}, u32[]{:S(2)}, u32[]{:S(2)}) async-start(s32[32,1,2]{2,1,0:T(1,128)} %copy.52), calls=%async_computation | async-start | bytes 32768 | tf_op jit(solution)/shard_map/all_to_all | solution.py:78
  23.1 3.7 copy-start.4
  26.5 0.8 copy-start.3
  30.1 7.8 %copy-start.8 = (s32[16,12]{1,0:T(8,128)S(1)}, s32[16,12]{1,0:T(8,128)}, u32[]{:S(2)}) copy-start(s32[16,12]{1,0:T(8,128)} %param.20) | copy-start | bytes 2308
  30.1 8.9 %copy-start.12 = (f32[2]{0:T(128)S(1)}, f32[2]{0:T(128)}, u32[]{:S(2)}) copy-start(f32[2]{0:T(128)} %param.14) | copy-start | bytes 28
  30.1 8.9 %copy-start.1 = (bf16[2048,512]{1,0:T(8,128)(2,1)S(1)}, bf16[2048,512]{1,0:T(8,128)(2,1)}, u32[]{:S(2)}) copy-start(bf16[2048,512]{1,0:T(8,128)(2,1)} %param.11) | copy-start | bytes 6291460
  30.1 57.8 %all-to-all-start.1 = ((bf16[32,2,128,256]{3,2,1,0:T(8,128)(2,1)}), bf16[32,2,128,256]{3,2,1,0:T(8,128)(2,1)}, u32[]{:S(2)}, u32[]{:S(2)}) async-start(bf16[32,2,128,256]{3,2,1,0:T(8,128)(2,1)} %bitcast.145), calls=%async_computation.1 | async-start | bytes 8388608 | tf_op jit(solution)/shard_map/all_to_all | solution.py:80
  37.6 212.9 %all-reduce.3.cloned.1.call-start = ((), (), s32[]{:S(2)}) async-start(), calls=%async_computation.5 | async-start | bytes 8388608 | tf_op jit(solution)/shard_map/psum | solution.py:108
  141.0 14.3 %copy-start.5 = (bf16[128,512]{1,0:T(8,128)(2,1)S(1)}, bf16[128,512]{1,0:T(8,128)(2,1)}, u32[]{:S(2)}) copy-start(bf16[128,512]{1,0:T(8,128)(2,1)} %param.13) | copy-start | bytes 393220
  153.9 4.1 copy-start.7
  159.6 95.6 %copy-start.9 = (f32[512]{0:T(512)S(1)}, f32[512]{0:T(512)}, u32[]{:S(2)}) copy-start(f32[512]{0:T(512)} %param.15) | copy-start | bytes 6148
  351.0 2.6 copy-start.2
  353.6 6.5 %copy-start.10 = (bf16[2,512,512]{2,1,0:T(8,128)(2,1)S(1)}, bf16[2,512,512]{2,1,0:T(8,128)(2,1)}, u32[]{:S(2)}) copy-start(bf16[2,512,512]{2,1,0:T(8,128)(2,1)} %param.19) | copy-start | bytes 3145732
  353.6 6.5 %copy-start.11 = (bf16[2,512,512]{2,1,0:T(8,128)(2,1)S(1)}, bf16[2,512,512]{2,1,0:T(8,128)(2,1)}, u32[]{:S(2)}) copy-start(bf16[2,512,512]{2,1,0:T(8,128)(2,1)} %param.17) | copy-start | bytes 3145732
  380.2 77.9 %all-to-all-start.3 = ((bf16[32,2,96,512]{3,2,1,0:T(8,128)(2,1)}), bf16[32,2,96,512]{3,2,1,0:T(8,128)(2,1)}, u32[]{:S(2)}, u32[]{:S(2)}) async-start(bf16[32,2,96,512]{3,2,1,0:T(8,128)(2,1)} %copy.63), calls=%async_computation.3 | async-start | bytes 12582912 | tf_op jit(solution)/shard_map/all_to_all | solution.py:132
  385.1 116.5 %reduce-scatter.4.cloned.1.call-start = ((), (), s32[]{:S(2)}) async-start(), calls=%async_computation.6 | async-start | bytes 2621440
  469.4 2.5 copy-start.6
Sparse Core Ops, SparseCore 0:
  158.1 92.3 all-reduce.2
  472.0 29.5 reduce-scatter.3
where the time goes:
time: 513 us; the launch traced here: 512 us
  waiting for transfers between devices  235 us (46%)
  blocking collectives  81.1 us (16%)
  local copies, waits for them, and re-layouts  74.3 us (14%)
  matrix products  55.3 us (11%)
  other arithmetic  29.3 us (6%)
  starting transfers between devices  22.3 us (4%)
  between operations  14.5 us (3%)
    psum x1, waiting for transfers between devices, on_device(): total = lax.psum(partial_value, 'mp')  90.8 us
    all_to_all x1, blocking collectives, on_device(): lax.all_to_all(buffer, 'graph', split_axis=0, concat_axis=0, tiled=True)  81.1 us
    all_to_all x1, waiting for transfers between devices, on_device(): lax.all_to_all(produced.astype(jnp.bfloat16), 'graph', split_axis=0, conc...  73 us
    all_to_all x1, waiting for transfers between devices, on_device(): lax.all_to_all(outgoing, 'graph', split_axis=0, concat_axis=0, tiled=True)  47 us
    unnamed x3, waiting for transfers between devices  24.6 us
    slice x2, local copies, waits for them, and re-layouts, on_device(): gathered[:, :, :local_width].reshape(blocks, -1, local_heads, HEAD_DIM)  20.4 us
    scatter x1, other arithmetic, on_device(): jnp.zeros((experts * capacity, width), jnp.bfloat16).at[target].set(normed)  14.8 us
    dot_general x1, matrix products, make_work(): jnp.einsum('gesf,efd->gesd', hidden, down_weights, preferred_element_type...  14 us
  transfers between devices with their start and end apart: 5, of which 4 were waited for; matrix products, arithmetic and copies ran while one was open for 3% of the time, Pallas kernels for 0%

commit v1 on v0

v1 whole, which is shorter than its diff:
```python
import math

import jax
import jax.numpy as jnp
from jax import lax
from jax.experimental import pallas as pl
from jax.experimental.pallas import tpu as pltpu
from jax.sharding import PartitionSpec as P

HEAD_DIM = 64
ROWS_BLK = 128
LOCAL_REFS = 4
CAP_H = 2
CAP_E = 96
EPS = 1e-06
LANES = 128
VMEM_BYTES = 48 * 2**20

VMEM = pl.BlockSpec(memory_space=pltpu.VMEM)
SMEM = pl.BlockSpec(memory_space=pltpu.SMEM)
ANY = pl.BlockSpec(memory_space=pl.ANY)
F32 = jnp.float32
BF16 = jnp.bfloat16


def params():
    return pltpu.CompilerParams(vmem_limit_bytes=VMEM_BYTES)


def cost(flops, moved, transcendentals=0):
    return pl.CostEstimate(flops=flops, bytes_accessed=moved, transcendentals=transcendentals)


def head_units(values):
    low = lax.broadcasted_iota(jnp.int32, values.shape, 1) < HEAD_DIM
    squares = values * values
    first = jnp.sum(jnp.where(low, squares, 0.0), axis=1, keepdims=True)
    second = jnp.sum(jnp.where(low, 0.0, squares), axis=1, keepdims=True)
    scale = lax.rsqrt(jnp.where(low, first, second) * (1.0 / HEAD_DIM) + EPS)
    return values * scale


def qkv_kernel(x_ref, w_ref, scale_ref, q_ref, kv_ref):
    x = x_ref[...]
    rows = x.shape[0]
    query = jnp.dot(x, w_ref[0], preferred_element_type=F32)
    q_ref[...] = (head_units(query) * scale_ref[...]).astype(BF16)
    key = jnp.dot(x, w_ref[1], preferred_element_type=F32)
    value = jnp.dot(x, w_ref[2], preferred_element_type=F32)
    kv_ref[:, :, :LANES] = head_units(key).astype(BF16).reshape(rows // ROWS_BLK, ROWS_BLK, LANES)
    kv_ref[:, :, LANES:] = value.astype(BF16).reshape(rows // ROWS_BLK, ROWS_BLK, LANES)


def qkv(x, w, scale):
    rows, width = x.shape
    tile = 512
    blocks = tile // ROWS_BLK
    return pl.pallas_call(
        qkv_kernel,
        grid=(rows // tile,),
        in_specs=[
            pl.BlockSpec((tile, width), lambda i: (i, 0)),
            pl.BlockSpec((3, width, LANES), lambda i: (0, 0, 0)),
            pl.BlockSpec((1, LANES), lambda i: (0, 0)),
        ],
        out_specs=[
            pl.BlockSpec((tile, LANES), lambda i: (i, 0)),
            pl.BlockSpec((blocks, ROWS_BLK, 2 * LANES), lambda i: (i, 0, 0)),
        ],
        out_shape=[
            jax.ShapeDtypeStruct((rows, LANES), BF16),
            jax.ShapeDtypeStruct((rows // ROWS_BLK, ROWS_BLK, 2 * LANES), BF16),
        ],
        compiler_params=params(),
        cost_estimate=cost(2 * rows * width * 3 * LANES, 2 * rows * (width + 3 * LANES)),
        name="qkv",
    )(x, w, scale)


def pick_kernel(wanted_ref, kv_ref, out_ref, sems):
    count = out_ref.shape[0]
    copies = [
        pltpu.make_async_copy(kv_ref.at[wanted_ref[i]], out_ref.at[i], sems.at[i])
        for i in range(count)
    ]
    for copy in copies:
        copy.start()
    for copy in copies:
        copy.wait()


def pick_blocks(wanted, kv):
    count = wanted.shape[0]
    out = jax.ShapeDtypeStruct((count,) + kv.shape[1:], kv.dtype)
    return pl.pallas_call(
        pick_kernel,
        in_specs=[SMEM, VMEM],
        out_specs=ANY,
        out_shape=out,
        scratch_shapes=[pltpu.SemaphoreType.DMA((count,))],
        compiler_params=params(),
        cost_estimate=cost(0, 2 * out.size * 2),
        name="pick_blocks",
    )(wanted, kv)


def attention_kernel(
    near_ref, far_ref, q_ref, kv_ref, halo_ref, spot_ref, lane_ref, heads_ref, send_ref, keys, values, spread
):
    blocks = kv_ref.shape[0]
    nears, fars = near_ref.shape[1], far_ref.shape[1]
    low = lax.broadcasted_iota(jnp.int32, (ROWS_BLK, LANES), 1) < HEAD_DIM

    @pl.loop(0, blocks)
    def _(b):
        rows = pl.ds(pl.multiple_of(b * ROWS_BLK, ROWS_BLK), ROWS_BLK)
        q = q_ref[rows, :].astype(F32)
        both = jnp.concatenate([jnp.where(low, q, 0.0), jnp.where(low, 0.0, q)], axis=0).astype(BF16)
        for j in range(nears + fars):
            if j < nears:
                block = kv_ref[near_ref[b, j]]
            else:
                block = halo_ref[far_ref[b, j - nears]]
            keys[j * ROWS_BLK : (j + 1) * ROWS_BLK, :] = block[:, :LANES]
            values[j * ROWS_BLK : (j + 1) * ROWS_BLK, :] = block[:, LANES:]
        scores = lax.dot_general(
            both, keys[...], (((1,), (1,)), ((), ())), preferred_element_type=F32
        )
        largest = jnp.max(scores, axis=1, keepdims=True)
        expo = jnp.exp(scores - largest)
        total = jnp.sum(expo, axis=1, keepdims=True)
        out = jnp.dot(expo.astype(BF16), values[...], preferred_element_type=F32) / total
        heads = jnp.where(low, out[:ROWS_BLK], out[ROWS_BLK:])
        heads_ref[rows, :] = heads.astype(BF16)
        lane = lane_ref[rows, :]
        for m in range(4):
            spread[rows, m * LANES : (m + 1) * LANES] = jnp.where(lane == m, heads, 0.0).astype(BF16)

    dests, cap = send_ref.shape[0], send_ref.shape[2]
    step = 4

    @pl.loop(0, dests // step)
    def _(i):
        tile = step * cap
        spot = spot_ref[...]
        here = lax.broadcasted_iota(jnp.int32, (tile, spot.shape[1]), 0) + i * tile
        hot = jnp.where(here == spot, 1.0, 0.0).astype(BF16)
        placed = jnp.dot(hot, spread[...], preferred_element_type=F32).astype(BF16)
        for d in range(step):
            for m in range(4):
                send_ref[i * step + d, m] = placed[d * cap : (d + 1) * cap, m * LANES : (m + 1) * LANES]


def attention(near, far, q, kv, halo, spot_row, lane_col, parts, cap):
    rows = q.shape[0]
    keys = (near.shape[1] + far.shape[1]) * ROWS_BLK
    return pl.pallas_call(
        attention_kernel,
        in_specs=[SMEM, SMEM, VMEM, VMEM, VMEM, VMEM, VMEM],
        out_specs=[VMEM, VMEM],
        out_shape=[
            jax.ShapeDtypeStruct((rows, LANES), BF16),
            jax.ShapeDtypeStruct((parts, 4, cap, LANES), BF16),
        ],
        scratch_shapes=[
            pltpu.VMEM((keys, LANES), BF16),
            pltpu.VMEM((keys, LANES), BF16),
            pltpu.VMEM((rows, 4 * LANES), BF16),
        ],
        compiler_params=params(),
        cost_estimate=cost(12 * 10**9, 8 * 2**20, 2 * rows * keys),
        name="attention",
    )(near, far, q, kv, halo, spot_row, lane_col)


def place_kernel(spot_ref, x_ref, out_ref):
    dests, cap = out_ref.shape[0], out_ref.shape[1]
    step = 4

    @pl.loop(0, dests // step)
    def _(i):
        tile = step * cap
        spot = spot_ref[...]
        here = lax.broadcasted_iota(jnp.int32, (tile, spot.shape[1]), 0) + i * tile
        hot = jnp.where(here == spot, 1.0, 0.0).astype(BF16)
        placed = jnp.dot(hot, x_ref[...], preferred_element_type=F32).astype(BF16)
        for d in range(step):
            out_ref[i * step + d] = placed[d * cap : (d + 1) * cap, :]


def place_rows(spot_row, x, parts, cap):
    rows, width = x.shape
    return pl.pallas_call(
        place_kernel,
        in_specs=[VMEM, VMEM],
        out_specs=VMEM,
        out_shape=jax.ShapeDtypeStruct((parts, cap, width), BF16),
        compiler_params=params(),
        cost_estimate=cost(2 * parts * cap * rows * width, 4 * 2**20),
        name="place_rows",
    )(spot_row, x)


def experts_kernel(
    me_ref, h_ref, x_ref, gain_ref, route_ref, w0_ref, w1_ref, w2_ref, w3_ref, out_ref
):
    me = me_ref[0]
    parts, cap, width = x_ref.shape
    tile = parts * cap
    quarters = (w0_ref, w1_ref, w2_ref, w3_ref)
    total = None
    for k, w in enumerate(quarters):
        piece = h_ref[:, me ^ k].reshape(tile, LANES)
        term = jnp.dot(piece, w[3 * width :, :], preferred_element_type=F32)
        total = term if total is None else total + term
    mixed = x_ref[...].reshape(tile, width).astype(F32) + total
    mean = jnp.mean(mixed * mixed, axis=1, keepdims=True)
    normed = (mixed * lax.rsqrt(mean + EPS) * gain_ref[...]).astype(BF16)
    logit = jnp.sum(normed.astype(F32) * route_ref[...], axis=1, keepdims=True)
    gate = 1.0 / (1.0 + jnp.exp(-logit))
    result = None
    for w in quarters:
        left = jnp.dot(normed, w[:width, :], preferred_element_type=F32)
        right = jnp.dot(normed, w[width : 2 * width, :], preferred_element_type=F32)
        half = 0.5 * left
        hidden = ((half + half * jnp.tanh(half)) * right).astype(BF16)
        term = jnp.dot(hidden, w[2 * width : 3 * width, :], preferred_element_type=F32)
        result = term if result is None else result + term
    result = (gate * result).astype(BF16).reshape(parts, cap, width)
    for m in range(4):
        out_ref[:, m] = result[:, :, m * LANES : (m + 1) * LANES]


def experts(me, heads, x, gain, route, weights):
    parts, cap, width = x.shape
    step = 8
    whole = pl.BlockSpec(weights[0].shape, lambda i: (0, 0))
    row = pl.BlockSpec((1, width), lambda i: (0, 0))
    return pl.pallas_call(
        experts_kernel,
        grid=(parts // step,),
        in_specs=[
            SMEM,
            pl.BlockSpec((step, 4, cap, LANES), lambda i: (i, 0, 0, 0)),
            pl.BlockSpec((step, cap, width), lambda i: (i, 0, 0)),
            row,
            row,
            whole,
            whole,
            whole,
            whole,
        ],
        out_specs=pl.BlockSpec((step, 4, cap, LANES), lambda i: (i, 0, 0, 0)),
        out_shape=jax.ShapeDtypeStruct((parts, 4, cap, LANES), BF16),
        compiler_params=params(),
        cost_estimate=cost(2 * parts * cap * width * (12 * width + width), 12 * 2**20),
        name="experts",
    )(me, heads, x, gain, route, *weights)


def columns_kernel(
    me_ref, h0_ref, h1_ref, h2_ref, h3_ref, w0_ref, w1_ref, w2_ref, w3_ref, x_ref, attn_ref, mixed_ref
):
    columns = pl.ds(pl.multiple_of(me_ref[0] * LANES, LANES), LANES)
    total = None
    for h, w in zip((h0_ref, h1_ref, h2_ref, h3_ref), (w0_ref, w1_ref, w2_ref, w3_ref)):
        term = jnp.dot(h[...], w[:, columns], preferred_element_type=F32)
        total = term if total is None else total + term
    attn_ref[...] = total.astype(BF16)
    mixed_ref[...] = x_ref[:, columns].astype(F32) + total


def attention_columns(me, heads, weights, x):
    rows, width = x.shape
    last = weights[0].shape[0] // LANES - 1
    out = pl.BlockSpec((rows, LANES), lambda i: (0, 0))
    return pl.pallas_call(
        columns_kernel,
        grid=(1,),
        in_specs=[SMEM]
        + [out] * 4
        + [pl.BlockSpec((LANES, width), lambda i: (last, 0))] * 4
        + [pl.BlockSpec((rows, width), lambda i: (0, 0))],
        out_specs=[out, out],
        out_shape=[
            jax.ShapeDtypeStruct((rows, LANES), BF16),
            jax.ShapeDtypeStruct((rows, LANES), F32),
        ],
        compiler_params=params(),
        cost_estimate=cost(2 * rows * width * LANES, 8 * 2**20),
        name="attention_columns",
    )(me, *heads, *weights, x)


def combine_kernel(spot_ref, lane_ref, back_ref, mixed_ref, out_ref, slots):
    dests, cap = back_ref.shape[0], back_ref.shape[2]
    rows = out_ref.shape[0]
    for m in range(4):
        slots[:, m * LANES : (m + 1) * LANES] = back_ref[:, m].reshape(dests * cap, LANES)
    tile = 256

    @pl.loop(0, rows // tile)
    def _(i):
        here = pl.ds(pl.multiple_of(i * tile, tile), tile)
        spot = lax.broadcasted_iota(jnp.int32, (tile, dests * cap), 1)
        hot = jnp.where(spot == spot_ref[here, :], 1.0, 0.0).astype(BF16)
        found = jnp.dot(hot, slots[...], preferred_element_type=F32)
        lane = lane_ref[here, :]
        total = mixed_ref[here, :]
        for m in range(4):
            total = total + jnp.where(lane == m, found[:, m * LANES : (m + 1) * LANES], 0.0)
        out_ref[here, :] = total.astype(BF16)


def combine(spot_col, lane_col, back, mixed):
    rows = mixed.shape[0]
    slots = back.shape[0] * back.shape[2]
    return pl.pallas_call(
        combine_kernel,
        in_specs=[VMEM] * 4,
        out_specs=VMEM,
        out_shape=jax.ShapeDtypeStruct((rows, LANES), BF16),
        scratch_shapes=[pltpu.VMEM((slots, 4 * LANES), BF16)],
        compiler_params=params(),
        cost_estimate=cost(2 * rows * slots * 4 * LANES, 4 * 2**20),
        name="combine",
    )(spot_col, lane_col, back, mixed)


def swap(array, change):
    return lax.ppermute(array, "mp", [(i, i ^ change) for i in range(4)])


def exchange(array, axes):
    return lax.all_to_all(array, axes, split_axis=0, concat_axis=0, tiled=True)


def on_device(
    node_features,
    w_qkv,
    w_out,
    head_scale,
    norm_gain,
    router,
    w_gate,
    w_up,
    w_down,
    neighbor_blocks,
    expert_ids,
):
    parts = lax.axis_size("graph")
    part = lax.axis_index("graph")
    me = lax.axis_index("mp")
    rows, width = node_features.shape
    blocks = rows // ROWS_BLK
    half_cap = CAP_E // 2

    far = neighbor_blocks[:, LOCAL_REFS:]
    names = jnp.arange(parts * blocks, dtype=jnp.int32).reshape(parts, blocks)
    wanted = jnp.any(far.reshape(-1)[:, None, None] == names[None], axis=0)
    inside = jnp.arange(blocks, dtype=jnp.int32)[None, :]
    first = jnp.min(jnp.where(wanted, inside, blocks - 1), axis=1)
    last = jnp.max(jnp.where(wanted, inside, 0), axis=1)
    requests = jnp.stack([first, last], axis=1)
    incoming = exchange(requests.reshape(parts, 1, CAP_H), "graph").reshape(-1)
    bases = jnp.arange(parts, dtype=jnp.int32)[:, None] * blocks
    pool = (bases + requests).reshape(-1)
    slots = jnp.arange(pool.shape[0], dtype=jnp.int32)
    far_slots = jnp.max(jnp.where(far[:, :, None] == pool[None, None, :], slots[None, None, :], 0), axis=2)
    near_slots = neighbor_blocks[:, :LOCAL_REFS] - part * blocks

    scale = jnp.repeat(head_scale / math.sqrt(HEAD_DIM), HEAD_DIM)[None, :]
    q, kv = qkv(node_features, w_qkv, scale)
    halo = exchange(pick_blocks(incoming, kv), "graph")

    routed = expert_ids[:, 0]
    experts_all = router.shape[1]
    chosen = routed[:, None] == jnp.arange(experts_all, dtype=jnp.int32)[None, :]
    row_ids = jnp.arange(rows, dtype=jnp.int32)
    earlier = (row_ids[:, None] > row_ids[None, :]).astype(BF16)
    before = jnp.dot(earlier, chosen.astype(BF16), preferred_element_type=F32)
    rank = jnp.sum(jnp.where(chosen, before, 0.0), axis=1).astype(jnp.int32)
    second = (rank >= half_cap).astype(jnp.int32)
    lane = (routed % 2) * 2 + second
    spot = (routed // 2) * half_cap + rank - second * half_cap
    spot_row, spot_col, lane_col = spot[None, :], spot[:, None], lane[:, None]
    mine_row = jnp.where(lane == me, spot, -1)[None, :]
    x_there = exchange(place_rows(mine_row, node_features, parts, half_cap), "graph")

    which = me // 2
    kept, given = [
        jnp.concatenate(
            [lax.dynamic_index_in_dim(w, i, 0, keepdims=False) for w in (w_gate, w_up, w_down)] + [w_out],
            axis=0,
        )
        for i in (which, 1 - which)
    ]
    weights = [kept, swap(kept, 1), swap(given, 2), swap(given, 3)]
    route = lax.dynamic_index_in_dim(router, 2 * part + which, 1, keepdims=False).astype(F32)[None, :]
    me_ref = me[None].astype(jnp.int32)

    heads, send = attention(
        near_slots, far_slots, q, kv, halo, spot_row, lane_col, parts, half_cap
    )
    heads_there = exchange(send.reshape(parts * 4, half_cap, LANES), ("graph", "mp"))
    all_heads = [heads] + [swap(heads, k) for k in (1, 2, 3)]
    attn_out, mixed = attention_columns(me_ref, all_heads, weights, node_features)

    produced = experts(
        me_ref,
        heads_there.reshape(parts, 4, half_cap, LANES),
        x_there,
        norm_gain[None, :],
        route,
        weights,
    )
    back = exchange(produced.reshape(parts * 4, half_cap, LANES), ("graph", "mp"))
    layer_out = combine(spot_col, lane_col, back.reshape(parts, 4, half_cap, LANES), mixed)
    return (attn_out, layer_out)


def solution(mesh):
    placed = (
        P("graph", None),
        P(None, None, "mp"),
        P("mp", None),
        P("mp"),
        P(),
        P(),
        P("graph", None, "mp"),
        P("graph", None, "mp"),
        P("graph", "mp", None),
        P("graph", None),
        P("graph", None),
    )
    return jax.shard_map(
        on_device,
        mesh=mesh,
        in_specs=placed,
        out_specs=(P("graph", "mp"), P("graph", "mp")),
        check_vma=False,
    )
```

time: 513 us -> 240 us (0.47)
  waiting for transfers between devices: 235 us -> 91.8 us
  blocking collectives: 81.1 us -> 0 us
  Pallas kernels: 0 us -> 63.5 us
  matrix products: 55.3 us -> 1.66 us
  local copies, waits for them, and re-layouts: 74.3 us -> 26.7 us
  starting transfers between devices: 22.3 us -> 45.6 us
  other arithmetic: 29.3 us -> 8.68 us
  between operations: 14.5 us -> 1 us
    psum x1 -> x0, waiting for transfers between devices: 90.8 us -> none  [on_device(): total = lax.psum(partial_value, 'mp')]
    all_to_all x1 -> x0, blocking collectives: 81.1 us -> none  [on_device(): lax.all_to_all(buffer, 'graph', split_axis=0, concat_axis=0, tiled=True)]
    all_to_all x3 -> x5, waiting for transfers between devices: 120 us -> 53.4 us  [exchange(): return lax.all_to_all(array, axes, split_axis=0, concat_axis=0, tiled=True)]
    pallas_call x0 -> x7, Pallas kernels: none -> 63.5 us  [the longest x1 22.7 us: attention(): pl.pallas_call(attention_kernel, in_specs=[SMEM, SMEM, VMEM, VMEM, VMEM,...]
    dot_general x9 -> x1, matrix products: 47.5 us -> 1.66 us  [on_device(): before = jnp.dot(earlier, chosen.astype(BF16), preferred_element_type=F32)]
    ppermute x0 -> x6, waiting for transfers between devices: none -> 38.4 us  [swap(): return lax.ppermute(array, 'mp', [(i, i ^ change) for i in range(4)])]
    slice x4 -> x1, local copies, waits for them, and re-layouts: 29.2 us -> 0.77 us  [on_device(): far = neighbor_blocks[:, LOCAL_REFS:]]
    gather x3 -> x0, local copies, waits for them, and re-layouts: 24.7 us -> none  [the longest x1 11.2 us: on_device(): mine = back.reshape(-1, width)[target]]
  transfers between devices with their start and end apart: 5 -> 11, of which waited for: 4 -> 4; matrix products, arithmetic and copies ran while one was open for 3% -> 6% of each run, Pallas kernels for 0% -> 14%
where the time goes in v1:
time: 240 us; the launch traced here: 239 us
  waiting for transfers between devices  91.8 us (38%)
  Pallas kernels  63.5 us (26%)
  starting transfers between devices  45.6 us (19%)
  local copies, waits for them, and re-layouts  26.7 us (11%)
  other arithmetic  8.68 us (4%)
    all_to_all x5, waiting for transfers between devices, exchange(): return lax.all_to_all(array, axes, split_axis=0, concat_axis=0, tiled=True)  53.4 us
    ppermute x6, waiting for transfers between devices, swap(): return lax.ppermute(array, 'mp', [(i, i ^ change) for i in range(4)])  38.4 us
    all_to_all x5, starting transfers between devices, exchange(): return lax.all_to_all(array, axes, split_axis=0, concat_axis=0, tiled=True)  38.1 us
    pallas_call x1, Pallas kernels, attention(): pl.pallas_call(attention_kernel, in_specs=[SMEM, SMEM, VMEM, VMEM, VMEM,...  22.7 us
    unnamed x55, local copies, waits for them, and re-layouts  21.5 us
    pallas_call x1, Pallas kernels, experts(): pl.pallas_call(experts_kernel, grid=(parts // step,), in_specs=[SMEM, pl....  17.2 us
    ppermute x6, starting transfers between devices, swap(): return lax.ppermute(array, 'mp', [(i, i ^ change) for i in range(4)])  7.56 us
    pallas_call x1, Pallas kernels, pick_blocks(): pl.pallas_call(pick_kernel, in_specs=[SMEM, VMEM], out_specs=ANY, out_sha...  6.84 us
  transfers between devices with their start and end apart: 11, of which 4 were waited for; matrix products, arithmetic and copies ran while one was open for 6% of the time, Pallas kernels for 14%

profile of v1, /device:TPU:1, one launch (start us, length us, event | category | flops | bytes accessed | tf_op | source)
XLA Modules:
  0.0 239.0 jit_solution(15093337028589260712)
XLA Ops:
  0.7 0.8 slice.7
  1.4 0.1 eq.59
  1.5 0.7 compare_reduce_fusion
  2.2 0.1 select_reduce_fusion.2
  2.4 0.7 copy.60
  3.1 9.6 %all-to-all-start = ((s32[32,1,2]{2,1,0:T(1,128)}), s32[32,1,2]{2,1,0:T(1,128)S(1)}, u32[]{:S(2)}, u32[]{:S(2)}) async-start(s32[32,1,2]{2,1,0:T(1,128)} %copy.60), calls=%async_computation | async-start | bytes 32768 | tf_op jit(solution)/shard_map/all_to_all | solution.py:335
  12.7 0.7 broadcast_multiply_fusion
  13.3 0.1 broadcast_in_dim.66
  13.4 0.1 broadcast_in_dim_reshape.15.scale_ref
  13.5 1.6 copy-done.3
  15.1 1.0 copy-done.17
  16.1 2.7 %qkv.1 = (bf16[2048,128]{1,0:T(8,128)(2,1)S(1)}, bf16[16,128,256]{2,1,0:T(8,128)(2,1)S(1)}) custom-call(bf16[2048,512]{1,0:T(8,128)(2,1)S(1)} %copy-done.3, bf16[3,512,128]{2,1,0:T(8,128)(2,1)S(1)} %copy-done.17, f32[1,128]{1,0:T(1,128)S(1)} %broadcast_in_dim_reshape.15.scale_ref), custom_call_target="tpu_custom_call" | custom-call | flops 805306368 | bytes 3670016 | tf_op jit(solution)/shard_map/qkv/pallas_call | solution.py:58
  18.8 0.0 copy-start.19
  18.8 0.8 copy-done.19
  19.6 0.5 broadcast.273
  20.1 0.7 reduce.3
  20.8 0.1 reshape.238.wanted_ref
  20.9 6.8 %pick_blocks.1 = bf16[64,128,256]{2,1,0:T(8,128)(2,1)S(1)} custom-call(s32[64]{0:T(128)S(1)} %reshape.238.wanted_ref, bf16[16,128,256]{2,1,0:T(8,128)(2,1)S(1)} %get-tuple-element.9.kv_ref), custom_call_target="tpu_custom_call" | custom-call | bytes 8388608 | tf_op jit(solution)/shard_map/pick_blocks/pallas_call | solution.py:95
  27.8 2.0 copy-done
  29.8 7.6 %all-to-all-start.1 = ((bf16[64,128,256]{2,1,0:T(8,128)(2,1)}), bf16[64,128,256]{2,1,0:T(8,128)(2,1)}, u32[]{:S(2)}, u32[]{:S(2)}) async-start(bf16[64,128,256]{2,1,0:T(8,128)(2,1)} %copy-done), calls=%async_computation.1 | async-start | bytes 8388608 | tf_op jit(solution)/shard_map/all_to_all | solution.py:335
  37.4 0.1 dynamic-slice_bitcast_fusion.2
  37.5 1.1 copy-done.21
  38.6 0.3 copy-done.22
  38.9 0.1 dynamic-slice_bitcast_fusion
  39.1 0.8 copy-done.24
  39.8 1.3 pad_maximum_fusion
  41.1 2.7 %collective-permute-start.4 = (bf16[1664,512]{1,0:T(8,128)(2,1)}, bf16[1664,512]{1,0:T(8,128)(2,1)}, u32[]{:S(2)}, u32[]{:S(2)}) collective-permute-start(bf16[1664,512]{1,0:T(8,128)(2,1)} %get-tuple-element.26), channel_id=1, source_target_pairs={{0,2},{1,3},{2,0},{3,1},{4,6},{5,7},{6,4},{7,5},{8,10},{9,11},{10,... | collective-permute-start | bytes 5111816 | tf_op jit(solution)/shard_map/ppermute | solution.py:331
  43.9 0.9 collective-permute-start.5
  44.7 0.1 copy.59
  44.8 0.1 add.102
  44.9 1.4 copy.62
  46.3 1.7 fusion.2
  48.0 1.3 copy.66
  49.4 1.1 copy.65
  50.5 0.4 select_reduce_fusion.far_ref
  50.9 0.1 compare_select_fusion
  51.0 1.6 copy-done.4
  52.6 4.6 %place_rows.1 = bf16[32,48,512]{2,1,0:T(8,128)(2,1)S(1)} custom-call(s32[1,2048]{1,0:T(1,128)S(1)} %get-tuple-element.16.spot_ref, bf16[2048,512]{1,0:T(8,128)(2,1)S(1)} %copy-done.4), custom_call_target="tpu_custom_call" | custom-call | flops 3221225472 | bytes 4194304 | tf_op jit(solution)/shard_map/place_rows/pallas_call | solution.py:193
  57.2 1.2 copy-done.7
  58.4 29.2 %all-to-all-done.1.halo_ref = bf16[64,128,256]{2,1,0:T(8,128)(2,1)} async-done(((bf16[64,128,256]{2,1,0:T(8,128)(2,1)}), bf16[64,128,256]{2,1,0:T(8,128)(2,1)}, u32[]{:S(2)}, u32[]{:S(2)}) %all-to-all-start.1) | async-done | bytes 4194336 | tf_op jit(solution)/shard_map/all_to_all | solution.py:335
  87.6 7.1 %all-to-all-start.3 = ((bf16[32,48,512]{2,1,0:T(8,128)(2,1)}), bf16[32,48,512]{2,1,0:T(8,128)(2,1)S(1)}, u32[]{:S(2)}, u32[]{:S(2)}) async-start(bf16[32,48,512]{2,1,0:T(8,128)(2,1)} %copy-done.7), calls=%async_computation.3 | async-start | bytes 3145728 | tf_op jit(solution)/shard_map/all_to_all | solution.py:335
  94.8 3.9 %fusion.7 = (s32[2048,1]{1,0:T(8,128)}, s32[2048,1]{1,0:T(8,128)S(1)}) fusion(s32[2048,1]{1,0:T(8,128)} %copy.66, pred[2048,1]{1,0:T(8,128)(4,1)} %copy.65, s32[2048,1]{1,0:T(8,128)} %copy.62), kind=kLoop, calls=%fused_computation.15 | loop fusion | flops 53248 | bytes 34816 | tf_op jit(solution)/shard_map/sub | solution.py:385
  98.7 22.7 %attention.1 = (bf16[2048,128]{1,0:T(8,128)(2,1)S(1)}, bf16[32,4,48,128]{3,2,1,0:T(8,128)(2,1)S(1)}) custom-call(s32[16,4]{1,0:T(8,128)S(1)} %slice_subtract_fusion.near_ref, s32[16,8]{1,0:T(8,128)S(1)} %select_reduce_fusion.far_ref, bf16[2048,128]{1,0:T(8,128)(2,1)S(1)} %copy-done.20, bf16[16,128,256]{2,1,0:T(8,128)(2,1)S(1)} %copy-done.12, ...), custom_call_target="tpu_custom_call" | custom-call | flops 12000000000 | bytes 8388608 | tf_op jit(solution)/shard_map/attention/pallas_call | solution.py:157
  121.5 1.2 copy-done.5
  122.6 1.0 copy-done.9
  123.6 0.8 copy-done.13
  124.4 9.8 %all-to-all-start.2 = ((bf16[128,48,128]{2,1,0:T(8,128)(2,1)}), bf16[128,48,128]{2,1,0:T(8,128)(2,1)}, u32[]{:S(2)}, u32[]{:S(2)}) async-start(bf16[128,48,128]{2,1,0:T(8,128)(2,1)} %bitcast.47), calls=%async_computation.2 | async-start | bytes 3145728 | tf_op jit(solution)/shard_map/all_to_all | solution.py:335
  134.2 0.7 bitcast_convert_fusion.route_ref
  135.0 24.2 %all-to-all-done.2 = bf16[128,48,128]{2,1,0:T(8,128)(2,1)} async-done(((bf16[128,48,128]{2,1,0:T(8,128)(2,1)}), bf16[128,48,128]{2,1,0:T(8,128)(2,1)}, u32[]{:S(2)}, u32[]{:S(2)}) %all-to-all-start.2) | async-done | bytes 1572896 | tf_op jit(solution)/shard_map/all_to_all | solution.py:335
  159.1 17.2 %experts.1 = bf16[32,4,48,128]{3,2,1,0:T(8,128)(2,1)S(1)} custom-call(s32[1]{0:T(128)} %bitcast.me_ref, bf16[32,4,48,128]{3,2,1,0:T(8,128)(2,1)} %bitcast.15.h_ref, bf16[32,48,512]{2,1,0:T(8,128)(2,1)S(1)} %all-to-all-done.3.x_ref, f32[1,512]{1,0:T(1,128)S(1)} %bitcast.49, f32[1,512]{1,0:T(1,128)S(1)} %bitcast_convert_fusion.route_ref, ...), custom_call_target="tpu_custom_call" | custom-call | flops 10468982784 | bytes 12582912 | tf_op jit(solution)/shard_map/experts/pallas_call | solution.py:239
  176.4 1.2 copy-done.6
  177.5 4.0 %all-to-all-start.4 = ((bf16[128,48,128]{2,1,0:T(8,128)(2,1)}), bf16[128,48,128]{2,1,0:T(8,128)(2,1)S(1)}, u32[]{:S(2)}, u32[]{:S(2)}) async-start(bf16[128,48,128]{2,1,0:T(8,128)(2,1)} %bitcast.48), calls=%async_computation.4 | async-start | bytes 3145728 | tf_op jit(solution)/shard_map/all_to_all | solution.py:335
  181.5 1.5 collective-permute-start
  183.0 2.4 %collective-permute-start.1 = (bf16[2048,128]{1,0:T(8,128)(2,1)}, bf16[2048,128]{1,0:T(8,128)(2,1)S(1)}, u32[]{:S(2)}, u32[]{:S(2)}) collective-permute-start(bf16[2048,128]{1,0:T(8,128)(2,1)} %copy-done.13), channel_id=1, source_target_pairs={{0,2},{1,3},{2,0},{3,1},{4,6},{5,7},{6,4},{7,5},{8,10},{9,11},{10,... | collective-permute-start | bytes 1572872 | tf_op jit(solution)/shard_map/ppermute | solution.py:331
  185.4 0.1 collective-permute-start.2
  185.4 25.6 %collective-permute-done.h1_ref = bf16[2048,128]{1,0:T(8,128)(2,1)S(1)} collective-permute-done((bf16[2048,128]{1,0:T(8,128)(2,1)}, bf16[2048,128]{1,0:T(8,128)(2,1)S(1)}, u32[]{:S(2)}, u32[]{:S(2)}) %collective-permute-start) | collective-permute-done | bytes 524320 | tf_op jit(solution)/shard_map/ppermute | solution.py:331
  211.1 12.8 %collective-permute-done.1.h2_ref = bf16[2048,128]{1,0:T(8,128)(2,1)S(1)} collective-permute-done((bf16[2048,128]{1,0:T(8,128)(2,1)}, bf16[2048,128]{1,0:T(8,128)(2,1)S(1)}, u32[]{:S(2)}, u32[]{:S(2)}) %collective-permute-start.1) | collective-permute-done | bytes 524320 | tf_op jit(solution)/shard_map/ppermute | solution.py:331
  223.8 1.0 copy-done.14
  224.9 3.3 %attention_columns.1 = (bf16[2048,128]{1,0:T(8,128)(2,1)}, f32[2048,128]{1,0:T(8,128)S(1)}) custom-call(s32[1]{0:T(128)} %bitcast.me_ref, bf16[2048,128]{1,0:T(8,128)(2,1)S(1)} %copy-done.14, bf16[2048,128]{1,0:T(8,128)(2,1)S(1)} %collective-permute-done.h1_ref, bf16[2048,128]{1,0:T(8,128)(2,1)S(1)} %collective-permute-done.1.h2_ref, ...), custom_call_target="tpu_custom_call" | custom-call | flops 268435456 | bytes 8388608 | tf_op jit(solution)/shard_map/attention_columns/pallas_call | solution.py:277
  228.2 1.0 copy-done.15
  229.2 1.2 copy-done.8
  230.4 1.2 copy-done.10
  231.6 1.2 copy-done.16
  232.9 6.1 %combine.1 = bf16[2048,128]{1,0:T(8,128)(2,1)} custom-call(s32[2048,1]{1,0:T(8,128)S(1)} %copy-done.8, s32[2048,1]{1,0:T(8,128)S(1)} %copy-done.10, bf16[32,4,48,128]{3,2,1,0:T(8,128)(2,1)S(1)} %bitcast.46, f32[2048,128]{1,0:T(8,128)S(1)} %copy-done.16), custom_call_target="tpu_custom_call" | custom-call | flops 3221225472 | bytes 4194304 | tf_op jit(solution)/shard_map/combine/pallas_call | solution.py:318
  (49 shorter events, 0.1 us)
Async XLA Ops:
  3.1 16.5 %all-to-all-start = ((s32[32,1,2]{2,1,0:T(1,128)}), s32[32,1,2]{2,1,0:T(1,128)S(1)}, u32[]{:S(2)}, u32[]{:S(2)}) async-start(s32[32,1,2]{2,1,0:T(1,128)} %copy.60), calls=%async_computation | async-start | bytes 32768 | tf_op jit(solution)/shard_map/all_to_all | solution.py:335
  13.5 1.6 copy-start.3
  15.1 1.0 copy-start.17
  18.8 0.8 copy-start.19
  19.6 8.2 %copy-start.11 = (bf16[16,128,256]{2,1,0:T(8,128)(2,1)}, bf16[16,128,256]{2,1,0:T(8,128)(2,1)S(1)}, u32[]{:S(2)}) copy-start(bf16[16,128,256]{2,1,0:T(8,128)(2,1)S(1)} %get-tuple-element.9.kv_ref) | copy-start | bytes 3145732
  27.8 2.0 copy-start
  29.8 7.6 %copy-start.23 = (bf16[2,512,512]{2,1,0:T(8,128)(2,1)S(1)}, bf16[2,512,512]{2,1,0:T(8,128)(2,1)}, u32[]{:S(2)}) copy-start(bf16[2,512,512]{2,1,0:T(8,128)(2,1)} %param.17) | copy-start | bytes 3145732
  29.8 57.8 %all-to-all-start.1 = ((bf16[64,128,256]{2,1,0:T(8,128)(2,1)}), bf16[64,128,256]{2,1,0:T(8,128)(2,1)}, u32[]{:S(2)}, u32[]{:S(2)}) async-start(bf16[64,128,256]{2,1,0:T(8,128)(2,1)} %copy-done), calls=%async_computation.1 | async-start | bytes 8388608 | tf_op jit(solution)/shard_map/all_to_all | solution.py:335
  37.4 1.2 copy-start.21
  37.4 1.5 copy-start.22
  38.9 0.9 copy-start.24
  39.8 5.1 %copy-start.25 = (s32[2048,1]{0,1:T(1,128)S(1)}, s32[2048,1]{0,1:T(1,128)}, u32[]{:S(2)}) copy-start(s32[2048,1]{0,1:T(1,128)} %param.21) | copy-start | bytes 24580
  41.1 6.9 %copy-start.1 = (bf16[1664,512]{1,0:T(8,128)(2,1)}, bf16[1664,512]{1,0:T(8,128)(2,1)S(1)}, u32[]{:S(2)}) copy-start(bf16[1664,512]{1,0:T(8,128)(2,1)S(1)} %get-tuple-element.27.w0_ref) | copy-start | bytes 5111812
  41.1 93.8 %collective-permute-start.4 = (bf16[1664,512]{1,0:T(8,128)(2,1)}, bf16[1664,512]{1,0:T(8,128)(2,1)}, u32[]{:S(2)}, u32[]{:S(2)}) collective-permute-start(bf16[1664,512]{1,0:T(8,128)(2,1)} %get-tuple-element.26), channel_id=1, source_target_pairs={{0,2},{1,3},{2,0},{3,1},{4,6},{5,7},{6,4},{7,5},{8,10},{9,11},{10,... | collective-permute-start | bytes 5111816 | tf_op jit(solution)/shard_map/ppermute | solution.py:331
  43.9 91.1 %collective-permute-start.5 = (bf16[1664,512]{1,0:T(8,128)(2,1)}, bf16[1664,512]{1,0:T(8,128)(2,1)}, u32[]{:S(2)}, u32[]{:S(2)}) collective-permute-start(bf16[1664,512]{1,0:T(8,128)(2,1)} %get-tuple-element.26), channel_id=1, source_target_pairs={{0,3},{1,2},{2,1},{3,0},{4,7},{5,6},{6,5},{7,4},{8,11},{9,10},{10,... | collective-permute-start | bytes 5111816 | tf_op jit(solution)/shard_map/ppermute | solution.py:331
  44.7 90.2 %collective-permute-start.3 = (bf16[1664,512]{1,0:T(8,128)(2,1)S(1)}, bf16[1664,512]{1,0:T(8,128)(2,1)}, u32[]{:S(2)}, u32[]{:S(2)}) collective-permute-start(bf16[1664,512]{1,0:T(8,128)(2,1)S(1)} %get-tuple-element.27.w0_ref), channel_id=1, source_target_pairs={{0,1},{1,0},{2,3},{3,2},{4,5},{5,4},{6,7},{7,6},{8,9},{9,8},{10,11... | collective-permute-start | bytes 5111816 | tf_op jit(solution)/shard_map/ppermute | solution.py:331
  46.3 4.6 %copy-start.26 = (s32[16,12]{1,0:T(8,128)S(1)}, s32[16,12]{1,0:T(8,128)}, u32[]{:S(2)}) copy-start(s32[16,12]{1,0:T(8,128)} %param.20) | copy-start | bytes 2308
  51.0 1.6 copy-start.4
  57.2 1.2 copy-start.7
  87.6 36.8 %all-to-all-start.3 = ((bf16[32,48,512]{2,1,0:T(8,128)(2,1)}), bf16[32,48,512]{2,1,0:T(8,128)(2,1)S(1)}, u32[]{:S(2)}, u32[]{:S(2)}) async-start(bf16[32,48,512]{2,1,0:T(8,128)(2,1)} %copy-done.7), calls=%async_computation.3 | async-start | bytes 3145728 | tf_op jit(solution)/shard_map/all_to_all | solution.py:335
  94.8 4.0 %copy-start.12 = (bf16[16,128,256]{2,1,0:T(8,128)(2,1)S(1)}, bf16[16,128,256]{2,1,0:T(8,128)(2,1)}, u32[]{:S(2)}) copy-start(bf16[16,128,256]{2,1,0:T(8,128)(2,1)} %copy-done.11) | copy-start | bytes 3145732
  94.8 3.9 %copy-start.20 = (bf16[2048,128]{1,0:T(8,128)(2,1)S(1)}, bf16[2048,128]{1,0:T(8,128)(2,1)}, u32[]{:S(2)}) copy-start(bf16[2048,128]{1,0:T(8,128)(2,1)} %copy-done.19) | copy-start | bytes 1572868
  121.5 1.2 copy-start.5
  122.6 1.0 copy-start.9
  123.6 0.8 copy-start.13
  124.4 34.7 %copy-start.18 = (f32[512]{0:T(512)S(1)}, f32[512]{0:T(512)}, u32[]{:S(2)}) copy-start(f32[512]{0:T(512)} %param.15) | copy-start | bytes 6148
  124.4 34.7 %all-to-all-start.2 = ((bf16[128,48,128]{2,1,0:T(8,128)(2,1)}), bf16[128,48,128]{2,1,0:T(8,128)(2,1)}, u32[]{:S(2)}, u32[]{:S(2)}) async-start(bf16[128,48,128]{2,1,0:T(8,128)(2,1)} %bitcast.47), calls=%async_computation.2 | async-start | bytes 3145728 | tf_op jit(solution)/shard_map/all_to_all | solution.py:335
  176.3 1.2 copy-start.6
  177.5 46.3 %copy-start.2 = (bf16[1664,512]{1,0:T(8,128)(2,1)S(1)}, bf16[1664,512]{1,0:T(8,128)(2,1)}, u32[]{:S(2)}) copy-start(bf16[1664,512]{1,0:T(8,128)(2,1)} %copy-done.1) | copy-start | bytes 5111812
  177.5 51.7 %all-to-all-start.4 = ((bf16[128,48,128]{2,1,0:T(8,128)(2,1)}), bf16[128,48,128]{2,1,0:T(8,128)(2,1)S(1)}, u32[]{:S(2)}, u32[]{:S(2)}) async-start(bf16[128,48,128]{2,1,0:T(8,128)(2,1)} %bitcast.48), calls=%async_computation.4 | async-start | bytes 3145728 | tf_op jit(solution)/shard_map/all_to_all | solution.py:335
  181.5 29.6 %collective-permute-start = (bf16[2048,128]{1,0:T(8,128)(2,1)}, bf16[2048,128]{1,0:T(8,128)(2,1)S(1)}, u32[]{:S(2)}, u32[]{:S(2)}) collective-permute-start(bf16[2048,128]{1,0:T(8,128)(2,1)} %copy-done.13), channel_id=1, source_target_pairs={{0,1},{1,0},{2,3},{3,2},{4,5},{5,4},{6,7},{7,6},{8,9},{9,8},{10,11... | collective-permute-start | bytes 1572872 | tf_op jit(solution)/shard_map/ppermute | solution.py:331
  183.0 40.9 %collective-permute-start.1 = (bf16[2048,128]{1,0:T(8,128)(2,1)}, bf16[2048,128]{1,0:T(8,128)(2,1)S(1)}, u32[]{:S(2)}, u32[]{:S(2)}) collective-permute-start(bf16[2048,128]{1,0:T(8,128)(2,1)} %copy-done.13), channel_id=1, source_target_pairs={{0,2},{1,3},{2,0},{3,1},{4,6},{5,7},{6,4},{7,5},{8,10},{9,11},{10,... | collective-permute-start | bytes 1572872 | tf_op jit(solution)/shard_map/ppermute | solution.py:331
  185.4 38.4 %collective-permute-start.2 = (bf16[2048,128]{1,0:T(8,128)(2,1)}, bf16[2048,128]{1,0:T(8,128)(2,1)S(1)}, u32[]{:S(2)}, u32[]{:S(2)}) collective-permute-start(bf16[2048,128]{1,0:T(8,128)(2,1)} %copy-done.13), channel_id=1, source_target_pairs={{0,3},{1,2},{2,1},{3,0},{4,7},{5,6},{6,5},{7,4},{8,11},{9,10},{10,... | collective-permute-start | bytes 1572872 | tf_op jit(solution)/shard_map/ppermute | solution.py:331
  223.8 1.0 copy-start.14
  228.2 1.0 copy-start.15
  229.2 1.2 copy-start.8
  230.4 1.2 copy-start.10
  231.6 1.2 copy-start.16

commit v2 on v1

v2 whole, which is shorter than its diff:
```python
import math

import jax
import jax.numpy as jnp
from jax import lax
from jax.experimental import pallas as pl
from jax.experimental.pallas import tpu as pltpu
from jax.sharding import PartitionSpec as P

HEAD_DIM = 64
ROWS_BLK = 128
LOCAL_REFS = 4
CAP_H = 2
CAP_E = 96
EPS = 1e-06
LANES = 128

VMEM = pl.BlockSpec(memory_space=pltpu.VMEM)
SMEM = pl.BlockSpec(memory_space=pltpu.SMEM)
ANY = pl.BlockSpec(memory_space=pl.ANY)
HBM = pl.BlockSpec(memory_space=pltpu.HBM)
F32 = jnp.float32
BF16 = jnp.bfloat16


def params(mebibytes):
    return pltpu.CompilerParams(vmem_limit_bytes=mebibytes * 2**20)


def cost(flops, moved, transcendentals=0):
    return pl.CostEstimate(flops=flops, bytes_accessed=moved, transcendentals=transcendentals)


def head_units(values):
    low = lax.broadcasted_iota(jnp.int32, values.shape, 1) < HEAD_DIM
    squares = values * values
    first = jnp.sum(jnp.where(low, squares, 0.0), axis=1, keepdims=True)
    second = jnp.sum(jnp.where(low, 0.0, squares), axis=1, keepdims=True)
    scale = lax.rsqrt(jnp.where(low, first, second) * (1.0 / HEAD_DIM) + EPS)
    return values * scale


def qkv_kernel(x_ref, w_ref, scale_ref, _, q_ref, kv_ref):
    x = x_ref[...]
    rows = x.shape[0]
    query = jnp.dot(x, w_ref[0], preferred_element_type=F32)
    low = lax.broadcasted_iota(jnp.int32, (1, LANES), 1) < HEAD_DIM
    scale = jnp.where(low, scale_ref[0], scale_ref[1]) * (1.0 / math.sqrt(HEAD_DIM))
    q_ref[...] = (head_units(query) * scale).astype(BF16)
    key = jnp.dot(x, w_ref[1], preferred_element_type=F32)
    value = jnp.dot(x, w_ref[2], preferred_element_type=F32)
    kv_ref[:, :, :LANES] = head_units(key).astype(BF16).reshape(rows // ROWS_BLK, ROWS_BLK, LANES)
    kv_ref[:, :, LANES:] = value.astype(BF16).reshape(rows // ROWS_BLK, ROWS_BLK, LANES)


def qkv(x, w, scale, after):
    rows, width = x.shape
    tile = 512
    blocks = tile // ROWS_BLK
    return pl.pallas_call(
        qkv_kernel,
        grid=(rows // tile,),
        in_specs=[
            pl.BlockSpec((tile, width), lambda i: (i, 0)),
            pl.BlockSpec((3, width, LANES), lambda i: (0, 0, 0)),
            SMEM,
            ANY,
        ],
        out_specs=[
            pl.BlockSpec((tile, LANES), lambda i: (i, 0)),
            pl.BlockSpec((blocks, ROWS_BLK, 2 * LANES), lambda i: (i, 0, 0)),
        ],
        out_shape=[
            jax.ShapeDtypeStruct((rows, LANES), BF16),
            jax.ShapeDtypeStruct((rows // ROWS_BLK, ROWS_BLK, 2 * LANES), BF16),
        ],
        compiler_params=params(60),
        cost_estimate=cost(2 * rows * width * 3 * LANES, 2 * rows * (width + 3 * LANES)),
        name="qkv",
    )(x, w, scale, after)


def split_kernel(me_ref, gate_ref, up_ref, down_ref, out_w_ref, kept_ref, given_ref, sems):
    which = me_ref[0] // 2
    width = gate_ref.shape[1]
    copies = []
    for target, index in ((kept_ref, which), (given_ref, 1 - which)):
        for i, source in enumerate((gate_ref, up_ref, down_ref)):
            copies.append((source.at[index], target.at[pl.ds(i * width, width)]))
        copies.append((out_w_ref, target.at[pl.ds(3 * width, LANES)]))
    copies = [pltpu.make_async_copy(a, b, sems.at[i]) for i, (a, b) in enumerate(copies)]
    for copy in copies:
        copy.start()
    for copy in copies:
        copy.wait()


def split_weights(me, gate, up, down, out_w):
    width = gate.shape[1]
    out = jax.ShapeDtypeStruct((3 * width + LANES, width), BF16)
    return pl.pallas_call(
        split_kernel,
        in_specs=[SMEM] + [HBM] * 4,
        out_specs=[HBM, HBM],
        out_shape=[out, out],
        scratch_shapes=[pltpu.SemaphoreType.DMA((8,))],
        compiler_params=params(60),
        cost_estimate=cost(0, 4 * out.size * 2),
        name="split_weights",
    )(me, gate, up, down, out_w)


def pick_kernel(wanted_ref, kv_ref, out_ref, sems):
    count = out_ref.shape[0]
    copies = [
        pltpu.make_async_copy(
            kv_ref.at[wanted_ref[i // CAP_H, 0, i % CAP_H]], out_ref.at[i], sems.at[i]
        )
        for i in range(count)
    ]
    for copy in copies:
        copy.start()
    for copy in copies:
        copy.wait()


def pick_blocks(wanted, kv):
    count = wanted.size
    out = jax.ShapeDtypeStruct((count,) + kv.shape[1:], kv.dtype)
    return pl.pallas_call(
        pick_kernel,
        in_specs=[SMEM, VMEM],
        out_specs=HBM,
        out_shape=out,
        scratch_shapes=[pltpu.SemaphoreType.DMA((count,))],
        compiler_params=params(60),
        cost_estimate=cost(0, 2 * out.size * 2),
        name="pick_blocks",
    )(wanted, kv)


def as_column(row):
    count = row.shape[1]
    shape = (count, count)
    same = lax.broadcasted_iota(jnp.int32, shape, 0) == lax.broadcasted_iota(jnp.int32, shape, 1)
    return jnp.sum(jnp.where(same, row.astype(F32), 0.0), axis=1, keepdims=True)


def attention_kernel(
    near_ref, far_ref, q_ref, kv_ref, halo_ref, spot_ref, lane_ref, *rest
):
    heads_ref, send_ref, keys, values, spread = rest[-5:]
    blocks = kv_ref.shape[0]
    together = keys.shape[0]
    nears, fars = near_ref.shape[1], far_ref.shape[1]
    low = lax.broadcasted_iota(jnp.int32, (ROWS_BLK, LANES), 1) < HEAD_DIM

    @pl.loop(0, blocks // together)
    def _(i):
        at = [i * together + t for t in range(together)]
        at_rows = [pl.ds(pl.multiple_of(b * ROWS_BLK, ROWS_BLK), ROWS_BLK) for b in at]
        scores = []
        for t, (b, rows) in enumerate(zip(at, at_rows)):
            q = q_ref[rows, :].astype(F32)
            both = jnp.concatenate([jnp.where(low, q, 0.0), jnp.where(low, 0.0, q)], axis=0).astype(BF16)
            for j in range(nears + fars):
                if j < nears:
                    block = kv_ref[near_ref[b, j]]
                else:
                    block = halo_ref[far_ref[b, j - nears]]
                keys[t, j * ROWS_BLK : (j + 1) * ROWS_BLK, :] = block[:, :LANES]
                values[t, j * ROWS_BLK : (j + 1) * ROWS_BLK, :] = block[:, LANES:]
            scores.append(
                lax.dot_general(both, keys[t], (((1,), (1,)), ((), ())), preferred_element_type=F32)
            )
        for t, rows in enumerate(at_rows):
            largest = jnp.max(scores[t], axis=1, keepdims=True)
            expo = jnp.exp(scores[t] - largest)
            total = jnp.sum(expo, axis=1, keepdims=True)
            out = jnp.dot(expo.astype(BF16), values[t], preferred_element_type=F32) / total
            heads = jnp.where(low, out[:ROWS_BLK], out[ROWS_BLK:])
            heads_ref[rows, :] = heads.astype(BF16)
            lane = as_column(lane_ref[:, rows])
            for m in range(4):
                spread[rows, m * LANES : (m + 1) * LANES] = jnp.where(lane == m, heads, 0.0).astype(BF16)

    dests, cap = send_ref.shape[0], send_ref.shape[2]
    step = 4

    @pl.loop(0, dests // step)
    def _(i):
        tile = step * cap
        spot = spot_ref[...]
        here = lax.broadcasted_iota(jnp.int32, (tile, spot.shape[1]), 0) + i * tile
        hot = jnp.where(here == spot, 1.0, 0.0).astype(BF16)
        placed = jnp.dot(hot, spread[...], preferred_element_type=F32).astype(BF16)
        for d in range(step):
            for m in range(4):
                send_ref[i * step + d, m] = placed[d * cap : (d + 1) * cap, m * LANES : (m + 1) * LANES]


def attention(near, far, q, kv, halo, spot_row, lane_row, after, parts, cap, together=4):
    rows = q.shape[0]
    keys = (near.shape[1] + far.shape[1]) * ROWS_BLK
    return pl.pallas_call(
        attention_kernel,
        in_specs=[SMEM, SMEM, VMEM, VMEM, VMEM, VMEM, VMEM] + [ANY] * len(after),
        out_specs=[VMEM, VMEM],
        out_shape=[
            jax.ShapeDtypeStruct((rows, LANES), BF16),
            jax.ShapeDtypeStruct((parts, 4, cap, LANES), BF16),
        ],
        scratch_shapes=[
            pltpu.VMEM((together, keys, LANES), BF16),
            pltpu.VMEM((together, keys, LANES), BF16),
            pltpu.VMEM((rows, 4 * LANES), BF16),
        ],
        compiler_params=params(60),
        cost_estimate=cost(12 * 10**9, 8 * 2**20, 2 * rows * keys),
        name="attention",
    )(near, far, q, kv, halo, spot_row, lane_row, *after)


def place_kernel(spot_ref, x_ref, out_ref):
    dests, cap = out_ref.shape[0], out_ref.shape[1]
    step = 4

    @pl.loop(0, dests // step)
    def _(i):
        tile = step * cap
        spot = spot_ref[...]
        here = lax.broadcasted_iota(jnp.int32, (tile, spot.shape[1]), 0) + i * tile
        hot = jnp.where(here == spot, 1.0, 0.0).astype(BF16)
        placed = jnp.dot(hot, x_ref[...], preferred_element_type=F32).astype(BF16)
        for d in range(step):
            out_ref[i * step + d] = placed[d * cap : (d + 1) * cap, :]


def place_rows(spot_row, x, parts, cap):
    rows, width = x.shape
    return pl.pallas_call(
        place_kernel,
        in_specs=[VMEM, VMEM],
        out_specs=VMEM,
        out_shape=jax.ShapeDtypeStruct((parts, cap, width), BF16),
        compiler_params=params(60),
        cost_estimate=cost(2 * parts * cap * rows * width, 4 * 2**20),
        name="place_rows",
    )(spot_row, x)


def experts_kernel(me_ref, gain_ref, route_ref, h_ref, x_ref, w0_ref, w1_ref, w2_ref, w3_ref, *rest):
    out_ref, heads, features, project, quarters, results, sems = rest[-7:]
    me = me_ref[0]
    tiles, step, cap, width = features.shape
    tile = step * cap
    sources = (w0_ref, w1_ref, w2_ref, w3_ref)
    sizes = ((h_ref, heads), (x_ref, features))
    small = [
        pltpu.make_async_copy(
            w.at[pl.ds(3 * width, LANES)], project.at[pl.ds(k * LANES, LANES)], sems.at[k]
        )
        for k, w in enumerate(sources)
    ]
    large = [
        pltpu.make_async_copy(w.at[pl.ds(0, 3 * width)], quarters.at[k], sems.at[4 + k])
        for k, w in enumerate(sources)
    ]
    rows = [
        [
            pltpu.make_async_copy(source.at[pl.ds(t * step, step)], target.at[t], sems.at[8 + 2 * t + i])
            for i, (source, target) in enumerate(sizes)
        ]
        for t in range(tiles)
    ]
    outs = [
        pltpu.make_async_copy(
            results.at[t], out_ref.at[pl.ds(t * step, step)], sems.at[8 + 2 * tiles + t]
        )
        for t in range(tiles)
    ]
    for copy in rows[0] + small + large + [c for later in rows[1:] for c in later]:
        copy.start()
    for copy in small:
        copy.wait()
    for t in range(tiles):
        for copy in rows[t]:
            copy.wait()
        arrived = jnp.concatenate([heads[t, :, me ^ k].reshape(tile, LANES) for k in range(4)], axis=1)
        mixed = features[t].reshape(tile, width).astype(F32) + jnp.dot(
            arrived, project[...], preferred_element_type=F32
        )
        mean = jnp.mean(mixed * mixed, axis=1, keepdims=True)
        normed = (mixed * lax.rsqrt(mean + EPS) * gain_ref[...]).astype(BF16)
        logit = jnp.sum(normed.astype(F32) * route_ref[...], axis=1, keepdims=True)
        gate = 1.0 / (1.0 + jnp.exp(-logit))
        result = None
        for k in range(4):
            if t == 0:
                large[k].wait()
            left = jnp.dot(normed, quarters[k, :width, :], preferred_element_type=F32)
            right = jnp.dot(normed, quarters[k, width : 2 * width, :], preferred_element_type=F32)
            half = 0.5 * left
            hidden = ((half + half * jnp.tanh(half)) * right).astype(BF16)
            term = jnp.dot(hidden, quarters[k, 2 * width :, :], preferred_element_type=F32)
            result = term if result is None else result + term
        result = (gate * result).astype(BF16).reshape(step, cap, width)
        for m in range(4):
            results[t, :, m] = result[:, :, m * LANES : (m + 1) * LANES]
        outs[t].start()
    for copy in outs:
        copy.wait()


def experts(me, heads, x, gain, route, weights, after, tiles=2):
    parts, cap, width = x.shape
    step = parts // tiles
    return pl.pallas_call(
        experts_kernel,
        in_specs=[SMEM, VMEM, VMEM, HBM, HBM] + [ANY] * (4 + len(after)),
        out_specs=HBM,
        out_shape=jax.ShapeDtypeStruct((parts, 4, cap, LANES), BF16),
        scratch_shapes=[
            pltpu.VMEM((tiles, step, 4, cap, LANES), BF16),
            pltpu.VMEM((tiles, step, cap, width), BF16),
            pltpu.VMEM((width, width), BF16),
            pltpu.VMEM((4, 3 * width, width), BF16),
            pltpu.VMEM((tiles, step, 4, cap, LANES), BF16),
            pltpu.SemaphoreType.DMA((8 + 3 * tiles,)),
        ],
        compiler_params=params(59),
        cost_estimate=cost(2 * parts * cap * width * (12 * width + width), 12 * 2**20),
        name="experts",
    )(me, gain, route, heads, x, *weights, *after)


def columns_kernel(
    me_ref, h0_ref, h1_ref, h2_ref, h3_ref, w0_ref, w1_ref, w2_ref, w3_ref, x_ref, attn_ref, mixed_ref
):
    columns = pl.ds(pl.multiple_of(me_ref[0] * LANES, LANES), LANES)
    total = None
    for h, w in zip((h0_ref, h1_ref, h2_ref, h3_ref), (w0_ref, w1_ref, w2_ref, w3_ref)):
        term = jnp.dot(h[...], w[:, columns], preferred_element_type=F32)
        total = term if total is None else total + term
    attn_ref[...] = total.astype(BF16)
    mixed_ref[...] = x_ref[:, columns].astype(F32) + total


def attention_columns(me, heads, weights, x):
    rows, width = x.shape
    last = weights[0].shape[0] // LANES - 1
    out = pl.BlockSpec((rows, LANES), lambda i: (0, 0))
    return pl.pallas_call(
        columns_kernel,
        grid=(1,),
        in_specs=[SMEM]
        + [out] * 4
        + [pl.BlockSpec((LANES, width), lambda i: (last, 0))] * 4
        + [pl.BlockSpec((rows, width), lambda i: (0, 0))],
        out_specs=[out, out],
        out_shape=[
            jax.ShapeDtypeStruct((rows, LANES), BF16),
            jax.ShapeDtypeStruct((rows, LANES), F32),
        ],
        compiler_params=params(60),
        cost_estimate=cost(2 * rows * width * LANES, 8 * 2**20),
        name="attention_columns",
    )(me, *heads, *weights, x)


def combine_kernel(spot_ref, lane_ref, mixed_ref, back_ref, out_ref, slots, sems):
    dests, cap, width = slots.shape
    rows = out_ref.shape[0]
    copies = [
        pltpu.make_async_copy(
            back_ref.at[:, m], slots.at[:, :, pl.ds(m * LANES, LANES)], sems.at[m]
        )
        for m in range(4)
    ]
    for copy in copies:
        copy.start()
    for copy in copies:
        copy.wait()
    tile = 256
    names = lax.broadcasted_iota(jnp.int32, (ROWS_BLK, dests * cap), 1).astype(F32)

    @pl.loop(0, rows // tile)
    def _(i):
        pieces = [
            pl.ds(pl.multiple_of(i * tile + t * ROWS_BLK, ROWS_BLK), ROWS_BLK) for t in range(tile // ROWS_BLK)
        ]
        hot = jnp.concatenate(
            [jnp.where(names == as_column(spot_ref[:, p]), 1.0, 0.0).astype(BF16) for p in pieces], axis=0
        )
        found = jnp.dot(hot, slots[...].reshape(dests * cap, width), preferred_element_type=F32)
        for t, p in enumerate(pieces):
            lane = as_column(lane_ref[:, p])
            total = mixed_ref[p, :]
            for m in range(4):
                part = found[t * ROWS_BLK : (t + 1) * ROWS_BLK, m * LANES : (m + 1) * LANES]
                total = total + jnp.where(lane == m, part, 0.0)
            out_ref[p, :] = total.astype(BF16)


def combine(spot_row, lane_row, back, mixed):
    rows = mixed.shape[0]
    slots = back.shape[0] * back.shape[2]
    return pl.pallas_call(
        combine_kernel,
        in_specs=[VMEM] * 3 + [HBM],
        out_specs=VMEM,
        out_shape=jax.ShapeDtypeStruct((rows, LANES), BF16),
        scratch_shapes=[
            pltpu.VMEM((back.shape[0], back.shape[2], 4 * LANES), BF16),
            pltpu.SemaphoreType.DMA((4,)),
        ],
        compiler_params=params(24),
        cost_estimate=cost(2 * rows * slots * 4 * LANES, 4 * 2**20),
        name="combine",
    )(spot_row, lane_row, mixed, back)


def swap(array, change):
    return lax.ppermute(array, "mp", [(i, i ^ change) for i in range(4)])


def exchange(array, axes):
    return lax.all_to_all(array, axes, split_axis=0, concat_axis=0, tiled=True)


def on_device(
    node_features,
    w_qkv,
    w_out,
    head_scale,
    norm_gain,
    router,
    w_gate,
    w_up,
    w_down,
    neighbor_blocks,
    expert_ids,
):
    parts = lax.axis_size("graph")
    part = lax.axis_index("graph")
    me = lax.axis_index("mp")
    rows, width = node_features.shape
    blocks = rows // ROWS_BLK
    half_cap = CAP_E // 2

    far = neighbor_blocks[:, LOCAL_REFS:]
    names = jnp.arange(parts * blocks, dtype=jnp.int32).reshape(parts, blocks)
    wanted = jnp.any(far.reshape(-1)[:, None, None] == names[None], axis=0)
    inside = jnp.arange(blocks, dtype=jnp.int32)[None, :]
    first = jnp.min(jnp.where(wanted, inside, blocks - 1), axis=1)
    last = jnp.max(jnp.where(wanted, inside, 0), axis=1)
    requests = jnp.stack([first, last], axis=1)
    incoming = exchange(requests.reshape(parts, 1, CAP_H), "graph")
    bases = jnp.arange(parts, dtype=jnp.int32)[:, None] * blocks
    pool = (bases + requests).reshape(-1)
    slots = jnp.arange(pool.shape[0], dtype=jnp.int32)
    far_slots = jnp.max(jnp.where(far[:, :, None] == pool[None, None, :], slots[None, None, :], 0), axis=2)
    near_slots = neighbor_blocks[:, :LOCAL_REFS] - part * blocks

    which = me // 2
    me_ref = me[None].astype(jnp.int32)
    kept, given = split_weights(me_ref, w_gate, w_up, w_down, w_out)
    weights = [kept, swap(kept, 1), swap(given, 2), swap(given, 3)]

    q, kv = qkv(node_features, w_qkv, head_scale, kept)
    halo = exchange(pick_blocks(incoming, kv), "graph")

    routed = expert_ids[:, 0]
    experts_all = router.shape[1]
    chosen = routed[:, None] == jnp.arange(experts_all, dtype=jnp.int32)[None, :]
    row_ids = jnp.arange(rows, dtype=jnp.int32)
    earlier = (row_ids[:, None] > row_ids[None, :]).astype(BF16)
    before = jnp.dot(earlier, chosen.astype(BF16), preferred_element_type=F32)
    rank = jnp.sum(jnp.where(chosen, before, 0.0), axis=1).astype(jnp.int32)
    second = (rank >= half_cap).astype(jnp.int32)
    lane = (routed % 2) * 2 + second
    spot = (routed // 2) * half_cap + rank - second * half_cap
    spot_row, lane_row = spot[None, :], lane[None, :]
    mine_row = jnp.where(lane == me, spot, -1)[None, :]
    x_there = exchange(place_rows(mine_row, node_features, parts, half_cap), "graph")

    route = lax.dynamic_index_in_dim(router, 2 * part + which, 1, keepdims=False).astype(F32)[None, :]
    heads, send = attention(
        near_slots, far_slots, q, kv, halo, spot_row, lane_row, weights[1:2], parts, half_cap
    )
    send, x_there, weights[2:] = lax.optimization_barrier((send, x_there, weights[2:]))
    heads_there = exchange(send.reshape(parts * 4, half_cap, LANES), ("graph", "mp"))
    all_heads = [heads] + [swap(heads, k) for k in (1, 2, 3)]
    attn_out, mixed = attention_columns(me_ref, all_heads, weights, node_features)

    produced = experts(
        me_ref,
        heads_there.reshape(parts, 4, half_cap, LANES),
        x_there,
        norm_gain[None, :],
        route,
        weights,
        all_heads[1:],
    )
    back = exchange(produced.reshape(parts * 4, half_cap, LANES), ("graph", "mp"))
    layer_out = combine(spot_row, lane_row, back.reshape(parts, 4, half_cap, LANES), mixed)
    return (attn_out, layer_out)


def solution(mesh):
    placed = (
        P("graph", None),
        P(None, None, "mp"),
        P("mp", None),
        P("mp"),
        P(),
        P(),
        P("graph", None, "mp"),
        P("graph", None, "mp"),
        P("graph", "mp", None),
        P("graph", None),
        P("graph", None),
    )
    return jax.shard_map(
        on_device,
        mesh=mesh,
        in_specs=placed,
        out_specs=(P("graph", "mp"), P("graph", "mp")),
        check_vma=False,
    )
```

time: 240 us -> 324 us (1.35)
  Pallas kernels: 63.5 us -> 167 us
  local copies, waits for them, and re-layouts: 26.7 us -> 4.74 us
  other arithmetic: 8.68 us -> 4.45 us
  waiting for transfers between devices: 91.8 us -> 95.6 us
  starting transfers between devices: 45.6 us -> 49 us
    pallas_call x3 -> x4, Pallas kernels: 30.2 us -> 131 us  [the longest x1 104 us: split_weights(): pl.pallas_call(split_kernel, in_specs=[SMEM] + [HBM] * 4, out_specs=[HBM,...]
    unnamed x55 -> x18, local copies, waits for them, and re-layouts: 21.5 us -> 3 us
    all_to_all x5, waiting for transfers between devices: 53.4 us -> 58.4 us  [exchange(): return lax.all_to_all(array, axes, split_axis=0, concat_axis=0, tiled=True)]
    sub x1 -> x0, other arithmetic: 3.93 us -> none  [on_device(): spot = routed // 2 * half_cap + rank - second * half_cap]
  transfers between devices with their start and end apart: 11 -> 11, of which waited for: 4 -> 5; matrix products, arithmetic and copies ran while one was open for 6% -> 2% of each run, Pallas kernels for 14% -> 44%
where the time goes in v2:
time: 324 us; the launch traced here: 323 us
  Pallas kernels  167 us (52%)
  waiting for transfers between devices  95.6 us (30%)
  starting transfers between devices  49 us (15%)
  local copies, waits for them, and re-layouts  4.74 us (1%)
  other arithmetic  4.45 us (1%)
    pallas_call x1, Pallas kernels, split_weights(): pl.pallas_call(split_kernel, in_specs=[SMEM] + [HBM] * 4, out_specs=[HBM,...  104 us
    all_to_all x5, waiting for transfers between devices, exchange(): return lax.all_to_all(array, axes, split_axis=0, concat_axis=0, tiled=True)  58.4 us
    all_to_all x5, starting transfers between devices, exchange(): return lax.all_to_all(array, axes, split_axis=0, concat_axis=0, tiled=True)  41.1 us
    ppermute x6, waiting for transfers between devices, swap(): return lax.ppermute(array, 'mp', [(i, i ^ change) for i in range(4)])  37.2 us
    pallas_call x1, Pallas kernels, attention(): pl.pallas_call(attention_kernel, in_specs=[SMEM, SMEM, VMEM, VMEM, VMEM,...  19.6 us
    pallas_call x1, Pallas kernels, experts(): pl.pallas_call(experts_kernel, in_specs=[SMEM, VMEM, VMEM, HBM, HBM] + [A...  16.3 us
    ppermute x6, starting transfers between devices, swap(): return lax.ppermute(array, 'mp', [(i, i ^ change) for i in range(4)])  7.89 us
    pallas_call x1, Pallas kernels, place_rows(): pl.pallas_call(place_kernel, in_specs=[VMEM, VMEM], out_specs=VMEM, out_s...  7.4 us
  transfers between devices with their start and end apart: 11, of which 5 were waited for; matrix products, arithmetic and copies ran while one was open for 2% of the time, Pallas kernels for 44%

profile of v2, /device:TPU:1, one launch (start us, length us, event | category | flops | bytes accessed | tf_op | source)
XLA Modules:
  0.0 323.4 jit_solution(3667265970983797054)
XLA Ops:
  0.7 0.8 slice.7
  1.4 0.1 eq.59
  1.5 0.7 compare_reduce_fusion
  2.2 0.1 select_reduce_fusion.2
  2.4 0.7 copy.20
  3.1 9.6 %all-to-all-start = ((s32[32,1,2]{2,1,0:T(1,128)}), s32[32,1,2]{2,1,0:T(1,128)S(1)}, u32[]{:S(2)}, u32[]{:S(2)}) async-start(s32[32,1,2]{2,1,0:T(1,128)} %copy.20), calls=%async_computation | async-start | bytes 32768 | tf_op jit(solution)/shard_map/all_to_all | solution.py:428
  12.7 104.4 %split_weights.1 = (bf16[1664,512]{1,0:T(8,128)(2,1)}, bf16[1664,512]{1,0:T(8,128)(2,1)}) custom-call(s32[1]{0:T(128)} %bitcast.me_ref, bf16[2,512,512]{2,1,0:T(8,128)(2,1)} %gate_ref.1, bf16[2,512,512]{2,1,0:T(8,128)(2,1)} %up_ref.1, bf16[2,512,512]{2,1,0:T(8,128)(2,1)} %down_ref.1, bf16[128,512]{1,0:T(8,128)(2,1)} %out_w_ref.1), custom_call_target="tpu_custom_call" | custom-call | bytes 6815744 | tf_op jit(solution)/shard_map/split_weights/pallas_call | solution.py:101
  117.1 5.1 %qkv.1 = (bf16[2048,128]{1,0:T(8,128)(2,1)}, bf16[16,128,256]{2,1,0:T(8,128)(2,1)}) custom-call(bf16[2048,512]{1,0:T(8,128)(2,1)} %x_ref.5, bf16[3,512,128]{2,1,0:T(8,128)(2,1)} %w_ref.1, f32[2]{0:T(128)} %scale_ref.1, bf16[1664,512]{1,0:T(8,128)(2,1)} %get-tuple-element.14._.w0_ref), custom_call_target="tpu_custom_call" | custom-call | flops 805306368 | bytes 3670016 | tf_op jit(solution)/shard_map/qkv/pallas_call | solution.py:60
  122.2 0.0 all-to-all-done.wanted_ref
  122.2 0.0 copy-start.6
  122.2 0.6 copy-done.6
  122.8 3.8 %pick_blocks.1 = bf16[64,128,256]{2,1,0:T(8,128)(2,1)} custom-call(s32[32,1,2]{2,1,0:T(1,128)} %copy-done.6, bf16[16,128,256]{2,1,0:T(8,128)(2,1)} %get-tuple-element.16.kv_ref), custom_call_target="tpu_custom_call" | custom-call | bytes 8388608 | tf_op jit(solution)/shard_map/pick_blocks/pallas_call | solution.py:130
  126.6 0.0 copy-start.3
  126.6 0.0 copy-start.8
  126.7 7.6 %all-to-all-start.1 = ((bf16[64,128,256]{2,1,0:T(8,128)(2,1)}), bf16[64,128,256]{2,1,0:T(8,128)(2,1)}, u32[]{:S(2)}, u32[]{:S(2)}) async-start(bf16[64,128,256]{2,1,0:T(8,128)(2,1)} %pick_blocks.1), calls=%async_computation.1 | async-start | bytes 8388608 | tf_op jit(solution)/shard_map/all_to_all | solution.py:428
  134.2 0.0 copy-done.3
  134.3 1.3 collective-permute-start
  135.5 2.5 collective-permute-start.4
  138.0 0.2 collective-permute-start.5
  138.2 0.0 copy-done.8
  138.2 1.7 fusion.2
  139.9 0.7 compare_select_fusion
  140.6 7.4 %place_rows.1 = bf16[32,48,512]{2,1,0:T(8,128)(2,1)} custom-call(s32[1,2048]{1,0:T(1,128)} %get-tuple-element.28.spot_ref, bf16[2048,512]{1,0:T(8,128)(2,1)} %x_ref.5), custom_call_target="tpu_custom_call" | custom-call | flops 3221225472 | bytes 4194304 | tf_op jit(solution)/shard_map/place_rows/pallas_call | solution.py:241
  148.0 0.0 copy-start.7
  148.0 36.6 %all-to-all-done.1.halo_ref = bf16[64,128,256]{2,1,0:T(8,128)(2,1)} async-done(((bf16[64,128,256]{2,1,0:T(8,128)(2,1)}), bf16[64,128,256]{2,1,0:T(8,128)(2,1)}, u32[]{:S(2)}, u32[]{:S(2)}) %all-to-all-start.1) | async-done | bytes 4194336 | tf_op jit(solution)/shard_map/all_to_all | solution.py:428
  184.5 7.1 %all-to-all-start.2 = ((bf16[32,48,512]{2,1,0:T(8,128)(2,1)}), bf16[32,48,512]{2,1,0:T(8,128)(2,1)S(1)}, u32[]{:S(2)}, u32[]{:S(2)}) async-start(bf16[32,48,512]{2,1,0:T(8,128)(2,1)} %place_rows.1), calls=%async_computation.2 | async-start | bytes 3145728 | tf_op jit(solution)/shard_map/all_to_all | solution.py:428
  191.7 0.1 copy.19
  191.7 0.1 add.88
  191.9 1.0 select_reduce_fusion.far_ref
  192.9 0.0 copy-done.7
  192.9 0.6 slice_subtract_fusion.near_ref
  193.5 0.0 collective-permute-done.rest_0_.w1_ref
  193.5 19.6 %attention.1 = (bf16[2048,128]{1,0:T(8,128)(2,1)}, bf16[32,4,48,128]{3,2,1,0:T(8,128)(2,1)}) custom-call(s32[16,4]{1,0:T(8,128)} %slice_subtract_fusion.near_ref, s32[16,8]{1,0:T(8,128)} %select_reduce_fusion.far_ref, bf16[2048,128]{1,0:T(8,128)(2,1)} %get-tuple-element.15.q_ref, bf16[16,128,256]{2,1,0:T(8,128)(2,1)} %get-tuple-element.16.kv_ref, ...), custom_call_target="tpu_custom_call" | custom-call | flops 12000000000 | bytes 8388608 | tf_op jit(solution)/shard_map/attention/pallas_call | solution.py:205
  213.1 0.9 all-to-all-done.2.x_ref
  213.9 0.0 copy-start.4
  213.9 0.0 collective-permute-done.4.w2_ref
  213.9 0.0 collective-permute-done.5.w3_ref
  213.9 8.6 %all-to-all-start.3 = ((bf16[128,48,128]{2,1,0:T(8,128)(2,1)}), bf16[128,48,128]{2,1,0:T(8,128)(2,1)S(1)}, u32[]{:S(2)}, u32[]{:S(2)}) async-start(bf16[128,48,128]{2,1,0:T(8,128)(2,1)} %bitcast.35), calls=%async_computation.3 | async-start | bytes 3145728 | tf_op jit(solution)/shard_map/all_to_all | solution.py:428
  222.5 1.5 collective-permute-start.1
  224.0 2.4 collective-permute-start.2
  226.4 0.1 collective-permute-start.3
  226.4 1.3 bitcast_convert_fusion.route_ref
  227.7 24.5 %collective-permute-done.1.h1_ref.rest_0_ = bf16[2048,128]{1,0:T(8,128)(2,1)} collective-permute-done((bf16[2048,128]{1,0:T(8,128)(2,1)}, bf16[2048,128]{1,0:T(8,128)(2,1)}, u32[]{:S(2)}, u32[]{:S(2)}) %collective-permute-start.1) | collective-permute-done | bytes 524320 | tf_op jit(solution)/shard_map/ppermute | solution.py:424
  252.2 12.7 %collective-permute-done.2.h2_ref.rest_1_ = bf16[2048,128]{1,0:T(8,128)(2,1)} collective-permute-done((bf16[2048,128]{1,0:T(8,128)(2,1)}, bf16[2048,128]{1,0:T(8,128)(2,1)}, u32[]{:S(2)}, u32[]{:S(2)}) %collective-permute-start.2) | collective-permute-done | bytes 524320 | tf_op jit(solution)/shard_map/ppermute | solution.py:424
  264.9 0.0 collective-permute-done.3.h3_ref.rest_2_
  264.9 0.0 all-to-all-done.3
  264.9 0.0 copy-start.5
  264.9 0.0 copy-done.4
  264.9 1.1 copy-done.5
  266.1 16.3 %experts.1 = bf16[32,4,48,128]{3,2,1,0:T(8,128)(2,1)} custom-call(s32[1]{0:T(128)} %bitcast.me_ref, f32[1,512]{1,0:T(1,128)} %bitcast.42, f32[1,512]{1,0:T(1,128)} %bitcast_convert_fusion.route_ref, bf16[32,4,48,128]{3,2,1,0:T(8,128)(2,1)} %bitcast.36, bf16[32,48,512]{2,1,0:T(8,128)(2,1)} %copy-done.4, bf16[1664,512]{1,0:T(8,128)(2,1)} %get-tuple-element.14._.w0_ref, ...), custom_call_target="tpu_custom_call" | custom-call | flops 10468982784 | bytes 12582912 | tf_op jit(solution)/shard_map/experts/pallas_call | solution.py:318
  282.4 8.3 %all-to-all-start.4 = ((bf16[128,48,128]{2,1,0:T(8,128)(2,1)}), bf16[128,48,128]{2,1,0:T(8,128)(2,1)S(1)}, u32[]{:S(2)}, u32[]{:S(2)}) async-start(bf16[128,48,128]{2,1,0:T(8,128)(2,1)} %bitcast.37), calls=%async_computation.4 | async-start | bytes 3145728 | tf_op jit(solution)/shard_map/all_to_all | solution.py:428
  290.7 0.0 copy-start
  290.7 0.0 copy-start.1
  290.7 4.3 %attention_columns.1 = (bf16[2048,128]{1,0:T(8,128)(2,1)}, f32[2048,128]{1,0:T(8,128)}) custom-call(s32[1]{0:T(128)} %bitcast.me_ref, bf16[2048,128]{1,0:T(8,128)(2,1)} %get-tuple-element.17.h0_ref, bf16[2048,128]{1,0:T(8,128)(2,1)} %collective-permute-done.1.h1_ref.rest_0_, bf16[2048,128]{1,0:T(8,128)(2,1)} %collective-permute-done.2.h2_ref.rest_1_, ...), custom_call_target="tpu_custom_call" | custom-call | flops 268435456 | bytes 8388608 | tf_op jit(solution)/shard_map/attention_columns/pallas_call | solution.py:353
  295.0 20.9 %all-to-all-done.4 = bf16[128,48,128]{2,1,0:T(8,128)(2,1)S(1)} async-done(((bf16[128,48,128]{2,1,0:T(8,128)(2,1)}), bf16[128,48,128]{2,1,0:T(8,128)(2,1)S(1)}, u32[]{:S(2)}, u32[]{:S(2)}) %all-to-all-start.4) | async-done | bytes 1572896 | tf_op jit(solution)/shard_map/all_to_all | solution.py:428
  315.9 0.0 copy-done
  315.9 0.0 copy-done.1
  315.9 0.0 copy-start.2
  315.9 1.2 copy-done.2
  317.1 6.1 %combine.1 = bf16[2048,128]{1,0:T(8,128)(2,1)} custom-call(s32[1,2048]{1,0:T(1,128)S(1)} %copy-done.1, s32[1,2048]{1,0:T(1,128)S(1)} %copy-done, f32[2048,128]{1,0:T(8,128)S(1)} %copy-done.2, bf16[32,4,48,128]{3,2,1,0:T(8,128)(2,1)S(1)} %bitcast.34), custom_call_target="tpu_custom_call" | custom-call | flops 3221225472 | bytes 4194304 | tf_op jit(solution)/shard_map/combine/pallas_call | solution.py:408
  (4 shorter events, 0.0 us)
Async XLA Ops:
  3.1 119.2 %all-to-all-start = ((s32[32,1,2]{2,1,0:T(1,128)}), s32[32,1,2]{2,1,0:T(1,128)S(1)}, u32[]{:S(2)}, u32[]{:S(2)}) async-start(s32[32,1,2]{2,1,0:T(1,128)} %copy.20), calls=%async_computation | async-start | bytes 32768 | tf_op jit(solution)/shard_map/all_to_all | solution.py:428
  122.2 0.6 copy-start.6
  126.6 7.6 %copy-start.3 = (bf16[1664,512]{1,0:T(8,128)(2,1)S(1)}, bf16[1664,512]{1,0:T(8,128)(2,1)}, u32[]{:S(2)}) copy-start(bf16[1664,512]{1,0:T(8,128)(2,1)} %get-tuple-element.14._.w0_ref) | copy-start | bytes 5111812
  126.6 11.6 %copy-start.8 = (s32[2048,1]{0,1:T(1,128)S(1)}, s32[2048,1]{0,1:T(1,128)}, u32[]{:S(2)}) copy-start(s32[2048,1]{0,1:T(1,128)} %param.21) | copy-start | bytes 24580
  126.7 57.9 %all-to-all-start.1 = ((bf16[64,128,256]{2,1,0:T(8,128)(2,1)}), bf16[64,128,256]{2,1,0:T(8,128)(2,1)}, u32[]{:S(2)}, u32[]{:S(2)}) async-start(bf16[64,128,256]{2,1,0:T(8,128)(2,1)} %pick_blocks.1), calls=%async_computation.1 | async-start | bytes 8388608 | tf_op jit(solution)/shard_map/all_to_all | solution.py:428
  134.3 59.2 %collective-permute-start = (bf16[1664,512]{1,0:T(8,128)(2,1)S(1)}, bf16[1664,512]{1,0:T(8,128)(2,1)}, u32[]{:S(2)}, u32[]{:S(2)}) collective-permute-start(bf16[1664,512]{1,0:T(8,128)(2,1)S(1)} %copy-done.3), channel_id=1, source_target_pairs={{0,1},{1,0},{2,3},{3,2},{4,5},{5,4},{6,7},{7,6},{8,9},{9,8},{10,11... | collective-permute-start | bytes 5111816 | tf_op jit(solution)/shard_map/ppermute | solution.py:424
  135.5 78.4 %collective-permute-start.4 = (bf16[1664,512]{1,0:T(8,128)(2,1)}, bf16[1664,512]{1,0:T(8,128)(2,1)}, u32[]{:S(2)}, u32[]{:S(2)}) collective-permute-start(bf16[1664,512]{1,0:T(8,128)(2,1)} %get-tuple-element.19), channel_id=1, source_target_pairs={{0,2},{1,3},{2,0},{3,1},{4,6},{5,7},{6,4},{7,5},{8,10},{9,11},{10,... | collective-permute-start | bytes 5111816 | tf_op jit(solution)/shard_map/ppermute | solution.py:424
  138.0 75.9 %collective-permute-start.5 = (bf16[1664,512]{1,0:T(8,128)(2,1)}, bf16[1664,512]{1,0:T(8,128)(2,1)}, u32[]{:S(2)}, u32[]{:S(2)}) collective-permute-start(bf16[1664,512]{1,0:T(8,128)(2,1)} %get-tuple-element.19), channel_id=1, source_target_pairs={{0,3},{1,2},{2,1},{3,0},{4,7},{5,6},{6,5},{7,4},{8,11},{9,10},{10,... | collective-permute-start | bytes 5111816 | tf_op jit(solution)/shard_map/ppermute | solution.py:424
  148.0 44.9 %copy-start.7 = (s32[16,12]{1,0:T(8,128)S(1)}, s32[16,12]{1,0:T(8,128)}, u32[]{:S(2)}) copy-start(s32[16,12]{1,0:T(8,128)} %param.20) | copy-start | bytes 2308
  184.5 29.4 %all-to-all-start.2 = ((bf16[32,48,512]{2,1,0:T(8,128)(2,1)}), bf16[32,48,512]{2,1,0:T(8,128)(2,1)S(1)}, u32[]{:S(2)}, u32[]{:S(2)}) async-start(bf16[32,48,512]{2,1,0:T(8,128)(2,1)} %place_rows.1), calls=%async_computation.2 | async-start | bytes 3145728 | tf_op jit(solution)/shard_map/all_to_all | solution.py:428
  213.9 51.0 %copy-start.4 = (bf16[32,48,512]{2,1,0:T(8,128)(2,1)}, bf16[32,48,512]{2,1,0:T(8,128)(2,1)S(1)}, u32[]{:S(2)}) copy-start(bf16[32,48,512]{2,1,0:T(8,128)(2,1)S(1)} %all-to-all-done.2.x_ref) | copy-start | bytes 4718596
  213.9 51.0 %all-to-all-start.3 = ((bf16[128,48,128]{2,1,0:T(8,128)(2,1)}), bf16[128,48,128]{2,1,0:T(8,128)(2,1)S(1)}, u32[]{:S(2)}, u32[]{:S(2)}) async-start(bf16[128,48,128]{2,1,0:T(8,128)(2,1)} %bitcast.35), calls=%async_computation.3 | async-start | bytes 3145728 | tf_op jit(solution)/shard_map/all_to_all | solution.py:428
  222.5 29.7 %collective-permute-start.1 = (bf16[2048,128]{1,0:T(8,128)(2,1)}, bf16[2048,128]{1,0:T(8,128)(2,1)}, u32[]{:S(2)}, u32[]{:S(2)}) collective-permute-start(bf16[2048,128]{1,0:T(8,128)(2,1)} %get-tuple-element.17.h0_ref), channel_id=1, source_target_pairs={{0,1},{1,0},{2,3},{3,2},{4,5},{5,4},{6,7},{7,6},{8,9},{9,8},{10,11... | collective-permute-start | bytes 1572872 | tf_op jit(solution)/shard_map/ppermute | solution.py:424
  224.0 41.0 %collective-permute-start.2 = (bf16[2048,128]{1,0:T(8,128)(2,1)}, bf16[2048,128]{1,0:T(8,128)(2,1)}, u32[]{:S(2)}, u32[]{:S(2)}) collective-permute-start(bf16[2048,128]{1,0:T(8,128)(2,1)} %get-tuple-element.17.h0_ref), channel_id=1, source_target_pairs={{0,2},{1,3},{2,0},{3,1},{4,6},{5,7},{6,4},{7,5},{8,10},{9,11},{10,... | collective-permute-start | bytes 1572872 | tf_op jit(solution)/shard_map/ppermute | solution.py:424
  226.4 38.6 %collective-permute-start.3 = (bf16[2048,128]{1,0:T(8,128)(2,1)}, bf16[2048,128]{1,0:T(8,128)(2,1)}, u32[]{:S(2)}, u32[]{:S(2)}) collective-permute-start(bf16[2048,128]{1,0:T(8,128)(2,1)} %get-tuple-element.17.h0_ref), channel_id=1, source_target_pairs={{0,3},{1,2},{2,1},{3,0},{4,7},{5,6},{6,5},{7,4},{8,11},{9,10},{10,... | collective-permute-start | bytes 1572872 | tf_op jit(solution)/shard_map/ppermute | solution.py:424
  264.9 1.2 copy-start.5
  282.4 33.5 %all-to-all-start.4 = ((bf16[128,48,128]{2,1,0:T(8,128)(2,1)}), bf16[128,48,128]{2,1,0:T(8,128)(2,1)S(1)}, u32[]{:S(2)}, u32[]{:S(2)}) async-start(bf16[128,48,128]{2,1,0:T(8,128)(2,1)} %bitcast.37), calls=%async_computation.4 | async-start | bytes 3145728 | tf_op jit(solution)/shard_map/all_to_all | solution.py:428
  290.7 25.2 %copy-start = (s32[1,2048]{1,0:T(1,128)S(1)}, s32[1,2048]{1,0:T(1,128)}, u32[]{:S(2)}) copy-start(s32[1,2048]{1,0:T(1,128)} %get-tuple-element.29.lane_ref) | copy-start | bytes 24580
  290.7 25.2 %copy-start.1 = (s32[1,2048]{1,0:T(1,128)S(1)}, s32[1,2048]{1,0:T(1,128)}, u32[]{:S(2)}) copy-start(s32[1,2048]{1,0:T(1,128)} %get-tuple-element.30.spot_ref) | copy-start | bytes 24580
  315.9 1.2 copy-start.2

commit v3 on v2

--- a/solution.py
+++ b/solution.py
@@ -100,7 +100,7 @@
     out = jax.ShapeDtypeStruct((3 * width + LANES, width), BF16)
     return pl.pallas_call(
         split_kernel,
-        in_specs=[SMEM] + [HBM] * 4,
+        in_specs=[SMEM] + [VMEM] * 4,
         out_specs=[HBM, HBM],
         out_shape=[out, out],
         scratch_shapes=[pltpu.SemaphoreType.DMA((8,))],
@@ -221,7 +221,8 @@
     )(near, far, q, kv, halo, spot_row, lane_row, *after)
 
 
-def place_kernel(spot_ref, x_ref, out_ref):
+def place_kernel(spot_ref, x_ref, *rest):
+    out_ref = rest[-1]
     dests, cap = out_ref.shape[0], out_ref.shape[1]
     step = 4
 
@@ -236,17 +237,17 @@
             out_ref[i * step + d] = placed[d * cap : (d + 1) * cap, :]
 
 
-def place_rows(spot_row, x, parts, cap):
+def place_rows(spot_row, x, after, parts, cap):
     rows, width = x.shape
     return pl.pallas_call(
         place_kernel,
-        in_specs=[VMEM, VMEM],
+        in_specs=[VMEM, VMEM] + [ANY] * len(after),
         out_specs=VMEM,
         out_shape=jax.ShapeDtypeStruct((parts, cap, width), BF16),
         compiler_params=params(60),
         cost_estimate=cost(2 * parts * cap * rows * width, 4 * 2**20),
         name="place_rows",
-    )(spot_row, x)
+    )(spot_row, x, *after)
 
 
 def experts_kernel(me_ref, gain_ref, route_ref, h_ref, x_ref, w0_ref, w1_ref, w2_ref, w3_ref, *rest):
@@ -335,26 +336,32 @@
 
 
 def columns_kernel(
-    me_ref, h0_ref, h1_ref, h2_ref, h3_ref, w0_ref, w1_ref, w2_ref, w3_ref, x_ref, attn_ref, mixed_ref
+    me_ref, h0_ref, h1_ref, h3_ref, top_ref, bottom_ref, w0_ref, w1_ref, w2_ref, w3_ref, x_ref, attn_ref, mixed_ref
 ):
     columns = pl.ds(pl.multiple_of(me_ref[0] * LANES, LANES), LANES)
-    total = None
-    for h, w in zip((h0_ref, h1_ref, h2_ref, h3_ref), (w0_ref, w1_ref, w2_ref, w3_ref)):
-        term = jnp.dot(h[...], w[:, columns], preferred_element_type=F32)
-        total = term if total is None else total + term
-    attn_ref[...] = total.astype(BF16)
-    mixed_ref[...] = x_ref[:, columns].astype(F32) + total
-
-
-def attention_columns(me, heads, weights, x):
+    half = top_ref.shape[0]
+    for start, h2_ref in ((0, top_ref), (half, bottom_ref)):
+        rows = slice(start, start + half)
+        pieces = [h0_ref[rows, :], h1_ref[rows, :], h2_ref[...], h3_ref[rows, :]]
+        weights = [w[:, columns] for w in (w0_ref, w1_ref, w2_ref, w3_ref)]
+        total = jnp.dot(
+            jnp.concatenate(pieces, axis=1), jnp.concatenate(weights, axis=0), preferred_element_type=F32
+        )
+        attn_ref[rows, :] = total.astype(BF16)
+        mixed_ref[rows, :] = x_ref[rows, columns].astype(F32) + total
+
+
+def attention_columns(me, heads, by_one, by_three, relayed, weights, x):
     rows, width = x.shape
     last = weights[0].shape[0] // LANES - 1
     out = pl.BlockSpec((rows, LANES), lambda i: (0, 0))
+    half = pl.BlockSpec((rows // 2, LANES), lambda i: (0, 0))
     return pl.pallas_call(
         columns_kernel,
         grid=(1,),
         in_specs=[SMEM]
-        + [out] * 4
+        + [out] * 3
+        + [half] * 2
         + [pl.BlockSpec((LANES, width), lambda i: (last, 0))] * 4
         + [pl.BlockSpec((rows, width), lambda i: (0, 0))],
         out_specs=[out, out],
@@ -365,10 +372,10 @@
         compiler_params=params(60),
         cost_estimate=cost(2 * rows * width * LANES, 8 * 2**20),
         name="attention_columns",
-    )(me, *heads, *weights, x)
-
-
-def combine_kernel(spot_ref, lane_ref, mixed_ref, back_ref, out_ref, slots, sems):
+    )(me, heads, by_one, by_three, *relayed, *weights, x)
+
+
+def combine_kernel(spot_ref, lane_ref, mixed_hbm, back_ref, out_ref, slots, mixed_ref, sems):
     dests, cap, width = slots.shape
     rows = out_ref.shape[0]
     copies = [
@@ -377,6 +384,7 @@
         )
         for m in range(4)
     ]
+    copies.append(pltpu.make_async_copy(mixed_hbm, mixed_ref, sems.at[4]))
     for copy in copies:
         copy.start()
     for copy in copies:
@@ -407,12 +415,13 @@
     slots = back.shape[0] * back.shape[2]
     return pl.pallas_call(
         combine_kernel,
-        in_specs=[VMEM] * 3 + [HBM],
+        in_specs=[VMEM] * 2 + [HBM] * 2,
         out_specs=VMEM,
         out_shape=jax.ShapeDtypeStruct((rows, LANES), BF16),
         scratch_shapes=[
             pltpu.VMEM((back.shape[0], back.shape[2], 4 * LANES), BF16),
-            pltpu.SemaphoreType.DMA((4,)),
+            pltpu.VMEM((rows, LANES), F32),
+            pltpu.SemaphoreType.DMA((5,)),
         ],
         compiler_params=params(24),
         cost_estimate=cost(2 * rows * slots * 4 * LANES, 4 * 2**20),
@@ -482,7 +491,7 @@
     spot = (routed // 2) * half_cap + rank - second * half_cap
     spot_row, lane_row = spot[None, :], lane[None, :]
     mine_row = jnp.where(lane == me, spot, -1)[None, :]
-    x_there = exchange(place_rows(mine_row, node_features, parts, half_cap), "graph")
+    x_there = exchange(place_rows(mine_row, node_features, (near_slots, far_slots), parts, half_cap), "graph")
 
     route = lax.dynamic_index_in_dim(router, 2 * part + which, 1, keepdims=False).astype(F32)[None, :]
     heads, send = attention(
@@ -490,8 +499,12 @@
     )
     send, x_there, weights[2:] = lax.optimization_barrier((send, x_there, weights[2:]))
     heads_there = exchange(send.reshape(parts * 4, half_cap, LANES), ("graph", "mp"))
-    all_heads = [heads] + [swap(heads, k) for k in (1, 2, 3)]
-    attn_out, mixed = attention_columns(me_ref, all_heads, weights, node_features)
+    by_one, by_three = swap(heads, 1), swap(heads, 3)
+    middle = rows // 2
+    relayed = [swap(by_three[:middle], 1), swap(by_one[middle:], 3)]
+    attn_out, mixed = attention_columns(
+        me_ref, heads, by_one, by_three, relayed, weights, node_features
+    )
 
     produced = experts(
         me_ref,
@@ -500,7 +513,7 @@
         norm_gain[None, :],
         route,
         weights,
-        all_heads[1:],
+        (by_one, by_three),
     )
     back = exchange(produced.reshape(parts * 4, half_cap, LANES), ("graph", "mp"))
     layer_out = combine(spot_row, lane_row, back.reshape(parts, 4, half_cap, LANES), mixed)

time: 324 us -> 217 us (0.67)
  Pallas kernels: 167 us -> 66.5 us
  waiting for transfers between devices: 95.6 us -> 83.7 us
    pallas_call x4, Pallas kernels: 122 us -> 21.6 us  [the longest x1 7.4 us: place_rows(): pl.pallas_call(place_kernel, in_specs=[VMEM, VMEM] + [ANY] * len(after),...]
    all_to_all x5, waiting for transfers between devices: 58.4 us -> 37.4 us  [exchange(): return lax.all_to_all(array, axes, split_axis=0, concat_axis=0, tiled=True)]
    ppermute x6 -> x7, waiting for transfers between devices: 37.2 us -> 46.2 us  [swap(): return lax.ppermute(array, 'mp', [(i, i ^ change) for i in range(4)])]
    ppermute x6 -> x7, starting transfers between devices: 7.89 us -> 10.5 us  [swap(): return lax.ppermute(array, 'mp', [(i, i ^ change) for i in range(4)])]
  transfers between devices with their start and end apart: 11 -> 12, of which waited for: 5 -> 6; matrix products, arithmetic and copies ran while one was open for 2% -> 3% of each run, Pallas kernels for 44% -> 19%
where the time goes in v3:
time: 217 us; the launch traced here: 216 us
  waiting for transfers between devices  83.7 us (39%)
  Pallas kernels  66.5 us (31%)
  starting transfers between devices  51.6 us (24%)
  local copies, waits for them, and re-layouts  7.38 us (3%)
  other arithmetic  4.43 us (2%)
    ppermute x7, waiting for transfers between devices, swap(): return lax.ppermute(array, 'mp', [(i, i ^ change) for i in range(4)])  46.2 us
    all_to_all x5, starting transfers between devices, exchange(): return lax.all_to_all(array, axes, split_axis=0, concat_axis=0, tiled=True)  41.1 us
    all_to_all x5, waiting for transfers between devices, exchange(): return lax.all_to_all(array, axes, split_axis=0, concat_axis=0, tiled=True)  37.4 us
    pallas_call x1, Pallas kernels, attention(): pl.pallas_call(attention_kernel, in_specs=[SMEM, SMEM, VMEM, VMEM, VMEM,...  19.6 us
    pallas_call x1, Pallas kernels, experts(): pl.pallas_call(experts_kernel, in_specs=[SMEM, VMEM, VMEM, HBM, HBM] + [A...  16.3 us
    ppermute x7, starting transfers between devices, swap(): return lax.ppermute(array, 'mp', [(i, i ^ change) for i in range(4)])  10.5 us
    pallas_call x1, Pallas kernels, place_rows(): pl.pallas_call(place_kernel, in_specs=[VMEM, VMEM] + [ANY] * len(after),...  7.4 us
    pallas_call x1, Pallas kernels, combine(): pl.pallas_call(combine_kernel, in_specs=[VMEM] * 2 + [HBM] * 2, out_specs...  6.2 us
  transfers between devices with their start and end apart: 12, of which 6 were waited for; matrix products, arithmetic and copies ran while one was open for 3% of the time, Pallas kernels for 19%

profile of v3, /device:TPU:1, one launch (start us, length us, event | category | flops | bytes accessed | tf_op | source)
XLA Modules:
  0.0 216.2 jit_solution(8367510222873028942)
XLA Ops:
  0.7 0.8 slice.13
  1.4 0.1 eq.59
  1.5 0.7 compare_reduce_fusion
  2.2 0.1 select_reduce_fusion.2
  2.4 0.7 copy.20
  3.1 9.6 %all-to-all-start = ((s32[32,1,2]{2,1,0:T(1,128)}), s32[32,1,2]{2,1,0:T(1,128)S(1)}, u32[]{:S(2)}, u32[]{:S(2)}) async-start(s32[32,1,2]{2,1,0:T(1,128)} %copy.20), calls=%async_computation | async-start | bytes 32768 | tf_op jit(solution)/shard_map/all_to_all | solution.py:437
  12.7 3.8 %split_weights.1 = (bf16[1664,512]{1,0:T(8,128)(2,1)}, bf16[1664,512]{1,0:T(8,128)(2,1)}) custom-call(s32[1]{0:T(128)} %bitcast.me_ref, bf16[2,512,512]{2,1,0:T(8,128)(2,1)} %gate_ref.1, bf16[2,512,512]{2,1,0:T(8,128)(2,1)} %up_ref.1, bf16[2,512,512]{2,1,0:T(8,128)(2,1)} %down_ref.1, bf16[128,512]{1,0:T(8,128)(2,1)} %out_w_ref.1), custom_call_target="tpu_custom_call" | custom-call | bytes 6815744 | tf_op jit(solution)/shard_map/split_weights/pallas_call | solution.py:101
  16.5 5.1 %qkv.1 = (bf16[2048,128]{1,0:T(8,128)(2,1)}, bf16[16,128,256]{2,1,0:T(8,128)(2,1)}) custom-call(bf16[2048,512]{1,0:T(8,128)(2,1)} %x_ref.5, bf16[3,512,128]{2,1,0:T(8,128)(2,1)} %w_ref.1, f32[2]{0:T(128)} %scale_ref.1, bf16[1664,512]{1,0:T(8,128)(2,1)} %get-tuple-element.14._.w0_ref), custom_call_target="tpu_custom_call" | custom-call | flops 805306368 | bytes 3670016 | tf_op jit(solution)/shard_map/qkv/pallas_call | solution.py:60
  21.6 0.0 all-to-all-done.wanted_ref
  21.6 0.0 copy-start.8
  21.6 0.6 copy-done.8
  22.2 3.8 %pick_blocks.1 = bf16[64,128,256]{2,1,0:T(8,128)(2,1)} custom-call(s32[32,1,2]{2,1,0:T(1,128)} %copy-done.8, bf16[16,128,256]{2,1,0:T(8,128)(2,1)} %get-tuple-element.16.kv_ref), custom_call_target="tpu_custom_call" | custom-call | bytes 8388608 | tf_op jit(solution)/shard_map/pick_blocks/pallas_call | solution.py:130
  26.0 0.0 copy-start.3
  26.0 0.0 copy-start.10
  26.0 7.6 %all-to-all-start.1 = ((bf16[64,128,256]{2,1,0:T(8,128)(2,1)}), bf16[64,128,256]{2,1,0:T(8,128)(2,1)}, u32[]{:S(2)}, u32[]{:S(2)}) async-start(bf16[64,128,256]{2,1,0:T(8,128)(2,1)} %pick_blocks.1), calls=%async_computation.1 | async-start | bytes 8388608 | tf_op jit(solution)/shard_map/all_to_all | solution.py:437
  33.6 0.0 copy-done.3
  33.6 1.3 collective-permute-start
  34.9 2.5 %collective-permute-start.5 = (bf16[1664,512]{1,0:T(8,128)(2,1)}, bf16[1664,512]{1,0:T(8,128)(2,1)}, u32[]{:S(2)}, u32[]{:S(2)}) collective-permute-start(bf16[1664,512]{1,0:T(8,128)(2,1)} %get-tuple-element.19), channel_id=1, source_target_pairs={{0,2},{1,3},{2,0},{3,1},{4,6},{5,7},{6,4},{7,5},{8,10},{9,11},{10,... | collective-permute-start | bytes 5111816 | tf_op jit(solution)/shard_map/ppermute | solution.py:433
  37.4 0.2 collective-permute-start.6
  37.6 0.0 copy-done.10
  37.6 0.0 copy-start.9
  37.6 1.7 fusion.2
  39.2 0.1 copy.19
  39.3 0.1 add.88
  39.4 1.0 select_reduce_fusion.far_ref.rest_1_
  40.4 0.0 copy-done.9
  40.4 0.6 slice_subtract_fusion.near_ref.rest_0_
  41.0 0.7 compare_select_fusion
  41.7 7.4 %place_rows.1 = bf16[32,48,512]{2,1,0:T(8,128)(2,1)} custom-call(s32[1,2048]{1,0:T(1,128)} %get-tuple-element.28.spot_ref, bf16[2048,512]{1,0:T(8,128)(2,1)} %x_ref.5, s32[16,4]{1,0:T(8,128)} %slice_subtract_fusion.near_ref.rest_0_, s32[16,8]{1,0:T(8,128)} %select_reduce_fusion.far_ref.rest_1_), custom_call_target="tpu_custom_call" | custom-call | flops 3221225472 | bytes 4194304 | tf_op jit(solution)/shard_map/place_rows/pallas_call | solution.py:242
  49.1 34.7 %all-to-all-done.1.halo_ref = bf16[64,128,256]{2,1,0:T(8,128)(2,1)} async-done(((bf16[64,128,256]{2,1,0:T(8,128)(2,1)}), bf16[64,128,256]{2,1,0:T(8,128)(2,1)}, u32[]{:S(2)}, u32[]{:S(2)}) %all-to-all-start.1) | async-done | bytes 4194336 | tf_op jit(solution)/shard_map/all_to_all | solution.py:437
  83.9 7.1 %all-to-all-start.2 = ((bf16[32,48,512]{2,1,0:T(8,128)(2,1)}), bf16[32,48,512]{2,1,0:T(8,128)(2,1)S(1)}, u32[]{:S(2)}, u32[]{:S(2)}) async-start(bf16[32,48,512]{2,1,0:T(8,128)(2,1)} %place_rows.1), calls=%async_computation.2 | async-start | bytes 3145728 | tf_op jit(solution)/shard_map/all_to_all | solution.py:437
  91.0 0.0 collective-permute-done.rest_0_.w1_ref
  91.0 19.6 %attention.1 = (bf16[2048,128]{1,0:T(8,128)(2,1)}, bf16[32,4,48,128]{3,2,1,0:T(8,128)(2,1)}) custom-call(s32[16,4]{1,0:T(8,128)} %slice_subtract_fusion.near_ref.rest_0_, s32[16,8]{1,0:T(8,128)} %select_reduce_fusion.far_ref.rest_1_, bf16[2048,128]{1,0:T(8,128)(2,1)} %get-tuple-element.15.q_ref, bf16[16,128,256]{2,1,0:T(8,128)(2,1)} %get-tuple-element.16.kv_ref, ...), custom_call_target="tpu_custom_call" | custom-call | flops 12000000000 | bytes 8388608 | tf_op jit(solution)/shard_map/attention/pallas_call | solution.py:205
  110.6 2.7 %all-to-all-done.2.x_ref = bf16[32,48,512]{2,1,0:T(8,128)(2,1)S(1)} async-done(((bf16[32,48,512]{2,1,0:T(8,128)(2,1)}), bf16[32,48,512]{2,1,0:T(8,128)(2,1)S(1)}, u32[]{:S(2)}, u32[]{:S(2)}) %all-to-all-start.2) | async-done | bytes 1572896 | tf_op jit(solution)/shard_map/all_to_all | solution.py:437
  113.3 0.0 collective-permute-done.5.w2_ref
  113.3 0.0 collective-permute-done.6.w3_ref
  113.3 8.2 %all-to-all-start.3 = ((bf16[128,48,128]{2,1,0:T(8,128)(2,1)}), bf16[128,48,128]{2,1,0:T(8,128)(2,1)S(1)}, u32[]{:S(2)}, u32[]{:S(2)}) async-start(bf16[128,48,128]{2,1,0:T(8,128)(2,1)} %bitcast.35), calls=%async_computation.3 | async-start | bytes 3145728 | tf_op jit(solution)/shard_map/all_to_all | solution.py:437
  121.5 1.5 collective-permute-start.1
  122.9 1.8 collective-permute-start.2
  124.7 1.3 bitcast_convert_fusion.route_ref
  126.0 25.1 %collective-permute-done.1.h1_ref.rest_0_ = bf16[2048,128]{1,0:T(8,128)(2,1)} collective-permute-done((bf16[2048,128]{1,0:T(8,128)(2,1)}, bf16[2048,128]{1,0:T(8,128)(2,1)}, u32[]{:S(2)}, u32[]{:S(2)}) %collective-permute-start.1) | collective-permute-done | bytes 524320 | tf_op jit(solution)/shard_map/ppermute | solution.py:433
  151.2 1.2 collective-permute-done.2.h3_ref.rest_1_
  152.4 0.0 all-to-all-done.3
  152.4 0.0 copy-done.4
  152.4 1.1 copy-done.5
  153.5 16.3 %experts.1 = bf16[32,4,48,128]{3,2,1,0:T(8,128)(2,1)} custom-call(s32[1]{0:T(128)} %bitcast.me_ref, f32[1,512]{1,0:T(1,128)} %bitcast.42, f32[1,512]{1,0:T(1,128)} %bitcast_convert_fusion.route_ref, bf16[32,4,48,128]{3,2,1,0:T(8,128)(2,1)} %bitcast.36, bf16[32,48,512]{2,1,0:T(8,128)(2,1)} %copy-done.4, bf16[1664,512]{1,0:T(8,128)(2,1)} %get-tuple-element.14._.w0_ref, ...), custom_call_target="tpu_custom_call" | custom-call | flops 10468982784 | bytes 12582912 | tf_op jit(solution)/shard_map/experts/pallas_call | solution.py:319
  169.9 8.6 %all-to-all-start.4 = ((bf16[128,48,128]{2,1,0:T(8,128)(2,1)}), bf16[128,48,128]{2,1,0:T(8,128)(2,1)S(1)}, u32[]{:S(2)}, u32[]{:S(2)}) async-start(bf16[128,48,128]{2,1,0:T(8,128)(2,1)} %bitcast.37), calls=%async_computation.4 | async-start | bytes 3145728 | tf_op jit(solution)/shard_map/all_to_all | solution.py:437
  178.5 1.0 slice.16
  179.5 1.5 collective-permute-start.3
  180.9 1.0 slice.17
  181.9 0.0 copy-start
  181.9 0.0 copy-start.1
  181.9 1.9 collective-permute-start.4
  183.8 18.7 %collective-permute-done.3.top_ref = bf16[1024,128]{1,0:T(8,128)(2,1)S(1)} collective-permute-done((bf16[1024,128]{1,0:T(8,128)(2,1)S(1)}, bf16[1024,128]{1,0:T(8,128)(2,1)S(1)}, u32[]{:S(2)}, u32[]{:S(2)}) %collective-permute-start.3) | collective-permute-done | bytes 262176 | tf_op jit(solution)/shard_map/ppermute | solution.py:433
  202.4 1.2 collective-permute-done.4.bottom_ref
  203.7 0.0 copy-done.6
  203.7 0.7 copy-done.7
  204.4 4.3 %attention_columns.1 = (bf16[2048,128]{1,0:T(8,128)(2,1)}, f32[2048,128]{1,0:T(8,128)}) custom-call(s32[1]{0:T(128)} %bitcast.me_ref, bf16[2048,128]{1,0:T(8,128)(2,1)} %get-tuple-element.17.h0_ref, bf16[2048,128]{1,0:T(8,128)(2,1)} %collective-permute-done.1.h1_ref.rest_0_, bf16[2048,128]{1,0:T(8,128)(2,1)} %collective-permute-done.2.h3_ref.rest_1_, ...), custom_call_target="tpu_custom_call" | custom-call | flops 268435456 | bytes 8388608 | tf_op jit(solution)/shard_map/attention_columns/pallas_call | solution.py:359
  208.6 0.0 all-to-all-done.4
  208.6 0.0 copy-done
  208.6 0.0 copy-done.1
  208.6 0.0 copy-start.2
  208.7 1.2 copy-done.2
  209.9 6.2 %combine.1 = bf16[2048,128]{1,0:T(8,128)(2,1)} custom-call(s32[1,2048]{1,0:T(1,128)S(1)} %copy-done.1, s32[1,2048]{1,0:T(1,128)S(1)} %copy-done, f32[2048,128]{1,0:T(8,128)S(1)} %copy-done.2, bf16[32,4,48,128]{3,2,1,0:T(8,128)(2,1)S(1)} %bitcast.34), custom_call_target="tpu_custom_call" | custom-call | flops 3221225472 | bytes 4194304 | tf_op jit(solution)/shard_map/combine/pallas_call | solution.py:416
  (8 shorter events, 0.0 us)
Async XLA Ops:
  3.1 18.5 %all-to-all-start = ((s32[32,1,2]{2,1,0:T(1,128)}), s32[32,1,2]{2,1,0:T(1,128)S(1)}, u32[]{:S(2)}, u32[]{:S(2)}) async-start(s32[32,1,2]{2,1,0:T(1,128)} %copy.20), calls=%async_computation | async-start | bytes 32768 | tf_op jit(solution)/shard_map/all_to_all | solution.py:437
  21.6 0.6 copy-start.8
  26.0 7.6 %copy-start.3 = (bf16[1664,512]{1,0:T(8,128)(2,1)S(1)}, bf16[1664,512]{1,0:T(8,128)(2,1)}, u32[]{:S(2)}) copy-start(bf16[1664,512]{1,0:T(8,128)(2,1)} %get-tuple-element.14._.w0_ref) | copy-start | bytes 5111812
  26.0 11.6 %copy-start.10 = (s32[2048,1]{0,1:T(1,128)S(1)}, s32[2048,1]{0,1:T(1,128)}, u32[]{:S(2)}) copy-start(s32[2048,1]{0,1:T(1,128)} %param.21) | copy-start | bytes 24580
  26.0 57.9 %all-to-all-start.1 = ((bf16[64,128,256]{2,1,0:T(8,128)(2,1)}), bf16[64,128,256]{2,1,0:T(8,128)(2,1)}, u32[]{:S(2)}, u32[]{:S(2)}) async-start(bf16[64,128,256]{2,1,0:T(8,128)(2,1)} %pick_blocks.1), calls=%async_computation.1 | async-start | bytes 8388608 | tf_op jit(solution)/shard_map/all_to_all | solution.py:437
  33.6 57.4 %collective-permute-start = (bf16[1664,512]{1,0:T(8,128)(2,1)S(1)}, bf16[1664,512]{1,0:T(8,128)(2,1)}, u32[]{:S(2)}, u32[]{:S(2)}) collective-permute-start(bf16[1664,512]{1,0:T(8,128)(2,1)S(1)} %copy-done.3), channel_id=1, source_target_pairs={{0,1},{1,0},{2,3},{3,2},{4,5},{5,4},{6,7},{7,6},{8,9},{9,8},{10,11... | collective-permute-start | bytes 5111816 | tf_op jit(solution)/shard_map/ppermute | solution.py:433
  34.9 78.4 %collective-permute-start.5 = (bf16[1664,512]{1,0:T(8,128)(2,1)}, bf16[1664,512]{1,0:T(8,128)(2,1)}, u32[]{:S(2)}, u32[]{:S(2)}) collective-permute-start(bf16[1664,512]{1,0:T(8,128)(2,1)} %get-tuple-element.19), channel_id=1, source_target_pairs={{0,2},{1,3},{2,0},{3,1},{4,6},{5,7},{6,4},{7,5},{8,10},{9,11},{10,... | collective-permute-start | bytes 5111816 | tf_op jit(solution)/shard_map/ppermute | solution.py:433
  37.4 75.9 %collective-permute-start.6 = (bf16[1664,512]{1,0:T(8,128)(2,1)}, bf16[1664,512]{1,0:T(8,128)(2,1)}, u32[]{:S(2)}, u32[]{:S(2)}) collective-permute-start(bf16[1664,512]{1,0:T(8,128)(2,1)} %get-tuple-element.19), channel_id=1, source_target_pairs={{0,3},{1,2},{2,1},{3,0},{4,7},{5,6},{6,5},{7,4},{8,11},{9,10},{10,... | collective-permute-start | bytes 5111816 | tf_op jit(solution)/shard_map/ppermute | solution.py:433
  37.6 2.9 %copy-start.9 = (s32[16,12]{1,0:T(8,128)S(1)}, s32[16,12]{1,0:T(8,128)}, u32[]{:S(2)}) copy-start(s32[16,12]{1,0:T(8,128)} %param.20) | copy-start | bytes 2308
  83.9 29.4 %all-to-all-start.2 = ((bf16[32,48,512]{2,1,0:T(8,128)(2,1)}), bf16[32,48,512]{2,1,0:T(8,128)(2,1)S(1)}, u32[]{:S(2)}, u32[]{:S(2)}) async-start(bf16[32,48,512]{2,1,0:T(8,128)(2,1)} %place_rows.1), calls=%async_computation.2 | async-start | bytes 3145728 | tf_op jit(solution)/shard_map/all_to_all | solution.py:437
  113.3 39.1 %copy-start.4 = (bf16[32,48,512]{2,1,0:T(8,128)(2,1)}, bf16[32,48,512]{2,1,0:T(8,128)(2,1)S(1)}, u32[]{:S(2)}) copy-start(bf16[32,48,512]{2,1,0:T(8,128)(2,1)S(1)} %all-to-all-done.2.x_ref) | copy-start | bytes 4718596
  113.3 39.1 %all-to-all-start.3 = ((bf16[128,48,128]{2,1,0:T(8,128)(2,1)}), bf16[128,48,128]{2,1,0:T(8,128)(2,1)S(1)}, u32[]{:S(2)}, u32[]{:S(2)}) async-start(bf16[128,48,128]{2,1,0:T(8,128)(2,1)} %bitcast.35), calls=%async_computation.3 | async-start | bytes 3145728 | tf_op jit(solution)/shard_map/all_to_all | solution.py:437
  121.5 29.7 %collective-permute-start.1 = (bf16[2048,128]{1,0:T(8,128)(2,1)}, bf16[2048,128]{1,0:T(8,128)(2,1)}, u32[]{:S(2)}, u32[]{:S(2)}) collective-permute-start(bf16[2048,128]{1,0:T(8,128)(2,1)} %get-tuple-element.17.h0_ref), channel_id=1, source_target_pairs={{0,1},{1,0},{2,3},{3,2},{4,5},{5,4},{6,7},{7,6},{8,9},{9,8},{10,11... | collective-permute-start | bytes 1572872 | tf_op jit(solution)/shard_map/ppermute | solution.py:433
  122.9 29.4 %collective-permute-start.2 = (bf16[2048,128]{1,0:T(8,128)(2,1)}, bf16[2048,128]{1,0:T(8,128)(2,1)}, u32[]{:S(2)}, u32[]{:S(2)}) collective-permute-start(bf16[2048,128]{1,0:T(8,128)(2,1)} %get-tuple-element.17.h0_ref), channel_id=1, source_target_pairs={{0,3},{1,2},{2,1},{3,0},{4,7},{5,6},{6,5},{7,4},{8,11},{9,10},{10,... | collective-permute-start | bytes 1572872 | tf_op jit(solution)/shard_map/ppermute | solution.py:433
  152.4 1.2 copy-start.5
  169.9 38.7 %all-to-all-start.4 = ((bf16[128,48,128]{2,1,0:T(8,128)(2,1)}), bf16[128,48,128]{2,1,0:T(8,128)(2,1)S(1)}, u32[]{:S(2)}, u32[]{:S(2)}) async-start(bf16[128,48,128]{2,1,0:T(8,128)(2,1)} %bitcast.37), calls=%async_computation.4 | async-start | bytes 3145728 | tf_op jit(solution)/shard_map/all_to_all | solution.py:437
  179.5 23.0 %collective-permute-start.3 = (bf16[1024,128]{1,0:T(8,128)(2,1)S(1)}, bf16[1024,128]{1,0:T(8,128)(2,1)S(1)}, u32[]{:S(2)}, u32[]{:S(2)}) collective-permute-start(bf16[1024,128]{1,0:T(8,128)(2,1)S(1)} %slice.16), channel_id=1, source_target_pairs={{0,1},{1,0},{2,3},{3,2},{4,5},{5,4},{6,7},{7,6},{8,9},{9,8},{10,11... | collective-permute-start | bytes 786440 | tf_op jit(solution)/shard_map/ppermute | solution.py:433
  181.9 26.7 %copy-start = (s32[1,2048]{1,0:T(1,128)S(1)}, s32[1,2048]{1,0:T(1,128)}, u32[]{:S(2)}) copy-start(s32[1,2048]{1,0:T(1,128)} %get-tuple-element.29.lane_ref) | copy-start | bytes 24580
  181.9 26.7 %copy-start.1 = (s32[1,2048]{1,0:T(1,128)S(1)}, s32[1,2048]{1,0:T(1,128)}, u32[]{:S(2)}) copy-start(s32[1,2048]{1,0:T(1,128)} %get-tuple-element.30.spot_ref) | copy-start | bytes 24580
  181.9 21.7 %collective-permute-start.4 = (bf16[1024,128]{1,0:T(8,128)(2,1)S(1)}, bf16[1024,128]{1,0:T(8,128)(2,1)S(1)}, u32[]{:S(2)}, u32[]{:S(2)}) collective-permute-start(bf16[1024,128]{1,0:T(8,128)(2,1)S(1)} %slice.17), channel_id=1, source_target_pairs={{0,3},{1,2},{2,1},{3,0},{4,7},{5,6},{6,5},{7,4},{8,11},{9,10},{10,... | collective-permute-start | bytes 786440 | tf_op jit(solution)/shard_map/ppermute | solution.py:433
  202.4 1.2 copy-start.6
  203.7 0.7 copy-start.7
  208.6 1.2 copy-start.2

commit v4 on v3

--- a/solution.py
+++ b/solution.py
@@ -40,7 +40,7 @@
     return values * scale
 
 
-def qkv_kernel(x_ref, w_ref, scale_ref, _, q_ref, kv_ref):
+def qkv_kernel(x_ref, w_ref, scale_ref, q_ref, kv_ref):
     x = x_ref[...]
     rows = x.shape[0]
     query = jnp.dot(x, w_ref[0], preferred_element_type=F32)
@@ -53,7 +53,7 @@
     kv_ref[:, :, LANES:] = value.astype(BF16).reshape(rows // ROWS_BLK, ROWS_BLK, LANES)
 
 
-def qkv(x, w, scale, after):
+def qkv(x, w, scale):
     rows, width = x.shape
     tile = 512
     blocks = tile // ROWS_BLK
@@ -64,7 +64,6 @@
             pl.BlockSpec((tile, width), lambda i: (i, 0)),
             pl.BlockSpec((3, width, LANES), lambda i: (0, 0, 0)),
             SMEM,
-            ANY,
         ],
         out_specs=[
             pl.BlockSpec((tile, LANES), lambda i: (i, 0)),
@@ -77,10 +76,37 @@
         compiler_params=params(60),
         cost_estimate=cost(2 * rows * width * 3 * LANES, 2 * rows * (width + 3 * LANES)),
         name="qkv",
-    )(x, w, scale, after)
-
-
-def split_kernel(me_ref, gate_ref, up_ref, down_ref, out_w_ref, kept_ref, given_ref, sems):
+    )(x, w, scale)
+
+
+def requests_kernel(near_ref, out_ref):
+    parts = out_ref.shape[0]
+    rows, listed = near_ref.shape
+    shape = (parts, rows)
+    inside = lax.broadcasted_iota(jnp.int32, shape, 1)
+    names = lax.broadcasted_iota(jnp.int32, shape, 0) * rows + inside
+    wanted = jnp.zeros(shape, jnp.int32)
+    for i in range(rows):
+        for j in range(LOCAL_REFS, listed):
+            wanted = jnp.where(names == near_ref[i, j], 1, wanted)
+    first = jnp.min(jnp.where(wanted == 1, inside, rows - 1), axis=1, keepdims=True)
+    last = jnp.max(jnp.where(wanted == 1, inside, 0), axis=1, keepdims=True)
+    lane = lax.broadcasted_iota(jnp.int32, (parts, CAP_H), 1)
+    out_ref[...] = jnp.where(lane == 0, first, last)
+
+
+def make_requests(neighbor_blocks, parts):
+    return pl.pallas_call(
+        requests_kernel,
+        in_specs=[SMEM],
+        out_specs=VMEM,
+        out_shape=jax.ShapeDtypeStruct((parts, CAP_H), jnp.int32),
+        compiler_params=params(60),
+        name="make_requests",
+    )(neighbor_blocks)
+
+
+def split_kernel(me_ref, gate_ref, up_ref, down_ref, out_w_ref, _, kept_ref, given_ref, sems):
     which = me_ref[0] // 2
     width = gate_ref.shape[1]
     copies = []
@@ -95,19 +121,19 @@
         copy.wait()
 
 
-def split_weights(me, gate, up, down, out_w):
+def split_weights(me, gate, up, down, out_w, after):
     width = gate.shape[1]
     out = jax.ShapeDtypeStruct((3 * width + LANES, width), BF16)
     return pl.pallas_call(
         split_kernel,
-        in_specs=[SMEM] + [VMEM] * 4,
+        in_specs=[SMEM] + [VMEM] * 4 + [ANY],
         out_specs=[HBM, HBM],
         out_shape=[out, out],
         scratch_shapes=[pltpu.SemaphoreType.DMA((8,))],
         compiler_params=params(60),
         cost_estimate=cost(0, 4 * out.size * 2),
         name="split_weights",
-    )(me, gate, up, down, out_w)
+    )(me, gate, up, down, out_w, after)
 
 
 def pick_kernel(wanted_ref, kv_ref, out_ref, sems):
@@ -147,12 +173,12 @@
 
 
 def attention_kernel(
-    near_ref, far_ref, q_ref, kv_ref, halo_ref, spot_ref, lane_ref, *rest
+    near_ref, asked_ref, q_ref, kv_ref, halo_ref, spot_ref, lane_ref, *rest
 ):
     heads_ref, send_ref, keys, values, spread = rest[-5:]
     blocks = kv_ref.shape[0]
     together = keys.shape[0]
-    nears, fars = near_ref.shape[1], far_ref.shape[1]
+    listed = near_ref.shape[1]
     low = lax.broadcasted_iota(jnp.int32, (ROWS_BLK, LANES), 1) < HEAD_DIM
 
     @pl.loop(0, blocks // together)
@@ -163,11 +189,15 @@
         for t, (b, rows) in enumerate(zip(at, at_rows)):
             q = q_ref[rows, :].astype(F32)
             both = jnp.concatenate([jnp.where(low, q, 0.0), jnp.where(low, 0.0, q)], axis=0).astype(BF16)
-            for j in range(nears + fars):
-                if j < nears:
-                    block = kv_ref[near_ref[b, j]]
+            for j in range(listed):
+                name = near_ref[b, j]
+                owner = name // blocks
+                inside = name - owner * blocks
+                if j < LOCAL_REFS:
+                    block = kv_ref[inside]
                 else:
-                    block = halo_ref[far_ref[b, j - nears]]
+                    second = (inside != asked_ref[owner, 0]).astype(jnp.int32)
+                    block = halo_ref[owner * CAP_H + second]
                 keys[t, j * ROWS_BLK : (j + 1) * ROWS_BLK, :] = block[:, :LANES]
                 values[t, j * ROWS_BLK : (j + 1) * ROWS_BLK, :] = block[:, LANES:]
             scores.append(
@@ -199,9 +229,9 @@
                 send_ref[i * step + d, m] = placed[d * cap : (d + 1) * cap, m * LANES : (m + 1) * LANES]
 
 
-def attention(near, far, q, kv, halo, spot_row, lane_row, after, parts, cap, together=4):
+def attention(near, asked, q, kv, halo, spot_row, lane_row, after, parts, cap, together=4):
     rows = q.shape[0]
-    keys = (near.shape[1] + far.shape[1]) * ROWS_BLK
+    keys = near.shape[1] * ROWS_BLK
     return pl.pallas_call(
         attention_kernel,
         in_specs=[SMEM, SMEM, VMEM, VMEM, VMEM, VMEM, VMEM] + [ANY] * len(after),
@@ -218,11 +248,10 @@
         compiler_params=params(60),
         cost_estimate=cost(12 * 10**9, 8 * 2**20, 2 * rows * keys),
         name="attention",
-    )(near, far, q, kv, halo, spot_row, lane_row, *after)
-
-
-def place_kernel(spot_ref, x_ref, *rest):
-    out_ref = rest[-1]
+    )(near, asked, q, kv, halo, spot_row, lane_row, *after)
+
+
+def place_kernel(spot_ref, x_ref, out_ref):
     dests, cap = out_ref.shape[0], out_ref.shape[1]
     step = 4
 
@@ -237,17 +266,17 @@
             out_ref[i * step + d] = placed[d * cap : (d + 1) * cap, :]
 
 
-def place_rows(spot_row, x, after, parts, cap):
+def place_rows(spot_row, x, parts, cap):
     rows, width = x.shape
     return pl.pallas_call(
         place_kernel,
-        in_specs=[VMEM, VMEM] + [ANY] * len(after),
+        in_specs=[VMEM, VMEM],
         out_specs=VMEM,
         out_shape=jax.ShapeDtypeStruct((parts, cap, width), BF16),
         compiler_params=params(60),
         cost_estimate=cost(2 * parts * cap * rows * width, 4 * 2**20),
         name="place_rows",
-    )(spot_row, x, *after)
+    )(spot_row, x)
 
 
 def experts_kernel(me_ref, gain_ref, route_ref, h_ref, x_ref, w0_ref, w1_ref, w2_ref, w3_ref, *rest):
@@ -329,7 +358,7 @@
             pltpu.VMEM((tiles, step, 4, cap, LANES), BF16),
             pltpu.SemaphoreType.DMA((8 + 3 * tiles,)),
         ],
-        compiler_params=params(59),
+        compiler_params=params(58),
         cost_estimate=cost(2 * parts * cap * width * (12 * width + width), 12 * 2**20),
         name="experts",
     )(me, gain, route, heads, x, *weights, *after)
@@ -454,30 +483,18 @@
     part = lax.axis_index("graph")
     me = lax.axis_index("mp")
     rows, width = node_features.shape
-    blocks = rows // ROWS_BLK
     half_cap = CAP_E // 2
 
-    far = neighbor_blocks[:, LOCAL_REFS:]
-    names = jnp.arange(parts * blocks, dtype=jnp.int32).reshape(parts, blocks)
-    wanted = jnp.any(far.reshape(-1)[:, None, None] == names[None], axis=0)
-    inside = jnp.arange(blocks, dtype=jnp.int32)[None, :]
-    first = jnp.min(jnp.where(wanted, inside, blocks - 1), axis=1)
-    last = jnp.max(jnp.where(wanted, inside, 0), axis=1)
-    requests = jnp.stack([first, last], axis=1)
+    requests = make_requests(neighbor_blocks, parts)
     incoming = exchange(requests.reshape(parts, 1, CAP_H), "graph")
-    bases = jnp.arange(parts, dtype=jnp.int32)[:, None] * blocks
-    pool = (bases + requests).reshape(-1)
-    slots = jnp.arange(pool.shape[0], dtype=jnp.int32)
-    far_slots = jnp.max(jnp.where(far[:, :, None] == pool[None, None, :], slots[None, None, :], 0), axis=2)
-    near_slots = neighbor_blocks[:, :LOCAL_REFS] - part * blocks
+    q, kv = qkv(node_features, w_qkv, head_scale)
+    outgoing = pick_blocks(incoming, kv)
+    halo = exchange(outgoing, "graph")
 
     which = me // 2
     me_ref = me[None].astype(jnp.int32)
-    kept, given = split_weights(me_ref, w_gate, w_up, w_down, w_out)
+    kept, given = split_weights(me_ref, w_gate, w_up, w_down, w_out, outgoing)
     weights = [kept, swap(kept, 1), swap(given, 2), swap(given, 3)]
-
-    q, kv = qkv(node_features, w_qkv, head_scale, kept)
-    halo = exchange(pick_blocks(incoming, kv), "graph")
 
     routed = expert_ids[:, 0]
     experts_all = router.shape[1]
@@ -491,21 +508,16 @@
     spot = (routed // 2) * half_cap + rank - second * half_cap
     spot_row, lane_row = spot[None, :], lane[None, :]
     mine_row = jnp.where(lane == me, spot, -1)[None, :]
-    x_there = exchange(place_rows(mine_row, node_features, (near_slots, far_slots), parts, half_cap), "graph")
+    x_there = exchange(place_rows(mine_row, node_features, parts, half_cap), "graph")
 
     route = lax.dynamic_index_in_dim(router, 2 * part + which, 1, keepdims=False).astype(F32)[None, :]
     heads, send = attention(
-        near_slots, far_slots, q, kv, halo, spot_row, lane_row, weights[1:2], parts, half_cap
+        neighbor_blocks, requests, q, kv, halo, spot_row, lane_row, weights[1:2], parts, half_cap
     )
     send, x_there, weights[2:] = lax.optimization_barrier((send, x_there, weights[2:]))
     heads_there = exchange(send.reshape(parts * 4, half_cap, LANES), ("graph", "mp"))
+    heads, heads_there = lax.optimization_barrier((heads, heads_there))
     by_one, by_three = swap(heads, 1), swap(heads, 3)
-    middle = rows // 2
-    relayed = [swap(by_three[:middle], 1), swap(by_one[middle:], 3)]
-    attn_out, mixed = attention_columns(
-        me_ref, heads, by_one, by_three, relayed, weights, node_features
-    )
-
     produced = experts(
         me_ref,
         heads_there.reshape(parts, 4, half_cap, LANES),
@@ -513,7 +525,13 @@
         norm_gain[None, :],
         route,
         weights,
-        (by_one, by_three),
+        (),
+    )
+    produced, by_one, by_three = lax.optimization_barrier((produced, by_one, by_three))
+    middle = rows // 2
+    relayed = [swap(by_three[:middle], 1), swap(by_one[middle:], 3)]
+    attn_out, mixed = attention_columns(
+        me_ref, heads, by_one, by_three, relayed, weights, node_features
     )
     back = exchange(produced.reshape(parts * 4, half_cap, LANES), ("graph", "mp"))
     layer_out = combine(spot_row, lane_row, back.reshape(parts, 4, half_cap, LANES), mixed)

time: 217 us -> 209 us (0.963)
  starting transfers between devices: 51.6 us -> 43.9 us
  other arithmetic: 4.43 us -> 1.98 us
    all_to_all x5, waiting for transfers between devices: 37.4 us -> 59.8 us  [exchange(): return lax.all_to_all(array, axes, split_axis=0, concat_axis=0, tiled=True)]
    ppermute x7, waiting for transfers between devices: 46.2 us -> 25.9 us  [swap(): return lax.ppermute(array, 'mp', [(i, i ^ change) for i in range(4)])]
    all_to_all x5, starting transfers between devices: 41.1 us -> 35.9 us  [exchange(): return lax.all_to_all(array, axes, split_axis=0, concat_axis=0, tiled=True)]
    ppermute x7, starting transfers between devices: 10.5 us -> 7.94 us  [swap(): return lax.ppermute(array, 'mp', [(i, i ^ change) for i in range(4)])]
    pallas_call x2 -> x3, Pallas kernels: 11.2 us -> 12.8 us  [the longest x1 7.38 us: place_rows(): pl.pallas_call(place_kernel, in_specs=[VMEM, VMEM], out_specs=VMEM, out_s...]
  transfers between devices with their start and end apart: 12 -> 12, of which waited for: 6 -> 8; matrix products, arithmetic and copies ran while one was open for 3% -> 3% of each run, Pallas kernels for 19% -> 27%
where the time goes in v4:
time: 209 us
  waiting for transfers between devices  85.7 us (41%)
  Pallas kernels  68.3 us (33%)
  starting transfers between devices  43.9 us (21%)
  local copies, waits for them, and re-layouts  6.16 us (3%)
    all_to_all x5, waiting for transfers between devices, exchange(): return lax.all_to_all(array, axes, split_axis=0, concat_axis=0, tiled=True)  59.8 us
    all_to_all x5, starting transfers between devices, exchange(): return lax.all_to_all(array, axes, split_axis=0, concat_axis=0, tiled=True)  35.9 us
    ppermute x7, waiting for transfers between devices, swap(): return lax.ppermute(array, 'mp', [(i, i ^ change) for i in range(4)])  25.9 us
    pallas_call x1, Pallas kernels, attention(): pl.pallas_call(attention_kernel, in_specs=[SMEM, SMEM, VMEM, VMEM, VMEM,...  19.8 us
    pallas_call x1, Pallas kernels, experts(): pl.pallas_call(experts_kernel, in_specs=[SMEM, VMEM, VMEM, HBM, HBM] + [A...  16.3 us
    ppermute x7, starting transfers between devices, swap(): return lax.ppermute(array, 'mp', [(i, i ^ change) for i in range(4)])  7.94 us
    pallas_call x1, Pallas kernels, place_rows(): pl.pallas_call(place_kernel, in_specs=[VMEM, VMEM], out_specs=VMEM, out_s...  7.38 us
    pallas_call x1, Pallas kernels, combine(): pl.pallas_call(combine_kernel, in_specs=[VMEM] * 2 + [HBM] * 2, out_specs...  6.2 us
  transfers between devices with their start and end apart: 12, of which 8 were waited for; matrix products, arithmetic and copies ran while one was open for 3% of the time, Pallas kernels for 27%

profile of v4, /device:TPU:1, one launch (start us, length us, event | category | flops | bytes accessed | tf_op | source)
XLA Modules:
  0.0 208.6 jit_solution(2230872566135285744)
XLA Ops:
  0.6 1.7 make_requests.1.asked_ref
  2.4 9.6 %all-to-all-start = ((s32[32,1,2]{2,1,0:T(1,128)}), s32[32,1,2]{2,1,0:T(1,128)S(1)}, u32[]{:S(2)}, u32[]{:S(2)}) async-start(s32[32,1,2]{2,1,0:T(1,128)} %bitcast.37), calls=%async_computation | async-start | bytes 32768 | tf_op jit(solution)/shard_map/all_to_all | solution.py:466
  12.0 5.1 %qkv.1 = (bf16[2048,128]{1,0:T(8,128)(2,1)}, bf16[16,128,256]{2,1,0:T(8,128)(2,1)}) custom-call(bf16[2048,512]{1,0:T(8,128)(2,1)} %x_ref.5, bf16[3,512,128]{2,1,0:T(8,128)(2,1)} %w_ref.1, f32[2]{0:T(128)} %scale_ref.1), custom_call_target="tpu_custom_call" | custom-call | flops 805306368 | bytes 3670016 | tf_op jit(solution)/shard_map/qkv/pallas_call | solution.py:60
  17.1 1.7 all-to-all-done.wanted_ref
  18.8 0.0 copy-start.8
  18.8 0.6 copy-done.8
  19.4 3.8 %pick_blocks.1._ = bf16[64,128,256]{2,1,0:T(8,128)(2,1)} custom-call(s32[32,1,2]{2,1,0:T(1,128)} %copy-done.8, bf16[16,128,256]{2,1,0:T(8,128)(2,1)} %get-tuple-element.20.kv_ref), custom_call_target="tpu_custom_call" | custom-call | bytes 8388608 | tf_op jit(solution)/shard_map/pick_blocks/pallas_call | solution.py:156
  23.3 5.7 %all-to-all-start.1 = ((bf16[64,128,256]{2,1,0:T(8,128)(2,1)}), bf16[64,128,256]{2,1,0:T(8,128)(2,1)}, u32[]{:S(2)}, u32[]{:S(2)}) async-start(bf16[64,128,256]{2,1,0:T(8,128)(2,1)} %pick_blocks.1._), calls=%async_computation.1 | async-start | bytes 8388608 | tf_op jit(solution)/shard_map/all_to_all | solution.py:466
  29.0 0.0 copy-start.9
  29.0 3.6 %split_weights.1 = (bf16[1664,512]{1,0:T(8,128)(2,1)}, bf16[1664,512]{1,0:T(8,128)(2,1)}) custom-call(s32[1]{0:T(128)} %bitcast.me_ref, bf16[2,512,512]{2,1,0:T(8,128)(2,1)} %gate_ref.1, bf16[2,512,512]{2,1,0:T(8,128)(2,1)} %up_ref.1, bf16[2,512,512]{2,1,0:T(8,128)(2,1)} %down_ref.1, bf16[128,512]{1,0:T(8,128)(2,1)} %out_w_ref.1, ...), custom_call_target="tpu_custom_call" | custom-call | bytes 6815744 | tf_op jit(solution)/shard_map/split_weights/pallas_call | solution.py:127
  32.7 1.3 collective-permute-start
  34.0 0.0 copy-done.9
  34.0 1.7 fusion.2
  35.6 0.7 compare_select_fusion
  36.3 2.5 %collective-permute-start.1 = (bf16[1664,512]{1,0:T(8,128)(2,1)}, bf16[1664,512]{1,0:T(8,128)(2,1)}, u32[]{:S(2)}, u32[]{:S(2)}) collective-permute-start(bf16[1664,512]{1,0:T(8,128)(2,1)} %get-tuple-element.24), channel_id=1, source_target_pairs={{0,2},{1,3},{2,0},{3,1},{4,6},{5,7},{6,4},{7,5},{8,10},{9,11},{10,... | collective-permute-start | bytes 5111816 | tf_op jit(solution)/shard_map/ppermute | solution.py:462
  38.8 0.2 collective-permute-start.2
  39.0 7.4 %place_rows.1 = bf16[32,48,512]{2,1,0:T(8,128)(2,1)} custom-call(s32[1,2048]{1,0:T(1,128)} %get-tuple-element.36.spot_ref, bf16[2048,512]{1,0:T(8,128)(2,1)} %x_ref.5), custom_call_target="tpu_custom_call" | custom-call | flops 3221225472 | bytes 4194304 | tf_op jit(solution)/shard_map/place_rows/pallas_call | solution.py:271
  46.4 32.9 %all-to-all-done.1.halo_ref = bf16[64,128,256]{2,1,0:T(8,128)(2,1)} async-done(((bf16[64,128,256]{2,1,0:T(8,128)(2,1)}), bf16[64,128,256]{2,1,0:T(8,128)(2,1)}, u32[]{:S(2)}, u32[]{:S(2)}) %all-to-all-start.1) | async-done | bytes 4194336 | tf_op jit(solution)/shard_map/all_to_all | solution.py:466
  79.3 7.1 %all-to-all-start.2 = ((bf16[32,48,512]{2,1,0:T(8,128)(2,1)}), bf16[32,48,512]{2,1,0:T(8,128)(2,1)S(1)}, u32[]{:S(2)}, u32[]{:S(2)}) async-start(bf16[32,48,512]{2,1,0:T(8,128)(2,1)} %place_rows.1), calls=%async_computation.2 | async-start | bytes 3145728 | tf_op jit(solution)/shard_map/all_to_all | solution.py:466
  86.4 0.0 collective-permute-done.rest_0_.w1_ref
  86.4 0.0 copy-start.3
  86.4 1.2 copy-done.3
  87.6 19.8 %attention.1 = (bf16[2048,128]{1,0:T(8,128)(2,1)}, bf16[32,4,48,128]{3,2,1,0:T(8,128)(2,1)}) custom-call(s32[16,12]{1,0:T(8,128)} %near_ref.3, s32[32,2]{1,0:T(8,128)} %make_requests.1.asked_ref, bf16[2048,128]{1,0:T(8,128)(2,1)} %get-tuple-element.19.q_ref, bf16[16,128,256]{2,1,0:T(8,128)(2,1)} %get-tuple-element.20.kv_ref, ...), custom_call_target="tpu_custom_call" | custom-call | flops 12000000000 | bytes 8388608 | tf_op jit(solution)/shard_map/attention/pallas_call | solution.py:235
  107.4 1.2 all-to-all-done.2.x_ref
  108.7 0.0 copy-start.4
  108.7 1.6 collective-permute-done.1.w2_ref
  110.3 4.4 %collective-permute-done.2.w3_ref = bf16[1664,512]{1,0:T(8,128)(2,1)} collective-permute-done((bf16[1664,512]{1,0:T(8,128)(2,1)}, bf16[1664,512]{1,0:T(8,128)(2,1)}, u32[]{:S(2)}, u32[]{:S(2)}) %collective-permute-start.2) | collective-permute-done | bytes 1703968 | tf_op jit(solution)/shard_map/ppermute | solution.py:462
  114.7 8.2 %all-to-all-start.3 = ((bf16[128,48,128]{2,1,0:T(8,128)(2,1)}), bf16[128,48,128]{2,1,0:T(8,128)(2,1)S(1)}, u32[]{:S(2)}, u32[]{:S(2)}) async-start(bf16[128,48,128]{2,1,0:T(8,128)(2,1)} %bitcast.34), calls=%async_computation.3 | async-start | bytes 3145728 | tf_op jit(solution)/shard_map/all_to_all | solution.py:466
  122.9 1.3 bitcast_convert_fusion.route_ref
  124.2 23.9 %all-to-all-done.3 = bf16[128,48,128]{2,1,0:T(8,128)(2,1)S(1)} async-done(((bf16[128,48,128]{2,1,0:T(8,128)(2,1)}), bf16[128,48,128]{2,1,0:T(8,128)(2,1)S(1)}, u32[]{:S(2)}, u32[]{:S(2)}) %all-to-all-start.3) | async-done | bytes 1572896 | tf_op jit(solution)/shard_map/all_to_all | solution.py:466
  148.1 0.0 copy-start.5
  148.1 0.3 collective-permute-start.3
  148.4 0.4 collective-permute-start.4
  148.8 0.0 copy-done.4
  148.8 0.5 copy-done.5
  149.3 16.3 %experts.1 = bf16[32,4,48,128]{3,2,1,0:T(8,128)(2,1)} custom-call(s32[1]{0:T(128)} %bitcast.me_ref, f32[1,512]{1,0:T(1,128)} %bitcast.40, f32[1,512]{1,0:T(1,128)} %bitcast_convert_fusion.route_ref, bf16[32,4,48,128]{3,2,1,0:T(8,128)(2,1)} %bitcast.35, bf16[32,48,512]{2,1,0:T(8,128)(2,1)} %copy-done.4, bf16[1664,512]{1,0:T(8,128)(2,1)} %get-tuple-element.21.w0_ref, ...), custom_call_target="tpu_custom_call" | custom-call | flops 10468982784 | bytes 12582912 | tf_op jit(solution)/shard_map/experts/pallas_call | solution.py:348
  165.6 0.0 collective-permute-done.3.h1_ref
  165.6 0.0 collective-permute-done.4.h3_ref
  165.6 5.2 %all-to-all-start.4 = ((bf16[128,48,128]{2,1,0:T(8,128)(2,1)}), bf16[128,48,128]{2,1,0:T(8,128)(2,1)S(1)}, u32[]{:S(2)}, u32[]{:S(2)}) async-start(bf16[128,48,128]{2,1,0:T(8,128)(2,1)} %bitcast.36), calls=%async_computation.4 | async-start | bytes 3145728 | tf_op jit(solution)/shard_map/all_to_all | solution.py:466
  170.8 1.0 slice.6
  171.8 1.5 collective-permute-start.5
  173.3 1.0 slice.7
  174.2 0.0 copy-start
  174.2 0.0 copy-start.1
  174.3 1.9 collective-permute-start.6
  176.1 18.7 %collective-permute-done.5.top_ref = bf16[1024,128]{1,0:T(8,128)(2,1)S(1)} collective-permute-done((bf16[1024,128]{1,0:T(8,128)(2,1)S(1)}, bf16[1024,128]{1,0:T(8,128)(2,1)S(1)}, u32[]{:S(2)}, u32[]{:S(2)}) %collective-permute-start.5) | collective-permute-done | bytes 262176 | tf_op jit(solution)/shard_map/ppermute | solution.py:462
  194.8 0.0 copy-start.6
  194.8 1.2 collective-permute-done.6.bottom_ref
  196.0 0.0 copy-done.6
  196.0 0.0 copy-start.7
  196.0 0.7 copy-done.7
  196.7 4.3 %attention_columns.1 = (bf16[2048,128]{1,0:T(8,128)(2,1)}, f32[2048,128]{1,0:T(8,128)}) custom-call(s32[1]{0:T(128)} %bitcast.me_ref, bf16[2048,128]{1,0:T(8,128)(2,1)} %get-tuple-element.26.h0_ref, bf16[2048,128]{1,0:T(8,128)(2,1)} %collective-permute-done.3.h1_ref, bf16[2048,128]{1,0:T(8,128)(2,1)} %collective-permute-done.4.h3_ref, ...), custom_call_target="tpu_custom_call" | custom-call | flops 268435456 | bytes 8388608 | tf_op jit(solution)/shard_map/attention_columns/pallas_call | solution.py:388
  201.0 0.0 all-to-all-done.4
  201.0 0.0 copy-done
  201.0 0.0 copy-done.1
  201.0 0.0 copy-start.2
  201.0 1.2 copy-done.2
  202.2 6.2 %combine.1 = bf16[2048,128]{1,0:T(8,128)(2,1)} custom-call(s32[1,2048]{1,0:T(1,128)S(1)} %copy-done.1, s32[1,2048]{1,0:T(1,128)S(1)} %copy-done, f32[2048,128]{1,0:T(8,128)S(1)} %copy-done.2, bf16[32,4,48,128]{3,2,1,0:T(8,128)(2,1)S(1)} %bitcast.33), custom_call_target="tpu_custom_call" | custom-call | flops 3221225472 | bytes 4194304 | tf_op jit(solution)/shard_map/combine/pallas_call | solution.py:445
  (1 shorter events, 0.0 us)
Async XLA Ops:
  2.4 16.5 %all-to-all-start = ((s32[32,1,2]{2,1,0:T(1,128)}), s32[32,1,2]{2,1,0:T(1,128)S(1)}, u32[]{:S(2)}, u32[]{:S(2)}) async-start(s32[32,1,2]{2,1,0:T(1,128)} %bitcast.37), calls=%async_computation | async-start | bytes 32768 | tf_op jit(solution)/shard_map/all_to_all | solution.py:466
  18.8 0.6 copy-start.8
  23.3 56.0 %all-to-all-start.1 = ((bf16[64,128,256]{2,1,0:T(8,128)(2,1)}), bf16[64,128,256]{2,1,0:T(8,128)(2,1)}, u32[]{:S(2)}, u32[]{:S(2)}) async-start(bf16[64,128,256]{2,1,0:T(8,128)(2,1)} %pick_blocks.1._), calls=%async_computation.1 | async-start | bytes 8388608 | tf_op jit(solution)/shard_map/all_to_all | solution.py:466
  29.0 5.0 %copy-start.9 = (s32[2048,1]{0,1:T(1,128)S(1)}, s32[2048,1]{0,1:T(1,128)}, u32[]{:S(2)}) copy-start(s32[2048,1]{0,1:T(1,128)} %param.21) | copy-start | bytes 24580
  32.7 53.8 %collective-permute-start = (bf16[1664,512]{1,0:T(8,128)(2,1)}, bf16[1664,512]{1,0:T(8,128)(2,1)S(1)}, u32[]{:S(2)}, u32[]{:S(2)}) collective-permute-start(bf16[1664,512]{1,0:T(8,128)(2,1)} %get-tuple-element.21.w0_ref), channel_id=1, source_target_pairs={{0,1},{1,0},{2,3},{3,2},{4,5},{5,4},{6,7},{7,6},{8,9},{9,8},{10,11... | collective-permute-start | bytes 5111816 | tf_op jit(solution)/shard_map/ppermute | solution.py:462
  36.3 74.0 %collective-permute-start.1 = (bf16[1664,512]{1,0:T(8,128)(2,1)}, bf16[1664,512]{1,0:T(8,128)(2,1)}, u32[]{:S(2)}, u32[]{:S(2)}) collective-permute-start(bf16[1664,512]{1,0:T(8,128)(2,1)} %get-tuple-element.24), channel_id=1, source_target_pairs={{0,2},{1,3},{2,0},{3,1},{4,6},{5,7},{6,4},{7,5},{8,10},{9,11},{10,... | collective-permute-start | bytes 5111816 | tf_op jit(solution)/shard_map/ppermute | solution.py:462
  38.8 75.9 %collective-permute-start.2 = (bf16[1664,512]{1,0:T(8,128)(2,1)}, bf16[1664,512]{1,0:T(8,128)(2,1)}, u32[]{:S(2)}, u32[]{:S(2)}) collective-permute-start(bf16[1664,512]{1,0:T(8,128)(2,1)} %get-tuple-element.24), channel_id=1, source_target_pairs={{0,3},{1,2},{2,1},{3,0},{4,7},{5,6},{6,5},{7,4},{8,11},{9,10},{10,... | collective-permute-start | bytes 5111816 | tf_op jit(solution)/shard_map/ppermute | solution.py:462
  79.3 29.4 %all-to-all-start.2 = ((bf16[32,48,512]{2,1,0:T(8,128)(2,1)}), bf16[32,48,512]{2,1,0:T(8,128)(2,1)S(1)}, u32[]{:S(2)}, u32[]{:S(2)}) async-start(bf16[32,48,512]{2,1,0:T(8,128)(2,1)} %place_rows.1), calls=%async_computation.2 | async-start | bytes 3145728 | tf_op jit(solution)/shard_map/all_to_all | solution.py:466
  86.4 1.2 copy-start.3
  108.7 40.1 %copy-start.4 = (bf16[32,48,512]{2,1,0:T(8,128)(2,1)}, bf16[32,48,512]{2,1,0:T(8,128)(2,1)S(1)}, u32[]{:S(2)}) copy-start(bf16[32,48,512]{2,1,0:T(8,128)(2,1)S(1)} %all-to-all-done.2.x_ref) | copy-start | bytes 4718596
  114.7 33.4 %all-to-all-start.3 = ((bf16[128,48,128]{2,1,0:T(8,128)(2,1)}), bf16[128,48,128]{2,1,0:T(8,128)(2,1)S(1)}, u32[]{:S(2)}, u32[]{:S(2)}) async-start(bf16[128,48,128]{2,1,0:T(8,128)(2,1)} %bitcast.34), calls=%async_computation.3 | async-start | bytes 3145728 | tf_op jit(solution)/shard_map/all_to_all | solution.py:466
  148.1 1.1 copy-start.5
  148.1 17.4 %collective-permute-start.3 = (bf16[2048,128]{1,0:T(8,128)(2,1)}, bf16[2048,128]{1,0:T(8,128)(2,1)}, u32[]{:S(2)}, u32[]{:S(2)}) collective-permute-start(bf16[2048,128]{1,0:T(8,128)(2,1)} %get-tuple-element.26.h0_ref), channel_id=1, source_target_pairs={{0,1},{1,0},{2,3},{3,2},{4,5},{5,4},{6,7},{7,6},{8,9},{9,8},{10,11... | collective-permute-start | bytes 1572872 | tf_op jit(solution)/shard_map/ppermute | solution.py:462
  148.4 17.2 %collective-permute-start.4 = (bf16[2048,128]{1,0:T(8,128)(2,1)}, bf16[2048,128]{1,0:T(8,128)(2,1)}, u32[]{:S(2)}, u32[]{:S(2)}) collective-permute-start(bf16[2048,128]{1,0:T(8,128)(2,1)} %get-tuple-element.26.h0_ref), channel_id=1, source_target_pairs={{0,3},{1,2},{2,1},{3,0},{4,7},{5,6},{6,5},{7,4},{8,11},{9,10},{10,... | collective-permute-start | bytes 1572872 | tf_op jit(solution)/shard_map/ppermute | solution.py:462
  165.6 35.4 %all-to-all-start.4 = ((bf16[128,48,128]{2,1,0:T(8,128)(2,1)}), bf16[128,48,128]{2,1,0:T(8,128)(2,1)S(1)}, u32[]{:S(2)}, u32[]{:S(2)}) async-start(bf16[128,48,128]{2,1,0:T(8,128)(2,1)} %bitcast.36), calls=%async_computation.4 | async-start | bytes 3145728 | tf_op jit(solution)/shard_map/all_to_all | solution.py:466
  171.8 23.0 %collective-permute-start.5 = (bf16[1024,128]{1,0:T(8,128)(2,1)S(1)}, bf16[1024,128]{1,0:T(8,128)(2,1)S(1)}, u32[]{:S(2)}, u32[]{:S(2)}) collective-permute-start(bf16[1024,128]{1,0:T(8,128)(2,1)S(1)} %slice.6), channel_id=1, source_target_pairs={{0,1},{1,0},{2,3},{3,2},{4,5},{5,4},{6,7},{7,6},{8,9},{9,8},{10,11... | collective-permute-start | bytes 786440 | tf_op jit(solution)/shard_map/ppermute | solution.py:462
  174.2 26.8 %copy-start = (s32[1,2048]{1,0:T(1,128)S(1)}, s32[1,2048]{1,0:T(1,128)}, u32[]{:S(2)}) copy-start(s32[1,2048]{1,0:T(1,128)} %get-tuple-element.37.lane_ref) | copy-start | bytes 24580
  174.2 26.8 %copy-start.1 = (s32[1,2048]{1,0:T(1,128)S(1)}, s32[1,2048]{1,0:T(1,128)}, u32[]{:S(2)}) copy-start(s32[1,2048]{1,0:T(1,128)} %get-tuple-element.38.spot_ref) | copy-start | bytes 24580
  174.3 21.7 %collective-permute-start.6 = (bf16[1024,128]{1,0:T(8,128)(2,1)S(1)}, bf16[1024,128]{1,0:T(8,128)(2,1)S(1)}, u32[]{:S(2)}, u32[]{:S(2)}) collective-permute-start(bf16[1024,128]{1,0:T(8,128)(2,1)S(1)} %slice.7), channel_id=1, source_target_pairs={{0,3},{1,2},{2,1},{3,0},{4,7},{5,6},{6,5},{7,4},{8,11},{9,10},{10,... | collective-permute-start | bytes 786440 | tf_op jit(solution)/shard_map/ppermute | solution.py:462
  194.8 1.2 copy-start.6
  196.0 0.7 copy-start.7
  201.0 1.2 copy-start.2

commit v5 on v4

--- a/solution.py
+++ b/solution.py
@@ -514,7 +514,7 @@
     heads, send = attention(
         neighbor_blocks, requests, q, kv, halo, spot_row, lane_row, weights[1:2], parts, half_cap
     )
-    send, x_there, weights[2:] = lax.optimization_barrier((send, x_there, weights[2:]))
+    send, x_there, weights[3] = lax.optimization_barrier((send, x_there, weights[3]))
     heads_there = exchange(send.reshape(parts * 4, half_cap, LANES), ("graph", "mp"))
     heads, heads_there = lax.optimization_barrier((heads, heads_there))
     by_one, by_three = swap(heads, 1), swap(heads, 3)

time: 209 us -> 212 us (1.014)
  starting transfers between devices: 43.9 us -> 47.2 us
    ppermute x7, waiting for transfers between devices: 25.9 us -> 19.9 us  [swap(): return lax.ppermute(array, 'mp', [(i, i ^ change) for i in range(4)])]
    all_to_all x5, waiting for transfers between devices: 59.8 us -> 64.9 us  [exchange(): return lax.all_to_all(array, axes, split_axis=0, concat_axis=0, tiled=True)]
    ppermute x7, starting transfers between devices: 7.94 us -> 12.1 us  [swap(): return lax.ppermute(array, 'mp', [(i, i ^ change) for i in range(4)])]
  transfers between devices with their start and end apart: 12 -> 12, of which waited for: 8 -> 5; matrix products, arithmetic and copies ran while one was open for 3% -> 3% of each run, Pallas kernels for 27% -> 27%
where the time goes in v5:
time: 212 us; the launch traced here: 211 us
  waiting for transfers between devices  84.8 us (40%)
  Pallas kernels  68.5 us (32%)
  starting transfers between devices  47.2 us (22%)
  local copies, waits for them, and re-layouts  5.7 us (3%)
    all_to_all x5, waiting for transfers between devices, exchange(): return lax.all_to_all(array, axes, split_axis=0, concat_axis=0, tiled=True)  64.9 us
    all_to_all x5, starting transfers between devices, exchange(): return lax.all_to_all(array, axes, split_axis=0, concat_axis=0, tiled=True)  35.2 us
    ppermute x7, waiting for transfers between devices, swap(): return lax.ppermute(array, 'mp', [(i, i ^ change) for i in range(4)])  19.9 us
    pallas_call x1, Pallas kernels, attention(): pl.pallas_call(attention_kernel, in_specs=[SMEM, SMEM, VMEM, VMEM, VMEM,...  19.8 us
    pallas_call x1, Pallas kernels, experts(): pl.pallas_call(experts_kernel, in_specs=[SMEM, VMEM, VMEM, HBM, HBM] + [A...  16.4 us
    ppermute x7, starting transfers between devices, swap(): return lax.ppermute(array, 'mp', [(i, i ^ change) for i in range(4)])  12.1 us
    pallas_call x1, Pallas kernels, place_rows(): pl.pallas_call(place_kernel, in_specs=[VMEM, VMEM], out_specs=VMEM, out_s...  7.38 us
    pallas_call x1, Pallas kernels, combine(): pl.pallas_call(combine_kernel, in_specs=[VMEM] * 2 + [HBM] * 2, out_specs...  6.2 us
  transfers between devices with their start and end apart: 12, of which 5 were waited for; matrix products, arithmetic and copies ran while one was open for 3% of the time, Pallas kernels for 27%

profile of v5, /device:TPU:1, one launch (start us, length us, event | category | flops | bytes accessed | tf_op | source)
XLA Modules:
  0.0 210.9 jit_solution(11965226236002135327)
XLA Ops:
  0.6 1.7 make_requests.1.asked_ref
  2.4 9.6 %all-to-all-start = ((s32[32,1,2]{2,1,0:T(1,128)}), s32[32,1,2]{2,1,0:T(1,128)S(1)}, u32[]{:S(2)}, u32[]{:S(2)}) async-start(s32[32,1,2]{2,1,0:T(1,128)} %bitcast.37), calls=%async_computation | async-start | bytes 32768 | tf_op jit(solution)/shard_map/all_to_all | solution.py:466
  12.0 5.1 %qkv.1 = (bf16[2048,128]{1,0:T(8,128)(2,1)}, bf16[16,128,256]{2,1,0:T(8,128)(2,1)}) custom-call(bf16[2048,512]{1,0:T(8,128)(2,1)} %x_ref.5, bf16[3,512,128]{2,1,0:T(8,128)(2,1)} %w_ref.1, f32[2]{0:T(128)} %scale_ref.1), custom_call_target="tpu_custom_call" | custom-call | flops 805306368 | bytes 3670016 | tf_op jit(solution)/shard_map/qkv/pallas_call | solution.py:60
  17.1 1.8 all-to-all-done.wanted_ref
  18.8 0.0 copy-start.8
  18.8 0.6 copy-done.8
  19.4 3.8 %pick_blocks.1._ = bf16[64,128,256]{2,1,0:T(8,128)(2,1)} custom-call(s32[32,1,2]{2,1,0:T(1,128)} %copy-done.8, bf16[16,128,256]{2,1,0:T(8,128)(2,1)} %get-tuple-element.19.kv_ref), custom_call_target="tpu_custom_call" | custom-call | bytes 8388608 | tf_op jit(solution)/shard_map/pick_blocks/pallas_call | solution.py:156
  23.3 5.7 %all-to-all-start.1 = ((bf16[64,128,256]{2,1,0:T(8,128)(2,1)}), bf16[64,128,256]{2,1,0:T(8,128)(2,1)}, u32[]{:S(2)}, u32[]{:S(2)}) async-start(bf16[64,128,256]{2,1,0:T(8,128)(2,1)} %pick_blocks.1._), calls=%async_computation.1 | async-start | bytes 8388608 | tf_op jit(solution)/shard_map/all_to_all | solution.py:466
  29.0 0.0 copy-start.9
  29.0 3.7 %split_weights.1 = (bf16[1664,512]{1,0:T(8,128)(2,1)}, bf16[1664,512]{1,0:T(8,128)(2,1)}) custom-call(s32[1]{0:T(128)} %bitcast.me_ref, bf16[2,512,512]{2,1,0:T(8,128)(2,1)} %gate_ref.1, bf16[2,512,512]{2,1,0:T(8,128)(2,1)} %up_ref.1, bf16[2,512,512]{2,1,0:T(8,128)(2,1)} %down_ref.1, bf16[128,512]{1,0:T(8,128)(2,1)} %out_w_ref.1, ...), custom_call_target="tpu_custom_call" | custom-call | bytes 6815744 | tf_op jit(solution)/shard_map/split_weights/pallas_call | solution.py:127
  32.7 1.3 collective-permute-start
  34.0 0.0 copy-done.9
  34.0 1.7 fusion.2
  35.7 0.7 compare_select_fusion
  36.4 1.8 collective-permute-start.1
  38.2 7.4 %place_rows.1 = bf16[32,48,512]{2,1,0:T(8,128)(2,1)} custom-call(s32[1,2048]{1,0:T(1,128)} %get-tuple-element.34.spot_ref, bf16[2048,512]{1,0:T(8,128)(2,1)} %x_ref.5), custom_call_target="tpu_custom_call" | custom-call | flops 3221225472 | bytes 4194304 | tf_op jit(solution)/shard_map/place_rows/pallas_call | solution.py:271
  45.6 33.6 %all-to-all-done.1.halo_ref = bf16[64,128,256]{2,1,0:T(8,128)(2,1)} async-done(((bf16[64,128,256]{2,1,0:T(8,128)(2,1)}), bf16[64,128,256]{2,1,0:T(8,128)(2,1)}, u32[]{:S(2)}, u32[]{:S(2)}) %all-to-all-start.1) | async-done | bytes 4194336 | tf_op jit(solution)/shard_map/all_to_all | solution.py:466
  79.2 7.1 %all-to-all-start.2 = ((bf16[32,48,512]{2,1,0:T(8,128)(2,1)}), bf16[32,48,512]{2,1,0:T(8,128)(2,1)S(1)}, u32[]{:S(2)}, u32[]{:S(2)}) async-start(bf16[32,48,512]{2,1,0:T(8,128)(2,1)} %place_rows.1), calls=%async_computation.2 | async-start | bytes 3145728 | tf_op jit(solution)/shard_map/all_to_all | solution.py:466
  86.4 2.8 %collective-permute-start.2 = (bf16[1664,512]{1,0:T(8,128)(2,1)}, bf16[1664,512]{1,0:T(8,128)(2,1)}, u32[]{:S(2)}, u32[]{:S(2)}) collective-permute-start(bf16[1664,512]{1,0:T(8,128)(2,1)} %get-tuple-element.23), channel_id=1, source_target_pairs={{0,2},{1,3},{2,0},{3,1},{4,6},{5,7},{6,4},{7,5},{8,10},{9,11},{10,... | collective-permute-start | bytes 5111816 | tf_op jit(solution)/shard_map/ppermute | solution.py:462
  89.2 0.0 collective-permute-done.rest_0_.w1_ref
  89.2 0.0 copy-start.3
  89.2 1.2 copy-done.3
  90.4 19.8 %attention.1 = (bf16[2048,128]{1,0:T(8,128)(2,1)}, bf16[32,4,48,128]{3,2,1,0:T(8,128)(2,1)}) custom-call(s32[16,12]{1,0:T(8,128)} %near_ref.3, s32[32,2]{1,0:T(8,128)} %make_requests.1.asked_ref, bf16[2048,128]{1,0:T(8,128)(2,1)} %get-tuple-element.18.q_ref, bf16[16,128,256]{2,1,0:T(8,128)(2,1)} %get-tuple-element.19.kv_ref, ...), custom_call_target="tpu_custom_call" | custom-call | flops 12000000000 | bytes 8388608 | tf_op jit(solution)/shard_map/attention/pallas_call | solution.py:235
  110.2 0.0 all-to-all-done.2.x_ref
  110.2 0.0 copy-start.4
  110.3 0.0 collective-permute-done.1.w3_ref
  110.3 7.8 %all-to-all-start.3 = ((bf16[128,48,128]{2,1,0:T(8,128)(2,1)}), bf16[128,48,128]{2,1,0:T(8,128)(2,1)S(1)}, u32[]{:S(2)}, u32[]{:S(2)}) async-start(bf16[128,48,128]{2,1,0:T(8,128)(2,1)} %bitcast.35), calls=%async_computation.3 | async-start | bytes 3145728 | tf_op jit(solution)/shard_map/all_to_all | solution.py:466
  118.1 1.3 bitcast_convert_fusion.route_ref
  119.4 29.5 %all-to-all-done.3 = bf16[128,48,128]{2,1,0:T(8,128)(2,1)S(1)} async-done(((bf16[128,48,128]{2,1,0:T(8,128)(2,1)}), bf16[128,48,128]{2,1,0:T(8,128)(2,1)S(1)}, u32[]{:S(2)}, u32[]{:S(2)}) %all-to-all-start.3) | async-done | bytes 1572896 | tf_op jit(solution)/shard_map/all_to_all | solution.py:466
  148.9 0.0 copy-start.5
  148.9 1.2 collective-permute-start.3
  150.1 1.5 collective-permute-start.4
  151.7 0.0 collective-permute-done.2.w2_ref
  151.7 0.0 copy-done.4
  151.7 0.0 copy-done.5
  151.7 16.4 %experts.1 = bf16[32,4,48,128]{3,2,1,0:T(8,128)(2,1)} custom-call(s32[1]{0:T(128)} %bitcast.me_ref, f32[1,512]{1,0:T(1,128)} %bitcast.40, f32[1,512]{1,0:T(1,128)} %bitcast_convert_fusion.route_ref, bf16[32,4,48,128]{3,2,1,0:T(8,128)(2,1)} %bitcast.34, bf16[32,48,512]{2,1,0:T(8,128)(2,1)} %copy-done.4, bf16[1664,512]{1,0:T(8,128)(2,1)} %get-tuple-element.20.w0_ref, ...), custom_call_target="tpu_custom_call" | custom-call | flops 10468982784 | bytes 12582912 | tf_op jit(solution)/shard_map/experts/pallas_call | solution.py:348
  168.0 0.0 collective-permute-done.3.h1_ref
  168.1 0.0 collective-permute-done.4.h3_ref
  168.1 4.9 %all-to-all-start.4 = ((bf16[128,48,128]{2,1,0:T(8,128)(2,1)}), bf16[128,48,128]{2,1,0:T(8,128)(2,1)S(1)}, u32[]{:S(2)}, u32[]{:S(2)}) async-start(bf16[128,48,128]{2,1,0:T(8,128)(2,1)} %bitcast.36), calls=%async_computation.4 | async-start | bytes 3145728 | tf_op jit(solution)/shard_map/all_to_all | solution.py:466
  173.0 1.0 slice.6
  174.0 1.5 collective-permute-start.5
  175.5 1.0 slice.7
  176.4 0.0 copy-start
  176.5 0.0 copy-start.1
  176.5 1.9 collective-permute-start.6
  178.3 18.6 %collective-permute-done.5.top_ref = bf16[1024,128]{1,0:T(8,128)(2,1)S(1)} collective-permute-done((bf16[1024,128]{1,0:T(8,128)(2,1)S(1)}, bf16[1024,128]{1,0:T(8,128)(2,1)S(1)}, u32[]{:S(2)}, u32[]{:S(2)}) %collective-permute-start.5) | collective-permute-done | bytes 262176 | tf_op jit(solution)/shard_map/ppermute | solution.py:462
  197.0 0.0 copy-start.6
  197.0 1.2 collective-permute-done.6.bottom_ref
  198.2 0.0 copy-done.6
  198.2 0.0 copy-start.7
  198.2 0.7 copy-done.7
  199.0 4.3 %attention_columns.1 = (bf16[2048,128]{1,0:T(8,128)(2,1)}, f32[2048,128]{1,0:T(8,128)}) custom-call(s32[1]{0:T(128)} %bitcast.me_ref, bf16[2048,128]{1,0:T(8,128)(2,1)} %get-tuple-element.25.h0_ref, bf16[2048,128]{1,0:T(8,128)(2,1)} %collective-permute-done.3.h1_ref, bf16[2048,128]{1,0:T(8,128)(2,1)} %collective-permute-done.4.h3_ref, ...), custom_call_target="tpu_custom_call" | custom-call | flops 268435456 | bytes 8388608 | tf_op jit(solution)/shard_map/attention_columns/pallas_call | solution.py:388
  203.2 0.0 all-to-all-done.4
  203.2 0.0 copy-done
  203.3 0.0 copy-done.1
  203.3 0.0 copy-start.2
  203.3 1.2 copy-done.2
  204.5 6.2 %combine.1 = bf16[2048,128]{1,0:T(8,128)(2,1)} custom-call(s32[1,2048]{1,0:T(1,128)S(1)} %copy-done.1, s32[1,2048]{1,0:T(1,128)S(1)} %copy-done, f32[2048,128]{1,0:T(8,128)S(1)} %copy-done.2, bf16[32,4,48,128]{3,2,1,0:T(8,128)(2,1)S(1)} %bitcast.33), custom_call_target="tpu_custom_call" | custom-call | flops 3221225472 | bytes 4194304 | tf_op jit(solution)/shard_map/combine/pallas_call | solution.py:445
  (1 shorter events, 0.0 us)
Async XLA Ops:
  2.4 16.5 %all-to-all-start = ((s32[32,1,2]{2,1,0:T(1,128)}), s32[32,1,2]{2,1,0:T(1,128)S(1)}, u32[]{:S(2)}, u32[]{:S(2)}) async-start(s32[32,1,2]{2,1,0:T(1,128)} %bitcast.37), calls=%async_computation | async-start | bytes 32768 | tf_op jit(solution)/shard_map/all_to_all | solution.py:466
  18.8 0.6 copy-start.8
  23.3 56.0 %all-to-all-start.1 = ((bf16[64,128,256]{2,1,0:T(8,128)(2,1)}), bf16[64,128,256]{2,1,0:T(8,128)(2,1)}, u32[]{:S(2)}, u32[]{:S(2)}) async-start(bf16[64,128,256]{2,1,0:T(8,128)(2,1)} %pick_blocks.1._), calls=%async_computation.1 | async-start | bytes 8388608 | tf_op jit(solution)/shard_map/all_to_all | solution.py:466
  29.0 5.0 %copy-start.9 = (s32[2048,1]{0,1:T(1,128)S(1)}, s32[2048,1]{0,1:T(1,128)}, u32[]{:S(2)}) copy-start(s32[2048,1]{0,1:T(1,128)} %param.21) | copy-start | bytes 24580
  32.7 56.5 %collective-permute-start = (bf16[1664,512]{1,0:T(8,128)(2,1)}, bf16[1664,512]{1,0:T(8,128)(2,1)S(1)}, u32[]{:S(2)}, u32[]{:S(2)}) collective-permute-start(bf16[1664,512]{1,0:T(8,128)(2,1)} %get-tuple-element.20.w0_ref), channel_id=1, source_target_pairs={{0,1},{1,0},{2,3},{3,2},{4,5},{5,4},{6,7},{7,6},{8,9},{9,8},{10,11... | collective-permute-start | bytes 5111816 | tf_op jit(solution)/shard_map/ppermute | solution.py:462
  36.4 73.8 %collective-permute-start.1 = (bf16[1664,512]{1,0:T(8,128)(2,1)}, bf16[1664,512]{1,0:T(8,128)(2,1)}, u32[]{:S(2)}, u32[]{:S(2)}) collective-permute-start(bf16[1664,512]{1,0:T(8,128)(2,1)} %get-tuple-element.23), channel_id=1, source_target_pairs={{0,3},{1,2},{2,1},{3,0},{4,7},{5,6},{6,5},{7,4},{8,11},{9,10},{10,... | collective-permute-start | bytes 5111816 | tf_op jit(solution)/shard_map/ppermute | solution.py:462
  79.2 31.0 %all-to-all-start.2 = ((bf16[32,48,512]{2,1,0:T(8,128)(2,1)}), bf16[32,48,512]{2,1,0:T(8,128)(2,1)S(1)}, u32[]{:S(2)}, u32[]{:S(2)}) async-start(bf16[32,48,512]{2,1,0:T(8,128)(2,1)} %place_rows.1), calls=%async_computation.2 | async-start | bytes 3145728 | tf_op jit(solution)/shard_map/all_to_all | solution.py:466
  86.4 65.3 %collective-permute-start.2 = (bf16[1664,512]{1,0:T(8,128)(2,1)}, bf16[1664,512]{1,0:T(8,128)(2,1)}, u32[]{:S(2)}, u32[]{:S(2)}) collective-permute-start(bf16[1664,512]{1,0:T(8,128)(2,1)} %get-tuple-element.23), channel_id=1, source_target_pairs={{0,2},{1,3},{2,0},{3,1},{4,6},{5,7},{6,4},{7,5},{8,10},{9,11},{10,... | collective-permute-start | bytes 5111816 | tf_op jit(solution)/shard_map/ppermute | solution.py:462
  89.2 1.2 copy-start.3
  110.2 41.4 %copy-start.4 = (bf16[32,48,512]{2,1,0:T(8,128)(2,1)}, bf16[32,48,512]{2,1,0:T(8,128)(2,1)S(1)}, u32[]{:S(2)}) copy-start(bf16[32,48,512]{2,1,0:T(8,128)(2,1)S(1)} %all-to-all-done.2.x_ref) | copy-start | bytes 4718596
  110.3 38.6 %all-to-all-start.3 = ((bf16[128,48,128]{2,1,0:T(8,128)(2,1)}), bf16[128,48,128]{2,1,0:T(8,128)(2,1)S(1)}, u32[]{:S(2)}, u32[]{:S(2)}) async-start(bf16[128,48,128]{2,1,0:T(8,128)(2,1)} %bitcast.35), calls=%async_computation.3 | async-start | bytes 3145728 | tf_op jit(solution)/shard_map/all_to_all | solution.py:466
  148.9 2.8 %copy-start.5 = (bf16[128,48,128]{2,1,0:T(8,128)(2,1)}, bf16[128,48,128]{2,1,0:T(8,128)(2,1)S(1)}, u32[]{:S(2)}) copy-start(bf16[128,48,128]{2,1,0:T(8,128)(2,1)S(1)} %all-to-all-done.3) | copy-start | bytes 4718596
  148.9 19.2 %collective-permute-start.3 = (bf16[2048,128]{1,0:T(8,128)(2,1)}, bf16[2048,128]{1,0:T(8,128)(2,1)}, u32[]{:S(2)}, u32[]{:S(2)}) collective-permute-start(bf16[2048,128]{1,0:T(8,128)(2,1)} %get-tuple-element.25.h0_ref), channel_id=1, source_target_pairs={{0,1},{1,0},{2,3},{3,2},{4,5},{5,4},{6,7},{7,6},{8,9},{9,8},{10,11... | collective-permute-start | bytes 1572872 | tf_op jit(solution)/shard_map/ppermute | solution.py:462
  150.1 17.9 %collective-permute-start.4 = (bf16[2048,128]{1,0:T(8,128)(2,1)}, bf16[2048,128]{1,0:T(8,128)(2,1)}, u32[]{:S(2)}, u32[]{:S(2)}) collective-permute-start(bf16[2048,128]{1,0:T(8,128)(2,1)} %get-tuple-element.25.h0_ref), channel_id=1, source_target_pairs={{0,3},{1,2},{2,1},{3,0},{4,7},{5,6},{6,5},{7,4},{8,11},{9,10},{10,... | collective-permute-start | bytes 1572872 | tf_op jit(solution)/shard_map/ppermute | solution.py:462
  168.1 35.2 %all-to-all-start.4 = ((bf16[128,48,128]{2,1,0:T(8,128)(2,1)}), bf16[128,48,128]{2,1,0:T(8,128)(2,1)S(1)}, u32[]{:S(2)}, u32[]{:S(2)}) async-start(bf16[128,48,128]{2,1,0:T(8,128)(2,1)} %bitcast.36), calls=%async_computation.4 | async-start | bytes 3145728 | tf_op jit(solution)/shard_map/all_to_all | solution.py:466
  174.0 23.0 %collective-permute-start.5 = (bf16[1024,128]{1,0:T(8,128)(2,1)S(1)}, bf16[1024,128]{1,0:T(8,128)(2,1)S(1)}, u32[]{:S(2)}, u32[]{:S(2)}) collective-permute-start(bf16[1024,128]{1,0:T(8,128)(2,1)S(1)} %slice.6), channel_id=1, source_target_pairs={{0,1},{1,0},{2,3},{3,2},{4,5},{5,4},{6,7},{7,6},{8,9},{9,8},{10,11... | collective-permute-start | bytes 786440 | tf_op jit(solution)/shard_map/ppermute | solution.py:462
  176.4 26.8 %copy-start = (s32[1,2048]{1,0:T(1,128)S(1)}, s32[1,2048]{1,0:T(1,128)}, u32[]{:S(2)}) copy-start(s32[1,2048]{1,0:T(1,128)} %get-tuple-element.35.lane_ref) | copy-start | bytes 24580
  176.5 26.8 %copy-start.1 = (s32[1,2048]{1,0:T(1,128)S(1)}, s32[1,2048]{1,0:T(1,128)}, u32[]{:S(2)}) copy-start(s32[1,2048]{1,0:T(1,128)} %get-tuple-element.36.spot_ref) | copy-start | bytes 24580
  176.5 21.8 %collective-permute-start.6 = (bf16[1024,128]{1,0:T(8,128)(2,1)S(1)}, bf16[1024,128]{1,0:T(8,128)(2,1)S(1)}, u32[]{:S(2)}, u32[]{:S(2)}) collective-permute-start(bf16[1024,128]{1,0:T(8,128)(2,1)S(1)} %slice.7), channel_id=1, source_target_pairs={{0,3},{1,2},{2,1},{3,0},{4,7},{5,6},{6,5},{7,4},{8,11},{9,10},{10,... | collective-permute-start | bytes 786440 | tf_op jit(solution)/shard_map/ppermute | solution.py:462
  197.0 1.2 copy-start.6
  198.2 0.7 copy-start.7
  203.3 1.2 copy-start.2

commit v6 on v5

--- a/solution.py
+++ b/solution.py
@@ -55,7 +55,7 @@
 
 def qkv(x, w, scale):
     rows, width = x.shape
-    tile = 512
+    tile = 1024
     blocks = tile // ROWS_BLK
     return pl.pallas_call(
         qkv_kernel,
@@ -279,6 +279,22 @@
     )(spot_row, x)
 
 
+def route_kernel(route_ref, *rest):
+    rest[-1][...] = route_ref[...]
+
+
+def hold_route(route, after):
+    return pl.pallas_call(
+        route_kernel,
+        in_specs=[VMEM] + [ANY] * len(after),
+        out_specs=VMEM,
+        out_shape=jax.ShapeDtypeStruct(route.shape, route.dtype),
+        compiler_params=params(60),
+        cost_estimate=cost(2 * 10**10, 10**7),
+        name="hold_route",
+    )(route, *after)
+
+
 def experts_kernel(me_ref, gain_ref, route_ref, h_ref, x_ref, w0_ref, w1_ref, w2_ref, w3_ref, *rest):
     out_ref, heads, features, project, quarters, results, sems = rest[-7:]
     me = me_ref[0]
@@ -514,9 +530,10 @@
     heads, send = attention(
         neighbor_blocks, requests, q, kv, halo, spot_row, lane_row, weights[1:2], parts, half_cap
     )
-    send, x_there, weights[3] = lax.optimization_barrier((send, x_there, weights[3]))
+    send, x_there = lax.optimization_barrier((send, x_there))
     heads_there = exchange(send.reshape(parts * 4, half_cap, LANES), ("graph", "mp"))
-    heads, heads_there = lax.optimization_barrier((heads, heads_there))
+    route = hold_route(route, [send] + weights[2:])
+    heads, heads_there, route = lax.optimization_barrier((heads, heads_there, route))
     by_one, by_three = swap(heads, 1), swap(heads, 3)
     produced = experts(
         me_ref,

time: 212 us -> 204 us (0.962)
  waiting for transfers between devices: 84.8 us -> 81.3 us
  starting transfers between devices: 47.2 us -> 44.4 us
    all_to_all x5, waiting for transfers between devices: 64.9 us -> 59.6 us  [exchange(): return lax.all_to_all(array, axes, split_axis=0, concat_axis=0, tiled=True)]
    ppermute x7, starting transfers between devices: 12.1 us -> 7.93 us  [swap(): return lax.ppermute(array, 'mp', [(i, i ^ change) for i in range(4)])]
    unnamed x20 -> x24, local copies, waits for them, and re-layouts: 3.77 us -> 4.27 us
  transfers between devices with their start and end apart: 12 -> 12, of which waited for: 5 -> 5; matrix products, arithmetic and copies ran while one was open for 3% -> 2% of each run, Pallas kernels for 27% -> 28%
where the time goes in v6:
time: 204 us; the launch traced here: 203 us
  waiting for transfers between devices  81.3 us (40%)
  Pallas kernels  68.7 us (34%)
  starting transfers between devices  44.4 us (22%)
  local copies, waits for them, and re-layouts  4.3 us (2%)
    all_to_all x5, waiting for transfers between devices, exchange(): return lax.all_to_all(array, axes, split_axis=0, concat_axis=0, tiled=True)  59.6 us
    all_to_all x5, starting transfers between devices, exchange(): return lax.all_to_all(array, axes, split_axis=0, concat_axis=0, tiled=True)  36.5 us
    ppermute x7, waiting for transfers between devices, swap(): return lax.ppermute(array, 'mp', [(i, i ^ change) for i in range(4)])  21.8 us
    pallas_call x1, Pallas kernels, attention(): pl.pallas_call(attention_kernel, in_specs=[SMEM, SMEM, VMEM, VMEM, VMEM,...  19.8 us
    pallas_call x1, Pallas kernels, experts(): pl.pallas_call(experts_kernel, in_specs=[SMEM, VMEM, VMEM, HBM, HBM] + [A...  16.3 us
    ppermute x7, starting transfers between devices, swap(): return lax.ppermute(array, 'mp', [(i, i ^ change) for i in range(4)])  7.93 us
    pallas_call x1, Pallas kernels, place_rows(): pl.pallas_call(place_kernel, in_specs=[VMEM, VMEM], out_specs=VMEM, out_s...  7.38 us
    pallas_call x1, Pallas kernels, combine(): pl.pallas_call(combine_kernel, in_specs=[VMEM] * 2 + [HBM] * 2, out_specs...  6.2 us
  transfers between devices with their start and end apart: 12, of which 5 were waited for; matrix products, arithmetic and copies ran while one was open for 2% of the time, Pallas kernels for 28%

profile of v6, /device:TPU:1, one launch (start us, length us, event | category | flops | bytes accessed | tf_op | source)
XLA Modules:
  0.0 203.4 jit_solution(4587536855548831731)
XLA Ops:
  0.6 1.7 make_requests.1.asked_ref
  2.4 9.6 %all-to-all-start = ((s32[32,1,2]{2,1,0:T(1,128)}), s32[32,1,2]{2,1,0:T(1,128)S(1)}, u32[]{:S(2)}, u32[]{:S(2)}) async-start(s32[32,1,2]{2,1,0:T(1,128)} %bitcast.37), calls=%async_computation | async-start | bytes 32768 | tf_op jit(solution)/shard_map/all_to_all | solution.py:482
  12.0 4.3 %qkv.1 = (bf16[2048,128]{1,0:T(8,128)(2,1)}, bf16[16,128,256]{2,1,0:T(8,128)(2,1)}) custom-call(bf16[2048,512]{1,0:T(8,128)(2,1)} %x_ref.5, bf16[3,512,128]{2,1,0:T(8,128)(2,1)} %w_ref.1, f32[2]{0:T(128)} %scale_ref.1), custom_call_target="tpu_custom_call" | custom-call | flops 805306368 | bytes 3670016 | tf_op jit(solution)/shard_map/qkv/pallas_call | solution.py:60
  16.3 2.5 %all-to-all-done.wanted_ref = s32[32,1,2]{2,1,0:T(1,128)S(1)} async-done(((s32[32,1,2]{2,1,0:T(1,128)}), s32[32,1,2]{2,1,0:T(1,128)S(1)}, u32[]{:S(2)}, u32[]{:S(2)}) %all-to-all-start) | async-done | bytes 288 | tf_op jit(solution)/shard_map/all_to_all | solution.py:482
  18.8 0.0 copy-start.10
  18.8 0.6 copy-done.10
  19.4 3.8 %pick_blocks.1._ = bf16[64,128,256]{2,1,0:T(8,128)(2,1)} custom-call(s32[32,1,2]{2,1,0:T(1,128)} %copy-done.10, bf16[16,128,256]{2,1,0:T(8,128)(2,1)} %get-tuple-element.19.kv_ref), custom_call_target="tpu_custom_call" | custom-call | bytes 8388608 | tf_op jit(solution)/shard_map/pick_blocks/pallas_call | solution.py:156
  23.3 5.1 %all-to-all-start.1 = ((bf16[64,128,256]{2,1,0:T(8,128)(2,1)}), bf16[64,128,256]{2,1,0:T(8,128)(2,1)}, u32[]{:S(2)}, u32[]{:S(2)}) async-start(bf16[64,128,256]{2,1,0:T(8,128)(2,1)} %pick_blocks.1._), calls=%async_computation.1 | async-start | bytes 8388608 | tf_op jit(solution)/shard_map/all_to_all | solution.py:482
  28.4 0.0 copy-start.11
  28.4 3.6 %split_weights.1 = (bf16[1664,512]{1,0:T(8,128)(2,1)}, bf16[1664,512]{1,0:T(8,128)(2,1)}) custom-call(s32[1]{0:T(128)} %bitcast.me_ref, bf16[2,512,512]{2,1,0:T(8,128)(2,1)} %gate_ref.1, bf16[2,512,512]{2,1,0:T(8,128)(2,1)} %up_ref.1, bf16[2,512,512]{2,1,0:T(8,128)(2,1)} %down_ref.1, bf16[128,512]{1,0:T(8,128)(2,1)} %out_w_ref.1, ...), custom_call_target="tpu_custom_call" | custom-call | bytes 6815744 | tf_op jit(solution)/shard_map/split_weights/pallas_call | solution.py:127
  32.0 1.3 collective-permute-start
  33.3 0.0 copy-done.11
  33.3 1.7 fusion.2
  35.0 0.7 compare_select_fusion
  35.7 2.4 %collective-permute-start.1 = (bf16[1664,512]{1,0:T(8,128)(2,1)}, bf16[1664,512]{1,0:T(8,128)(2,1)}, u32[]{:S(2)}, u32[]{:S(2)}) collective-permute-start(bf16[1664,512]{1,0:T(8,128)(2,1)} %get-tuple-element.24), channel_id=1, source_target_pairs={{0,2},{1,3},{2,0},{3,1},{4,6},{5,7},{6,4},{7,5},{8,10},{9,11},{10,... | collective-permute-start | bytes 5111816 | tf_op jit(solution)/shard_map/ppermute | solution.py:478
  38.1 0.2 collective-permute-start.2
  38.3 7.4 %place_rows.1 = bf16[32,48,512]{2,1,0:T(8,128)(2,1)} custom-call(s32[1,2048]{1,0:T(1,128)} %get-tuple-element.34.spot_ref, bf16[2048,512]{1,0:T(8,128)(2,1)} %x_ref.5), custom_call_target="tpu_custom_call" | custom-call | flops 3221225472 | bytes 4194304 | tf_op jit(solution)/shard_map/place_rows/pallas_call | solution.py:271
  45.7 33.1 %all-to-all-done.1.halo_ref = bf16[64,128,256]{2,1,0:T(8,128)(2,1)} async-done(((bf16[64,128,256]{2,1,0:T(8,128)(2,1)}), bf16[64,128,256]{2,1,0:T(8,128)(2,1)}, u32[]{:S(2)}, u32[]{:S(2)}) %all-to-all-start.1) | async-done | bytes 4194336 | tf_op jit(solution)/shard_map/all_to_all | solution.py:482
  78.8 7.1 %all-to-all-start.2 = ((bf16[32,48,512]{2,1,0:T(8,128)(2,1)}), bf16[32,48,512]{2,1,0:T(8,128)(2,1)S(1)}, u32[]{:S(2)}, u32[]{:S(2)}) async-start(bf16[32,48,512]{2,1,0:T(8,128)(2,1)} %place_rows.1), calls=%async_computation.2 | async-start | bytes 3145728 | tf_op jit(solution)/shard_map/all_to_all | solution.py:482
  85.9 1.3 bitcast_convert_fusion.route_ref
  87.2 0.0 collective-permute-done.rest_0_.w1_ref
  87.2 0.0 copy-start.3
  87.2 1.2 copy-done.3
  88.4 19.8 %attention.1 = (bf16[2048,128]{1,0:T(8,128)(2,1)}, bf16[32,4,48,128]{3,2,1,0:T(8,128)(2,1)}) custom-call(s32[16,12]{1,0:T(8,128)} %near_ref.3, s32[32,2]{1,0:T(8,128)} %make_requests.1.asked_ref, bf16[2048,128]{1,0:T(8,128)(2,1)} %get-tuple-element.18.q_ref, bf16[16,128,256]{2,1,0:T(8,128)(2,1)} %get-tuple-element.19.kv_ref, ...), custom_call_target="tpu_custom_call" | custom-call | flops 12000000000 | bytes 8388608 | tf_op jit(solution)/shard_map/attention/pallas_call | solution.py:235
  108.2 0.0 all-to-all-done.2.x_ref
  108.2 0.0 copy-start.4
  108.2 9.4 %all-to-all-start.3 = ((bf16[128,48,128]{2,1,0:T(8,128)(2,1)}), bf16[128,48,128]{2,1,0:T(8,128)(2,1)S(1)}, u32[]{:S(2)}, u32[]{:S(2)}) async-start(bf16[128,48,128]{2,1,0:T(8,128)(2,1)} %bitcast.36), calls=%async_computation.3 | async-start | bytes 3145728 | tf_op jit(solution)/shard_map/all_to_all | solution.py:482
  117.6 0.0 collective-permute-done.1.rest_1_.w2_ref
  117.7 0.0 collective-permute-done.2.rest_2_.w3_ref
  117.7 1.2 hold_route.1.route_ref
  118.9 0.0 copy-done.4
  118.9 23.9 %all-to-all-done.3 = bf16[128,48,128]{2,1,0:T(8,128)(2,1)S(1)} async-done(((bf16[128,48,128]{2,1,0:T(8,128)(2,1)}), bf16[128,48,128]{2,1,0:T(8,128)(2,1)S(1)}, u32[]{:S(2)}, u32[]{:S(2)}) %all-to-all-start.3) | async-done | bytes 1572896 | tf_op jit(solution)/shard_map/all_to_all | solution.py:482
  142.9 0.0 copy-start.5
  142.9 0.3 collective-permute-start.3
  143.2 0.4 collective-permute-start.4
  143.5 0.5 copy-done.5
  144.0 16.3 %experts.1 = bf16[32,4,48,128]{3,2,1,0:T(8,128)(2,1)} custom-call(s32[1]{0:T(128)} %bitcast.me_ref, f32[1,512]{1,0:T(1,128)} %bitcast.40, f32[1,512]{1,0:T(1,128)} %hold_route.1.route_ref, bf16[32,4,48,128]{3,2,1,0:T(8,128)(2,1)} %bitcast.35, bf16[32,48,512]{2,1,0:T(8,128)(2,1)} %copy-done.4, bf16[1664,512]{1,0:T(8,128)(2,1)} %get-tuple-element.20.w0_ref, ...), custom_call_target="tpu_custom_call" | custom-call | flops 10468982784 | bytes 12582912 | tf_op jit(solution)/shard_map/experts/pallas_call | solution.py:364
  160.3 0.0 collective-permute-done.3.h1_ref
  160.3 0.0 copy-start.6
  160.3 0.0 collective-permute-done.4.h3_ref
  160.4 0.0 copy-start.7
  160.4 5.2 %all-to-all-start.4 = ((bf16[128,48,128]{2,1,0:T(8,128)(2,1)}), bf16[128,48,128]{2,1,0:T(8,128)(2,1)S(1)}, u32[]{:S(2)}, u32[]{:S(2)}) async-start(bf16[128,48,128]{2,1,0:T(8,128)(2,1)} %bitcast.34), calls=%async_computation.4 | async-start | bytes 3145728 | tf_op jit(solution)/shard_map/all_to_all | solution.py:482
  165.6 0.0 copy-done.7
  165.6 1.5 collective-permute-start.5
  167.1 0.0 copy-done.6
  167.1 0.0 copy-start
  167.1 0.0 copy-start.1
  167.1 1.9 collective-permute-start.6
  169.0 20.5 %collective-permute-done.5.top_ref = bf16[1024,128]{1,0:T(8,128)(2,1)S(1)} collective-permute-done((bf16[1024,128]{1,0:T(8,128)(2,1)S(1)}, bf16[1024,128]{1,0:T(8,128)(2,1)S(1)}, u32[]{:S(2)}, u32[]{:S(2)}) %collective-permute-start.5) | collective-permute-done | bytes 262176 | tf_op jit(solution)/shard_map/ppermute | solution.py:478
  189.6 0.0 copy-start.8
  189.6 1.2 collective-permute-done.6.bottom_ref
  190.8 0.0 copy-done.8
  190.8 0.0 copy-start.9
  190.8 0.7 copy-done.9
  191.5 4.3 %attention_columns.1 = (bf16[2048,128]{1,0:T(8,128)(2,1)}, f32[2048,128]{1,0:T(8,128)}) custom-call(s32[1]{0:T(128)} %bitcast.me_ref, bf16[2048,128]{1,0:T(8,128)(2,1)} %get-tuple-element.25.h0_ref, bf16[2048,128]{1,0:T(8,128)(2,1)} %copy-done.6, bf16[2048,128]{1,0:T(8,128)(2,1)} %copy-done.7, bf16[1024,128]{1,0:T(8,128)(2,1)} %copy-done.8, ...), custom_call_target="tpu_custom_call" | custom-call | flops 268435456 | bytes 8388608 | tf_op jit(solution)/shard_map/attention_columns/pallas_call | solution.py:404
  195.8 0.0 all-to-all-done.4
  195.8 0.0 copy-done
  195.8 0.0 copy-done.1
  195.8 0.0 copy-start.2
  195.8 1.2 copy-done.2
  197.0 6.2 %combine.1 = bf16[2048,128]{1,0:T(8,128)(2,1)} custom-call(s32[1,2048]{1,0:T(1,128)S(1)} %copy-done.1, s32[1,2048]{1,0:T(1,128)S(1)} %copy-done, f32[2048,128]{1,0:T(8,128)S(1)} %copy-done.2, bf16[32,4,48,128]{3,2,1,0:T(8,128)(2,1)S(1)} %bitcast.33), custom_call_target="tpu_custom_call" | custom-call | flops 3221225472 | bytes 4194304 | tf_op jit(solution)/shard_map/combine/pallas_call | solution.py:461
  (3 shorter events, 0.0 us)
Async XLA Ops:
  2.4 16.5 %all-to-all-start = ((s32[32,1,2]{2,1,0:T(1,128)}), s32[32,1,2]{2,1,0:T(1,128)S(1)}, u32[]{:S(2)}, u32[]{:S(2)}) async-start(s32[32,1,2]{2,1,0:T(1,128)} %bitcast.37), calls=%async_computation | async-start | bytes 32768 | tf_op jit(solution)/shard_map/all_to_all | solution.py:482
  18.8 0.6 copy-start.10
  23.3 55.5 %all-to-all-start.1 = ((bf16[64,128,256]{2,1,0:T(8,128)(2,1)}), bf16[64,128,256]{2,1,0:T(8,128)(2,1)}, u32[]{:S(2)}, u32[]{:S(2)}) async-start(bf16[64,128,256]{2,1,0:T(8,128)(2,1)} %pick_blocks.1._), calls=%async_computation.1 | async-start | bytes 8388608 | tf_op jit(solution)/shard_map/all_to_all | solution.py:482
  28.4 4.9 %copy-start.11 = (s32[2048,1]{0,1:T(1,128)S(1)}, s32[2048,1]{0,1:T(1,128)}, u32[]{:S(2)}) copy-start(s32[2048,1]{0,1:T(1,128)} %param.21) | copy-start | bytes 24580
  32.0 55.2 %collective-permute-start = (bf16[1664,512]{1,0:T(8,128)(2,1)}, bf16[1664,512]{1,0:T(8,128)(2,1)S(1)}, u32[]{:S(2)}, u32[]{:S(2)}) collective-permute-start(bf16[1664,512]{1,0:T(8,128)(2,1)} %get-tuple-element.20.w0_ref), channel_id=1, source_target_pairs={{0,1},{1,0},{2,3},{3,2},{4,5},{5,4},{6,7},{7,6},{8,9},{9,8},{10,11... | collective-permute-start | bytes 5111816 | tf_op jit(solution)/shard_map/ppermute | solution.py:478
  35.7 82.0 %collective-permute-start.1 = (bf16[1664,512]{1,0:T(8,128)(2,1)}, bf16[1664,512]{1,0:T(8,128)(2,1)}, u32[]{:S(2)}, u32[]{:S(2)}) collective-permute-start(bf16[1664,512]{1,0:T(8,128)(2,1)} %get-tuple-element.24), channel_id=1, source_target_pairs={{0,2},{1,3},{2,0},{3,1},{4,6},{5,7},{6,4},{7,5},{8,10},{9,11},{10,... | collective-permute-start | bytes 5111816 | tf_op jit(solution)/shard_map/ppermute | solution.py:478
  38.1 79.5 %collective-permute-start.2 = (bf16[1664,512]{1,0:T(8,128)(2,1)}, bf16[1664,512]{1,0:T(8,128)(2,1)}, u32[]{:S(2)}, u32[]{:S(2)}) collective-permute-start(bf16[1664,512]{1,0:T(8,128)(2,1)} %get-tuple-element.24), channel_id=1, source_target_pairs={{0,3},{1,2},{2,1},{3,0},{4,7},{5,6},{6,5},{7,4},{8,11},{9,10},{10,... | collective-permute-start | bytes 5111816 | tf_op jit(solution)/shard_map/ppermute | solution.py:478
  78.8 29.5 %all-to-all-start.2 = ((bf16[32,48,512]{2,1,0:T(8,128)(2,1)}), bf16[32,48,512]{2,1,0:T(8,128)(2,1)S(1)}, u32[]{:S(2)}, u32[]{:S(2)}) async-start(bf16[32,48,512]{2,1,0:T(8,128)(2,1)} %place_rows.1), calls=%async_computation.2 | async-start | bytes 3145728 | tf_op jit(solution)/shard_map/all_to_all | solution.py:482
  87.2 1.2 copy-start.3
  108.2 10.7 %copy-start.4 = (bf16[32,48,512]{2,1,0:T(8,128)(2,1)}, bf16[32,48,512]{2,1,0:T(8,128)(2,1)S(1)}, u32[]{:S(2)}) copy-start(bf16[32,48,512]{2,1,0:T(8,128)(2,1)S(1)} %all-to-all-done.2.x_ref) | copy-start | bytes 4718596
  108.2 34.6 %all-to-all-start.3 = ((bf16[128,48,128]{2,1,0:T(8,128)(2,1)}), bf16[128,48,128]{2,1,0:T(8,128)(2,1)S(1)}, u32[]{:S(2)}, u32[]{:S(2)}) async-start(bf16[128,48,128]{2,1,0:T(8,128)(2,1)} %bitcast.36), calls=%async_computation.3 | async-start | bytes 3145728 | tf_op jit(solution)/shard_map/all_to_all | solution.py:482
  142.9 1.1 copy-start.5
  142.9 17.5 %collective-permute-start.3 = (bf16[2048,128]{1,0:T(8,128)(2,1)}, bf16[2048,128]{1,0:T(8,128)(2,1)S(1)}, u32[]{:S(2)}, u32[]{:S(2)}) collective-permute-start(bf16[2048,128]{1,0:T(8,128)(2,1)} %get-tuple-element.25.h0_ref), channel_id=1, source_target_pairs={{0,1},{1,0},{2,3},{3,2},{4,5},{5,4},{6,7},{7,6},{8,9},{9,8},{10,11... | collective-permute-start | bytes 1572872 | tf_op jit(solution)/shard_map/ppermute | solution.py:478
  143.2 17.2 %collective-permute-start.4 = (bf16[2048,128]{1,0:T(8,128)(2,1)}, bf16[2048,128]{1,0:T(8,128)(2,1)S(1)}, u32[]{:S(2)}, u32[]{:S(2)}) collective-permute-start(bf16[2048,128]{1,0:T(8,128)(2,1)} %get-tuple-element.25.h0_ref), channel_id=1, source_target_pairs={{0,3},{1,2},{2,1},{3,0},{4,7},{5,6},{6,5},{7,4},{8,11},{9,10},{10,... | collective-permute-start | bytes 1572872 | tf_op jit(solution)/shard_map/ppermute | solution.py:478
  160.3 6.8 %copy-start.6 = (bf16[2048,128]{1,0:T(8,128)(2,1)}, bf16[2048,128]{1,0:T(8,128)(2,1)S(1)}, u32[]{:S(2)}) copy-start(bf16[2048,128]{1,0:T(8,128)(2,1)S(1)} %collective-permute-done.3.h1_ref) | copy-start | bytes 1572868
  160.4 5.3 %copy-start.7 = (bf16[2048,128]{1,0:T(8,128)(2,1)}, bf16[2048,128]{1,0:T(8,128)(2,1)S(1)}, u32[]{:S(2)}) copy-start(bf16[2048,128]{1,0:T(8,128)(2,1)S(1)} %collective-permute-done.4.h3_ref) | copy-start | bytes 1572868
  160.4 35.4 %all-to-all-start.4 = ((bf16[128,48,128]{2,1,0:T(8,128)(2,1)}), bf16[128,48,128]{2,1,0:T(8,128)(2,1)S(1)}, u32[]{:S(2)}, u32[]{:S(2)}) async-start(bf16[128,48,128]{2,1,0:T(8,128)(2,1)} %bitcast.34), calls=%async_computation.4 | async-start | bytes 3145728 | tf_op jit(solution)/shard_map/all_to_all | solution.py:482
  165.6 23.9 %collective-permute-start.5 = (bf16[1024,128]{1,0:T(8,128)(2,1)S(1)}, bf16[1024,128]{1,0:T(8,128)(2,1)S(1)}, u32[]{:S(2)}, u32[]{:S(2)}) collective-permute-start(bf16[1024,128]{1,0:T(8,128)(2,1)S(1)} %slice.6), channel_id=1, source_target_pairs={{0,1},{1,0},{2,3},{3,2},{4,5},{5,4},{6,7},{7,6},{8,9},{9,8},{10,11... | collective-permute-start | bytes 786440 | tf_op jit(solution)/shard_map/ppermute | solution.py:478
  167.1 28.6 %copy-start = (s32[1,2048]{1,0:T(1,128)S(1)}, s32[1,2048]{1,0:T(1,128)}, u32[]{:S(2)}) copy-start(s32[1,2048]{1,0:T(1,128)} %get-tuple-element.35.lane_ref) | copy-start | bytes 24580
  167.1 28.6 %copy-start.1 = (s32[1,2048]{1,0:T(1,128)S(1)}, s32[1,2048]{1,0:T(1,128)}, u32[]{:S(2)}) copy-start(s32[1,2048]{1,0:T(1,128)} %get-tuple-element.36.spot_ref) | copy-start | bytes 24580
  167.1 23.6 %collective-permute-start.6 = (bf16[1024,128]{1,0:T(8,128)(2,1)S(1)}, bf16[1024,128]{1,0:T(8,128)(2,1)S(1)}, u32[]{:S(2)}, u32[]{:S(2)}) collective-permute-start(bf16[1024,128]{1,0:T(8,128)(2,1)S(1)} %slice.7), channel_id=1, source_target_pairs={{0,3},{1,2},{2,1},{3,0},{4,7},{5,6},{6,5},{7,4},{8,11},{9,10},{10,... | collective-permute-start | bytes 786440 | tf_op jit(solution)/shard_map/ppermute | solution.py:478
  189.6 1.2 copy-start.8
  190.8 0.7 copy-start.9
  195.8 1.2 copy-start.2

commit v7 on v6

--- a/solution.py
+++ b/solution.py
@@ -344,10 +344,15 @@
         for k in range(4):
             if t == 0:
                 large[k].wait()
-            left = jnp.dot(normed, quarters[k, :width, :], preferred_element_type=F32)
-            right = jnp.dot(normed, quarters[k, width : 2 * width, :], preferred_element_type=F32)
-            half = 0.5 * left
-            hidden = ((half + half * jnp.tanh(half)) * right).astype(BF16)
+            hidden = []
+            for c in range(0, width, 256):
+                left = jnp.dot(normed, quarters[k, :width, c : c + 256], preferred_element_type=F32)
+                right = jnp.dot(
+                    normed, quarters[k, width : 2 * width, c : c + 256], preferred_element_type=F32
+                )
+                half = 0.5 * left
+                hidden.append(((half + half * jnp.tanh(half)) * right).astype(BF16))
+            hidden = jnp.concatenate(hidden, axis=1)
             term = jnp.dot(hidden, quarters[k, 2 * width :, :], preferred_element_type=F32)
             result = term if result is None else result + term
         result = (gate * result).astype(BF16).reshape(step, cap, width)
@@ -381,46 +386,48 @@
 
 
 def columns_kernel(
-    me_ref, h0_ref, h1_ref, h3_ref, top_ref, bottom_ref, w0_ref, w1_ref, w2_ref, w3_ref, x_ref, attn_ref, mixed_ref
+    me_ref, h0_ref, h1_ref, h3_ref, w0_ref, w1_ref, w2_ref, w3_ref, x_ref, part_ref, kept_ref, last_ref, sem
 ):
     columns = pl.ds(pl.multiple_of(me_ref[0] * LANES, LANES), LANES)
-    half = top_ref.shape[0]
-    for start, h2_ref in ((0, top_ref), (half, bottom_ref)):
-        rows = slice(start, start + half)
-        pieces = [h0_ref[rows, :], h1_ref[rows, :], h2_ref[...], h3_ref[rows, :]]
-        weights = [w[:, columns] for w in (w0_ref, w1_ref, w2_ref, w3_ref)]
-        total = jnp.dot(
-            jnp.concatenate(pieces, axis=1), jnp.concatenate(weights, axis=0), preferred_element_type=F32
-        )
-        attn_ref[rows, :] = total.astype(BF16)
-        mixed_ref[rows, :] = x_ref[rows, columns].astype(F32) + total
-
-
-def attention_columns(me, heads, by_one, by_three, relayed, weights, x):
+    copy = pltpu.make_async_copy(x_ref.at[:, columns], kept_ref, sem)
+    copy.start()
+    pieces = [h[...] for h in (h0_ref, h1_ref, h3_ref)]
+    weights = [w[:, columns] for w in (w0_ref, w1_ref, w3_ref)]
+    part_ref[...] = jnp.dot(
+        jnp.concatenate(pieces, axis=1), jnp.concatenate(weights, axis=0), preferred_element_type=F32
+    )
+    last_ref[...] = w2_ref[:, columns]
+    copy.wait()
+
+
+def attention_columns(me, heads, by_one, by_three, weights, x):
     rows, width = x.shape
     last = weights[0].shape[0] // LANES - 1
     out = pl.BlockSpec((rows, LANES), lambda i: (0, 0))
-    half = pl.BlockSpec((rows // 2, LANES), lambda i: (0, 0))
     return pl.pallas_call(
         columns_kernel,
         grid=(1,),
         in_specs=[SMEM]
         + [out] * 3
-        + [half] * 2
         + [pl.BlockSpec((LANES, width), lambda i: (last, 0))] * 4
-        + [pl.BlockSpec((rows, width), lambda i: (0, 0))],
-        out_specs=[out, out],
+        + [ANY],
+        out_specs=[out, out, pl.BlockSpec((LANES, LANES), lambda i: (0, 0))],
         out_shape=[
+            jax.ShapeDtypeStruct((rows, LANES), F32),
             jax.ShapeDtypeStruct((rows, LANES), BF16),
-            jax.ShapeDtypeStruct((rows, LANES), F32),
-        ],
+            jax.ShapeDtypeStruct((LANES, LANES), BF16),
+        ],
+        scratch_shapes=[pltpu.SemaphoreType.DMA],
         compiler_params=params(60),
         cost_estimate=cost(2 * rows * width * LANES, 8 * 2**20),
         name="attention_columns",
-    )(me, heads, by_one, by_three, *relayed, *weights, x)
-
-
-def combine_kernel(spot_ref, lane_ref, mixed_hbm, back_ref, out_ref, slots, mixed_ref, sems):
+    )(me, heads, by_one, by_three, *weights, x)
+
+
+def combine_kernel(
+    spot_ref, lane_ref, last_ref, part_hbm, kept_hbm, top_hbm, bottom_hbm, back_ref, attn_ref, out_ref,
+    slots, part_ref, kept_ref, h2_ref, sems
+):
     dests, cap, width = slots.shape
     rows = out_ref.shape[0]
     copies = [
@@ -429,49 +436,59 @@
         )
         for m in range(4)
     ]
-    copies.append(pltpu.make_async_copy(mixed_hbm, mixed_ref, sems.at[4]))
+    half = rows // 2
+    for source, target in (
+        (part_hbm, part_ref),
+        (kept_hbm, kept_ref),
+        (top_hbm, h2_ref.at[pl.ds(0, half)]),
+        (bottom_hbm, h2_ref.at[pl.ds(half, half)]),
+    ):
+        copies.append(pltpu.make_async_copy(source, target, sems.at[len(copies)]))
     for copy in copies:
         copy.start()
-    for copy in copies:
-        copy.wait()
     tile = 256
     names = lax.broadcasted_iota(jnp.int32, (ROWS_BLK, dests * cap), 1).astype(F32)
 
-    @pl.loop(0, rows // tile)
-    def _(i):
-        pieces = [
-            pl.ds(pl.multiple_of(i * tile + t * ROWS_BLK, ROWS_BLK), ROWS_BLK) for t in range(tile // ROWS_BLK)
-        ]
+    for i in range(rows // tile):
+        pieces = [pl.ds(i * tile + t * ROWS_BLK, ROWS_BLK) for t in range(tile // ROWS_BLK)]
         hot = jnp.concatenate(
             [jnp.where(names == as_column(spot_ref[:, p]), 1.0, 0.0).astype(BF16) for p in pieces], axis=0
         )
+        if i == 0:
+            for copy in copies:
+                copy.wait()
         found = jnp.dot(hot, slots[...].reshape(dests * cap, width), preferred_element_type=F32)
         for t, p in enumerate(pieces):
             lane = as_column(lane_ref[:, p])
-            total = mixed_ref[p, :]
+            total = part_ref[p, :] + jnp.dot(h2_ref[p, :], last_ref[...], preferred_element_type=F32)
+            attn_ref[p, :] = total.astype(BF16)
+            total = kept_ref[p, :].astype(F32) + total
             for m in range(4):
                 part = found[t * ROWS_BLK : (t + 1) * ROWS_BLK, m * LANES : (m + 1) * LANES]
                 total = total + jnp.where(lane == m, part, 0.0)
             out_ref[p, :] = total.astype(BF16)
 
 
-def combine(spot_row, lane_row, back, mixed):
-    rows = mixed.shape[0]
+def combine(spot_row, lane_row, last, part, kept, relayed, back):
+    rows = part.shape[0]
     slots = back.shape[0] * back.shape[2]
+    out = jax.ShapeDtypeStruct((rows, LANES), BF16)
     return pl.pallas_call(
         combine_kernel,
-        in_specs=[VMEM] * 2 + [HBM] * 2,
-        out_specs=VMEM,
-        out_shape=jax.ShapeDtypeStruct((rows, LANES), BF16),
+        in_specs=[VMEM] * 3 + [HBM] * 5,
+        out_specs=[VMEM, VMEM],
+        out_shape=[out, out],
         scratch_shapes=[
             pltpu.VMEM((back.shape[0], back.shape[2], 4 * LANES), BF16),
             pltpu.VMEM((rows, LANES), F32),
-            pltpu.SemaphoreType.DMA((5,)),
-        ],
-        compiler_params=params(24),
+            pltpu.VMEM((rows, LANES), BF16),
+            pltpu.VMEM((rows, LANES), BF16),
+            pltpu.SemaphoreType.DMA((8,)),
+        ],
+        compiler_params=params(60),
         cost_estimate=cost(2 * rows * slots * 4 * LANES, 4 * 2**20),
         name="combine",
-    )(spot_row, lane_row, mixed, back)
+    )(spot_row, lane_row, last, part, kept, *relayed, back)
 
 
 def swap(array, change):
@@ -547,11 +564,13 @@
     produced, by_one, by_three = lax.optimization_barrier((produced, by_one, by_three))
     middle = rows // 2
     relayed = [swap(by_three[:middle], 1), swap(by_one[middle:], 3)]
-    attn_out, mixed = attention_columns(
-        me_ref, heads, by_one, by_three, relayed, weights, node_features
+    part, kept_columns, last = attention_columns(
+        me_ref, heads, by_one, by_three, weights, node_features
     )
     back = exchange(produced.reshape(parts * 4, half_cap, LANES), ("graph", "mp"))
-    layer_out = combine(spot_row, lane_row, back.reshape(parts, 4, half_cap, LANES), mixed)
+    attn_out, layer_out = combine(
+        spot_row, lane_row, last, part, kept_columns, relayed, back.reshape(parts, 4, half_cap, LANES)
+    )
     return (attn_out, layer_out)
 
 

time: 204 us -> 202 us (level)
  waiting for transfers between devices: 81.3 us -> 74.7 us
  local copies, waits for them, and re-layouts: 4.3 us -> 6.61 us
    ppermute x7, waiting for transfers between devices: 21.8 us -> 15.9 us  [swap(): return lax.ppermute(array, 'mp', [(i, i ^ change) for i in range(4)])]
    unnamed x24 -> x16, local copies, waits for them, and re-layouts: 4.27 us -> 4.68 us
  transfers between devices with their start and end apart: 12 -> 12, of which waited for: 5 -> 6; matrix products, arithmetic and copies ran while one was open for 2% -> 3% of each run, Pallas kernels for 28% -> 28%
where the time goes in v7:
time: 202 us; the launch traced here: 201 us
  waiting for transfers between devices  74.7 us (37%)
  Pallas kernels  69.5 us (34%)
  starting transfers between devices  45.2 us (22%)
  local copies, waits for them, and re-layouts  6.61 us (3%)
    all_to_all x5, waiting for transfers between devices, exchange(): return lax.all_to_all(array, axes, split_axis=0, concat_axis=0, tiled=True)  58.8 us
    all_to_all x5, starting transfers between devices, exchange(): return lax.all_to_all(array, axes, split_axis=0, concat_axis=0, tiled=True)  37.1 us
    pallas_call x1, Pallas kernels, attention(): pl.pallas_call(attention_kernel, in_specs=[SMEM, SMEM, VMEM, VMEM, VMEM,...  19.8 us
    ppermute x7, waiting for transfers between devices, swap(): return lax.ppermute(array, 'mp', [(i, i ^ change) for i in range(4)])  15.9 us
    pallas_call x1, Pallas kernels, experts(): pl.pallas_call(experts_kernel, in_specs=[SMEM, VMEM, VMEM, HBM, HBM] + [A...  15.6 us
    ppermute x7, starting transfers between devices, swap(): return lax.ppermute(array, 'mp', [(i, i ^ change) for i in range(4)])  8.16 us
    pallas_call x1, Pallas kernels, combine(): pl.pallas_call(combine_kernel, in_specs=[VMEM] * 3 + [HBM] * 5, out_specs...  8.01 us
    pallas_call x1, Pallas kernels, place_rows(): pl.pallas_call(place_kernel, in_specs=[VMEM, VMEM], out_specs=VMEM, out_s...  7.39 us
  transfers between devices with their start and end apart: 12, of which 6 were waited for; matrix products, arithmetic and copies ran while one was open for 3% of the time, Pallas kernels for 28%

profile of v7, /device:TPU:1, one launch (start us, length us, event | category | flops | bytes accessed | tf_op | source)
XLA Modules:
  0.0 200.7 jit_solution(2262499257336585710)
XLA Ops:
  0.6 1.7 make_requests.1.asked_ref
  2.4 9.6 %all-to-all-start = ((s32[32,1,2]{2,1,0:T(1,128)}), s32[32,1,2]{2,1,0:T(1,128)S(1)}, u32[]{:S(2)}, u32[]{:S(2)}) async-start(s32[32,1,2]{2,1,0:T(1,128)} %bitcast.37), calls=%async_computation | async-start | bytes 32768 | tf_op jit(solution)/shard_map/all_to_all | solution.py:499
  12.0 4.3 %qkv.1 = (bf16[2048,128]{1,0:T(8,128)(2,1)}, bf16[16,128,256]{2,1,0:T(8,128)(2,1)}) custom-call(bf16[2048,512]{1,0:T(8,128)(2,1)} %x_ref.5, bf16[3,512,128]{2,1,0:T(8,128)(2,1)} %w_ref.1, f32[2]{0:T(128)} %scale_ref.1), custom_call_target="tpu_custom_call" | custom-call | flops 805306368 | bytes 3670016 | tf_op jit(solution)/shard_map/qkv/pallas_call | solution.py:60
  16.3 2.6 %all-to-all-done.wanted_ref = s32[32,1,2]{2,1,0:T(1,128)S(1)} async-done(((s32[32,1,2]{2,1,0:T(1,128)}), s32[32,1,2]{2,1,0:T(1,128)S(1)}, u32[]{:S(2)}, u32[]{:S(2)}) %all-to-all-start) | async-done | bytes 288 | tf_op jit(solution)/shard_map/all_to_all | solution.py:499
  18.9 0.0 copy-start.4
  18.9 0.6 copy-done.4
  19.5 3.8 %pick_blocks.1._ = bf16[64,128,256]{2,1,0:T(8,128)(2,1)} custom-call(s32[32,1,2]{2,1,0:T(1,128)} %copy-done.4, bf16[16,128,256]{2,1,0:T(8,128)(2,1)} %get-tuple-element.20.kv_ref), custom_call_target="tpu_custom_call" | custom-call | bytes 8388608 | tf_op jit(solution)/shard_map/pick_blocks/pallas_call | solution.py:156
  23.4 5.1 %all-to-all-start.1 = ((bf16[64,128,256]{2,1,0:T(8,128)(2,1)}), bf16[64,128,256]{2,1,0:T(8,128)(2,1)}, u32[]{:S(2)}, u32[]{:S(2)}) async-start(bf16[64,128,256]{2,1,0:T(8,128)(2,1)} %pick_blocks.1._), calls=%async_computation.1 | async-start | bytes 8388608 | tf_op jit(solution)/shard_map/all_to_all | solution.py:499
  28.5 0.0 copy-start.5
  28.5 3.7 %split_weights.1 = (bf16[1664,512]{1,0:T(8,128)(2,1)}, bf16[1664,512]{1,0:T(8,128)(2,1)}) custom-call(s32[1]{0:T(128)} %bitcast.3.me_ref, bf16[2,512,512]{2,1,0:T(8,128)(2,1)} %gate_ref.1, bf16[2,512,512]{2,1,0:T(8,128)(2,1)} %up_ref.1, bf16[2,512,512]{2,1,0:T(8,128)(2,1)} %down_ref.1, bf16[128,512]{1,0:T(8,128)(2,1)} %out_w_ref.1, ...), custom_call_target="tpu_custom_call" | custom-call | bytes 6815744 | tf_op jit(solution)/shard_map/split_weights/pallas_call | solution.py:127
  32.2 1.3 collective-permute-start
  33.5 0.0 copy-done.5
  33.5 1.7 fusion.2
  35.2 0.7 compare_select_fusion
  35.9 2.4 %collective-permute-start.1 = (bf16[1664,512]{1,0:T(8,128)(2,1)}, bf16[1664,512]{1,0:T(8,128)(2,1)S(1)}, u32[]{:S(2)}, u32[]{:S(2)}) collective-permute-start(bf16[1664,512]{1,0:T(8,128)(2,1)} %get-tuple-element.25), channel_id=1, source_target_pairs={{0,2},{1,3},{2,0},{3,1},{4,6},{5,7},{6,4},{7,5},{8,10},{9,11},{10,... | collective-permute-start | bytes 5111816 | tf_op jit(solution)/shard_map/ppermute | solution.py:495
  38.3 0.2 collective-permute-start.2
  38.5 7.4 %place_rows.1 = bf16[32,48,512]{2,1,0:T(8,128)(2,1)} custom-call(s32[1,2048]{1,0:T(1,128)} %get-tuple-element.36.spot_ref, bf16[2048,512]{1,0:T(8,128)(2,1)} %x_ref.5), custom_call_target="tpu_custom_call" | custom-call | flops 3221225472 | bytes 4194304 | tf_op jit(solution)/shard_map/place_rows/pallas_call | solution.py:271
  45.9 32.9 %all-to-all-done.1.halo_ref = bf16[64,128,256]{2,1,0:T(8,128)(2,1)} async-done(((bf16[64,128,256]{2,1,0:T(8,128)(2,1)}), bf16[64,128,256]{2,1,0:T(8,128)(2,1)}, u32[]{:S(2)}, u32[]{:S(2)}) %all-to-all-start.1) | async-done | bytes 4194336 | tf_op jit(solution)/shard_map/all_to_all | solution.py:499
  78.8 7.8 %all-to-all-start.2 = ((bf16[32,48,512]{2,1,0:T(8,128)(2,1)}), bf16[32,48,512]{2,1,0:T(8,128)(2,1)}, u32[]{:S(2)}, u32[]{:S(2)}) async-start(bf16[32,48,512]{2,1,0:T(8,128)(2,1)} %place_rows.1), calls=%async_computation.2 | async-start | bytes 3145728 | tf_op jit(solution)/shard_map/all_to_all | solution.py:499
  86.7 1.3 bitcast_convert_fusion.route_ref
  88.0 0.0 collective-permute-done.rest_0_.w1_ref
  88.0 0.0 copy-start
  88.0 1.2 copy-done
  89.2 19.8 %attention.1 = (bf16[2048,128]{1,0:T(8,128)(2,1)}, bf16[32,4,48,128]{3,2,1,0:T(8,128)(2,1)}) custom-call(s32[16,12]{1,0:T(8,128)} %near_ref.3, s32[32,2]{1,0:T(8,128)} %make_requests.1.asked_ref, bf16[2048,128]{1,0:T(8,128)(2,1)} %get-tuple-element.19.q_ref, bf16[16,128,256]{2,1,0:T(8,128)(2,1)} %get-tuple-element.20.kv_ref, ...), custom_call_target="tpu_custom_call" | custom-call | flops 12000000000 | bytes 8388608 | tf_op jit(solution)/shard_map/attention/pallas_call | solution.py:235
  109.0 0.0 all-to-all-done.2.x_ref
  109.0 9.4 %all-to-all-start.3 = ((bf16[128,48,128]{2,1,0:T(8,128)(2,1)}), bf16[128,48,128]{2,1,0:T(8,128)(2,1)S(1)}, u32[]{:S(2)}, u32[]{:S(2)}) async-start(bf16[128,48,128]{2,1,0:T(8,128)(2,1)} %bitcast.36), calls=%async_computation.3 | async-start | bytes 3145728 | tf_op jit(solution)/shard_map/all_to_all | solution.py:499
  118.4 0.0 collective-permute-done.1.rest_1_.w2_ref
  118.4 0.0 copy-start.1
  118.4 0.0 collective-permute-done.2.rest_2_.w3_ref
  118.4 1.2 copy-done.1
  119.6 1.3 hold_route.1.route_ref
  120.9 22.7 %all-to-all-done.3 = bf16[128,48,128]{2,1,0:T(8,128)(2,1)S(1)} async-done(((bf16[128,48,128]{2,1,0:T(8,128)(2,1)}), bf16[128,48,128]{2,1,0:T(8,128)(2,1)S(1)}, u32[]{:S(2)}, u32[]{:S(2)}) %all-to-all-start.3) | async-done | bytes 1572896 | tf_op jit(solution)/shard_map/all_to_all | solution.py:499
  143.6 0.0 copy-start.3
  143.6 0.3 collective-permute-start.3
  143.9 0.4 collective-permute-start.4
  144.3 0.5 copy-done.3
  144.8 15.6 %experts.1 = bf16[32,4,48,128]{3,2,1,0:T(8,128)(2,1)} custom-call(s32[1]{0:T(128)} %bitcast.3.me_ref, f32[1,512]{1,0:T(1,128)} %bitcast.40, f32[1,512]{1,0:T(1,128)} %hold_route.1.route_ref, bf16[32,4,48,128]{3,2,1,0:T(8,128)(2,1)} %bitcast.35, bf16[32,48,512]{2,1,0:T(8,128)(2,1)} %all-to-all-done.2.x_ref, bf16[1664,512]{1,0:T(8,128)(2,1)} %get-tuple-element.21.w0_ref, ...), custom_call_target="tpu_custom_call" | custom-call | flops 10468982784 | bytes 12582912 | tf_op jit(solution)/shard_map/experts/pallas_call | solution.py:369
  160.4 0.0 collective-permute-done.3.h1_ref
  160.5 0.0 collective-permute-done.4.h3_ref
  160.5 5.2 %all-to-all-start.4 = ((bf16[128,48,128]{2,1,0:T(8,128)(2,1)}), bf16[128,48,128]{2,1,0:T(8,128)(2,1)S(1)}, u32[]{:S(2)}, u32[]{:S(2)}) async-start(bf16[128,48,128]{2,1,0:T(8,128)(2,1)} %bitcast.34), calls=%async_computation.4 | async-start | bytes 3145728 | tf_op jit(solution)/shard_map/all_to_all | solution.py:499
  165.7 1.0 slice.6
  166.6 1.5 collective-permute-start.5
  168.1 1.0 slice.7
  169.1 2.1 %collective-permute-start.6 = (bf16[1024,128]{1,0:T(8,128)(2,1)S(1)}, bf16[1024,128]{1,0:T(8,128)(2,1)S(1)}, u32[]{:S(2)}, u32[]{:S(2)}) collective-permute-start(bf16[1024,128]{1,0:T(8,128)(2,1)S(1)} %slice.7), channel_id=1, source_target_pairs={{0,3},{1,2},{2,1},{3,0},{4,7},{5,6},{6,5},{7,4},{8,11},{9,10},{10,... | collective-permute-start | bytes 786440 | tf_op jit(solution)/shard_map/ppermute | solution.py:495
  171.2 3.8 %attention_columns.1 = (f32[2048,128]{1,0:T(8,128)}, bf16[2048,128]{1,0:T(8,128)(2,1)}, bf16[128,128]{1,0:T(8,128)(2,1)}) custom-call(s32[1]{0:T(128)} %bitcast.3.me_ref, bf16[2048,128]{1,0:T(8,128)(2,1)} %get-tuple-element.26.h0_ref, bf16[2048,128]{1,0:T(8,128)(2,1)} %collective-permute-done.3.h1_ref, bf16[2048,128]{1,0:T(8,128)(2,1)} %collective-permute-done.4.h3_ref, ...), custom_call_target="tpu_custom_call" | custom-call | flops 268435456 | bytes 8388608 | tf_op jit(solution)/shard_map/attention_columns/pallas_call | solution.py:407
  175.0 14.7 %collective-permute-done.5.top_hbm = bf16[1024,128]{1,0:T(8,128)(2,1)S(1)} collective-permute-done((bf16[1024,128]{1,0:T(8,128)(2,1)S(1)}, bf16[1024,128]{1,0:T(8,128)(2,1)S(1)}, u32[]{:S(2)}, u32[]{:S(2)}) %collective-permute-start.5) | collective-permute-done | bytes 262176 | tf_op jit(solution)/shard_map/ppermute | solution.py:495
  189.6 0.0 copy-start.6
  189.6 1.2 collective-permute-done.6.bottom_hbm
  190.8 0.0 copy-start.7
  190.8 0.5 all-to-all-done.4
  191.3 0.0 copy-start.2
  191.3 0.0 copy-done.6
  191.3 0.2 copy-done.7
  191.6 0.9 copy-done.2
  192.5 8.0 %combine.1 = (bf16[2048,128]{1,0:T(8,128)(2,1)}, bf16[2048,128]{1,0:T(8,128)(2,1)}) custom-call(s32[1,2048]{1,0:T(1,128)} %get-tuple-element.38.spot_ref, s32[1,2048]{1,0:T(1,128)} %get-tuple-element.37.lane_ref, bf16[128,128]{1,0:T(8,128)(2,1)} %get-tuple-element.32.last_ref, f32[2048,128]{1,0:T(8,128)} %get-tuple-element.33.part_hbm, ...), custom_call_target="tpu_custom_call" | custom-call | flops 3221225472 | bytes 4194304 | tf_op jit(solution)/shard_map/combine/pallas_call | solution.py:476
  (1 shorter events, 0.0 us)
Async XLA Ops:
  2.4 16.5 %all-to-all-start = ((s32[32,1,2]{2,1,0:T(1,128)}), s32[32,1,2]{2,1,0:T(1,128)S(1)}, u32[]{:S(2)}, u32[]{:S(2)}) async-start(s32[32,1,2]{2,1,0:T(1,128)} %bitcast.37), calls=%async_computation | async-start | bytes 32768 | tf_op jit(solution)/shard_map/all_to_all | solution.py:499
  18.9 0.6 copy-start.4
  23.4 55.5 %all-to-all-start.1 = ((bf16[64,128,256]{2,1,0:T(8,128)(2,1)}), bf16[64,128,256]{2,1,0:T(8,128)(2,1)}, u32[]{:S(2)}, u32[]{:S(2)}) async-start(bf16[64,128,256]{2,1,0:T(8,128)(2,1)} %pick_blocks.1._), calls=%async_computation.1 | async-start | bytes 8388608 | tf_op jit(solution)/shard_map/all_to_all | solution.py:499
  28.5 5.0 %copy-start.5 = (s32[2048,1]{0,1:T(1,128)S(1)}, s32[2048,1]{0,1:T(1,128)}, u32[]{:S(2)}) copy-start(s32[2048,1]{0,1:T(1,128)} %param.21) | copy-start | bytes 24580
  32.2 55.8 %collective-permute-start = (bf16[1664,512]{1,0:T(8,128)(2,1)}, bf16[1664,512]{1,0:T(8,128)(2,1)S(1)}, u32[]{:S(2)}, u32[]{:S(2)}) collective-permute-start(bf16[1664,512]{1,0:T(8,128)(2,1)} %get-tuple-element.21.w0_ref), channel_id=1, source_target_pairs={{0,1},{1,0},{2,3},{3,2},{4,5},{5,4},{6,7},{7,6},{8,9},{9,8},{10,11... | collective-permute-start | bytes 5111816 | tf_op jit(solution)/shard_map/ppermute | solution.py:495
  35.9 82.5 %collective-permute-start.1 = (bf16[1664,512]{1,0:T(8,128)(2,1)}, bf16[1664,512]{1,0:T(8,128)(2,1)S(1)}, u32[]{:S(2)}, u32[]{:S(2)}) collective-permute-start(bf16[1664,512]{1,0:T(8,128)(2,1)} %get-tuple-element.25), channel_id=1, source_target_pairs={{0,2},{1,3},{2,0},{3,1},{4,6},{5,7},{6,4},{7,5},{8,10},{9,11},{10,... | collective-permute-start | bytes 5111816 | tf_op jit(solution)/shard_map/ppermute | solution.py:495
  38.3 80.1 %collective-permute-start.2 = (bf16[1664,512]{1,0:T(8,128)(2,1)}, bf16[1664,512]{1,0:T(8,128)(2,1)}, u32[]{:S(2)}, u32[]{:S(2)}) collective-permute-start(bf16[1664,512]{1,0:T(8,128)(2,1)} %get-tuple-element.25), channel_id=1, source_target_pairs={{0,3},{1,2},{2,1},{3,0},{4,7},{5,6},{6,5},{7,4},{8,11},{9,10},{10,... | collective-permute-start | bytes 5111816 | tf_op jit(solution)/shard_map/ppermute | solution.py:495
  78.8 30.2 %all-to-all-start.2 = ((bf16[32,48,512]{2,1,0:T(8,128)(2,1)}), bf16[32,48,512]{2,1,0:T(8,128)(2,1)}, u32[]{:S(2)}, u32[]{:S(2)}) async-start(bf16[32,48,512]{2,1,0:T(8,128)(2,1)} %place_rows.1), calls=%async_computation.2 | async-start | bytes 3145728 | tf_op jit(solution)/shard_map/all_to_all | solution.py:499
  88.0 1.2 copy-start
  109.0 34.6 %all-to-all-start.3 = ((bf16[128,48,128]{2,1,0:T(8,128)(2,1)}), bf16[128,48,128]{2,1,0:T(8,128)(2,1)S(1)}, u32[]{:S(2)}, u32[]{:S(2)}) async-start(bf16[128,48,128]{2,1,0:T(8,128)(2,1)} %bitcast.36), calls=%async_computation.3 | async-start | bytes 3145728 | tf_op jit(solution)/shard_map/all_to_all | solution.py:499
  118.4 1.2 copy-start.1
  143.6 1.2 copy-start.3
  143.6 16.8 %collective-permute-start.3 = (bf16[2048,128]{1,0:T(8,128)(2,1)}, bf16[2048,128]{1,0:T(8,128)(2,1)}, u32[]{:S(2)}, u32[]{:S(2)}) collective-permute-start(bf16[2048,128]{1,0:T(8,128)(2,1)} %get-tuple-element.26.h0_ref), channel_id=1, source_target_pairs={{0,1},{1,0},{2,3},{3,2},{4,5},{5,4},{6,7},{7,6},{8,9},{9,8},{10,11... | collective-permute-start | bytes 1572872 | tf_op jit(solution)/shard_map/ppermute | solution.py:495
  143.9 16.5 %collective-permute-start.4 = (bf16[2048,128]{1,0:T(8,128)(2,1)}, bf16[2048,128]{1,0:T(8,128)(2,1)}, u32[]{:S(2)}, u32[]{:S(2)}) collective-permute-start(bf16[2048,128]{1,0:T(8,128)(2,1)} %get-tuple-element.26.h0_ref), channel_id=1, source_target_pairs={{0,3},{1,2},{2,1},{3,0},{4,7},{5,6},{6,5},{7,4},{8,11},{9,10},{10,... | collective-permute-start | bytes 1572872 | tf_op jit(solution)/shard_map/ppermute | solution.py:495
  160.5 30.9 %all-to-all-start.4 = ((bf16[128,48,128]{2,1,0:T(8,128)(2,1)}), bf16[128,48,128]{2,1,0:T(8,128)(2,1)S(1)}, u32[]{:S(2)}, u32[]{:S(2)}) async-start(bf16[128,48,128]{2,1,0:T(8,128)(2,1)} %bitcast.34), calls=%async_computation.4 | async-start | bytes 3145728 | tf_op jit(solution)/shard_map/all_to_all | solution.py:499
  166.6 23.0 %collective-permute-start.5 = (bf16[1024,128]{1,0:T(8,128)(2,1)S(1)}, bf16[1024,128]{1,0:T(8,128)(2,1)S(1)}, u32[]{:S(2)}, u32[]{:S(2)}) collective-permute-start(bf16[1024,128]{1,0:T(8,128)(2,1)S(1)} %slice.6), channel_id=1, source_target_pairs={{0,1},{1,0},{2,3},{3,2},{4,5},{5,4},{6,7},{7,6},{8,9},{9,8},{10,11... | collective-permute-start | bytes 786440 | tf_op jit(solution)/shard_map/ppermute | solution.py:495
  169.1 21.8 %collective-permute-start.6 = (bf16[1024,128]{1,0:T(8,128)(2,1)S(1)}, bf16[1024,128]{1,0:T(8,128)(2,1)S(1)}, u32[]{:S(2)}, u32[]{:S(2)}) collective-permute-start(bf16[1024,128]{1,0:T(8,128)(2,1)S(1)} %slice.7), channel_id=1, source_target_pairs={{0,3},{1,2},{2,1},{3,0},{4,7},{5,6},{6,5},{7,4},{8,11},{9,10},{10,... | collective-permute-start | bytes 786440 | tf_op jit(solution)/shard_map/ppermute | solution.py:495
  189.6 1.7 copy-start.6
  190.8 0.7 copy-start.7
  191.3 1.2 copy-start.2

commit v8 on v7

--- a/solution.py
+++ b/solution.py
@@ -425,8 +425,8 @@
 
 
 def combine_kernel(
-    spot_ref, lane_ref, last_ref, part_hbm, kept_hbm, top_hbm, bottom_hbm, back_ref, attn_ref, out_ref,
-    slots, part_ref, kept_ref, h2_ref, sems
+    spot_ref, lane_ref, last_ref, part_hbm, kept_hbm, top_hbm, bottom_hbm, back_ref, attn_hbm, out_hbm,
+    slots, part_ref, kept_ref, h2_ref, attn_ref, out_ref, sems
 ):
     dests, cap, width = slots.shape
     rows = out_ref.shape[0]
@@ -447,6 +447,7 @@
     for copy in copies:
         copy.start()
     tile = 256
+    outs = []
     names = lax.broadcasted_iota(jnp.int32, (ROWS_BLK, dests * cap), 1).astype(F32)
 
     for i in range(rows // tile):
@@ -455,18 +456,29 @@
             [jnp.where(names == as_column(spot_ref[:, p]), 1.0, 0.0).astype(BF16) for p in pieces], axis=0
         )
         if i == 0:
-            for copy in copies:
+            for copy in copies[:4]:
                 copy.wait()
         found = jnp.dot(hot, slots[...].reshape(dests * cap, width), preferred_element_type=F32)
+        if i == 0:
+            for copy in copies[4:]:
+                copy.wait()
+        whole = slice(i * tile, (i + 1) * tile)
+        added = jnp.dot(h2_ref[whole, :], last_ref[...], preferred_element_type=F32)
         for t, p in enumerate(pieces):
             lane = as_column(lane_ref[:, p])
-            total = part_ref[p, :] + jnp.dot(h2_ref[p, :], last_ref[...], preferred_element_type=F32)
+            total = part_ref[p, :] + added[t * ROWS_BLK : (t + 1) * ROWS_BLK]
             attn_ref[p, :] = total.astype(BF16)
             total = kept_ref[p, :].astype(F32) + total
             for m in range(4):
                 part = found[t * ROWS_BLK : (t + 1) * ROWS_BLK, m * LANES : (m + 1) * LANES]
                 total = total + jnp.where(lane == m, part, 0.0)
             out_ref[p, :] = total.astype(BF16)
+        for source, target in ((attn_ref, attn_hbm), (out_ref, out_hbm)):
+            here = pl.ds(i * tile, tile)
+            outs.append(pltpu.make_async_copy(source.at[here], target.at[here], sems.at[8 + len(outs)]))
+            outs[-1].start()
+    for copy in outs:
+        copy.wait()
 
 
 def combine(spot_row, lane_row, last, part, kept, relayed, back):
@@ -476,14 +488,16 @@
     return pl.pallas_call(
         combine_kernel,
         in_specs=[VMEM] * 3 + [HBM] * 5,
-        out_specs=[VMEM, VMEM],
+        out_specs=[HBM, HBM],
         out_shape=[out, out],
         scratch_shapes=[
             pltpu.VMEM((back.shape[0], back.shape[2], 4 * LANES), BF16),
             pltpu.VMEM((rows, LANES), F32),
             pltpu.VMEM((rows, LANES), BF16),
             pltpu.VMEM((rows, LANES), BF16),
-            pltpu.SemaphoreType.DMA((8,)),
+            pltpu.VMEM((rows, LANES), BF16),
+            pltpu.VMEM((rows, LANES), BF16),
+            pltpu.SemaphoreType.DMA((8 + 2 * (rows // 256),)),
         ],
         compiler_params=params(60),
         cost_estimate=cost(2 * rows * slots * 4 * LANES, 4 * 2**20),

time: 202 us -> 201 us (level)
  no operation moved by 1% of the time
where the time goes in v8:
time: 201 us; the launch traced here: 200 us
  waiting for transfers between devices  74.7 us (37%)
  Pallas kernels  68.6 us (34%)
  starting transfers between devices  45.2 us (22%)
  local copies, waits for them, and re-layouts  6.61 us (3%)
    all_to_all x5, waiting for transfers between devices, exchange(): return lax.all_to_all(array, axes, split_axis=0, concat_axis=0, tiled=True)  58.8 us
    all_to_all x5, starting transfers between devices, exchange(): return lax.all_to_all(array, axes, split_axis=0, concat_axis=0, tiled=True)  37.1 us
    pallas_call x1, Pallas kernels, attention(): pl.pallas_call(attention_kernel, in_specs=[SMEM, SMEM, VMEM, VMEM, VMEM,...  19.8 us
    ppermute x7, waiting for transfers between devices, swap(): return lax.ppermute(array, 'mp', [(i, i ^ change) for i in range(4)])  15.9 us
    pallas_call x1, Pallas kernels, experts(): pl.pallas_call(experts_kernel, in_specs=[SMEM, VMEM, VMEM, HBM, HBM] + [A...  15.6 us
    ppermute x7, starting transfers between devices, swap(): return lax.ppermute(array, 'mp', [(i, i ^ change) for i in range(4)])  8.16 us
    pallas_call x1, Pallas kernels, place_rows(): pl.pallas_call(place_kernel, in_specs=[VMEM, VMEM], out_specs=VMEM, out_s...  7.39 us
    pallas_call x1, Pallas kernels, combine(): pl.pallas_call(combine_kernel, in_specs=[VMEM] * 3 + [HBM] * 5, out_specs...  7.1 us
  transfers between devices with their start and end apart: 12, of which 6 were waited for; matrix products, arithmetic and copies ran while one was open for 3% of the time, Pallas kernels for 28%

profile of v8, /device:TPU:1, one launch (start us, length us, event | category | flops | bytes accessed | tf_op | source)
XLA Modules:
  0.0 199.8 jit_solution(18332378454625135589)
XLA Ops:
  0.6 1.7 make_requests.1.asked_ref
  2.4 9.6 %all-to-all-start = ((s32[32,1,2]{2,1,0:T(1,128)}), s32[32,1,2]{2,1,0:T(1,128)S(1)}, u32[]{:S(2)}, u32[]{:S(2)}) async-start(s32[32,1,2]{2,1,0:T(1,128)} %bitcast.37), calls=%async_computation | async-start | bytes 32768 | tf_op jit(solution)/shard_map/all_to_all | solution.py:513
  12.0 4.3 %qkv.1 = (bf16[2048,128]{1,0:T(8,128)(2,1)}, bf16[16,128,256]{2,1,0:T(8,128)(2,1)}) custom-call(bf16[2048,512]{1,0:T(8,128)(2,1)} %x_ref.5, bf16[3,512,128]{2,1,0:T(8,128)(2,1)} %w_ref.1, f32[2]{0:T(128)} %scale_ref.1), custom_call_target="tpu_custom_call" | custom-call | flops 805306368 | bytes 3670016 | tf_op jit(solution)/shard_map/qkv/pallas_call | solution.py:60
  16.3 2.6 %all-to-all-done.wanted_ref = s32[32,1,2]{2,1,0:T(1,128)S(1)} async-done(((s32[32,1,2]{2,1,0:T(1,128)}), s32[32,1,2]{2,1,0:T(1,128)S(1)}, u32[]{:S(2)}, u32[]{:S(2)}) %all-to-all-start) | async-done | bytes 288 | tf_op jit(solution)/shard_map/all_to_all | solution.py:513
  18.9 0.0 copy-start.4
  18.9 0.6 copy-done.4
  19.5 3.8 %pick_blocks.1._ = bf16[64,128,256]{2,1,0:T(8,128)(2,1)} custom-call(s32[32,1,2]{2,1,0:T(1,128)} %copy-done.4, bf16[16,128,256]{2,1,0:T(8,128)(2,1)} %get-tuple-element.20.kv_ref), custom_call_target="tpu_custom_call" | custom-call | bytes 8388608 | tf_op jit(solution)/shard_map/pick_blocks/pallas_call | solution.py:156
  23.4 5.1 %all-to-all-start.1 = ((bf16[64,128,256]{2,1,0:T(8,128)(2,1)}), bf16[64,128,256]{2,1,0:T(8,128)(2,1)}, u32[]{:S(2)}, u32[]{:S(2)}) async-start(bf16[64,128,256]{2,1,0:T(8,128)(2,1)} %pick_blocks.1._), calls=%async_computation.1 | async-start | bytes 8388608 | tf_op jit(solution)/shard_map/all_to_all | solution.py:513
  28.5 0.0 copy-start.5
  28.5 3.7 %split_weights.1 = (bf16[1664,512]{1,0:T(8,128)(2,1)}, bf16[1664,512]{1,0:T(8,128)(2,1)}) custom-call(s32[1]{0:T(128)} %bitcast.3.me_ref, bf16[2,512,512]{2,1,0:T(8,128)(2,1)} %gate_ref.1, bf16[2,512,512]{2,1,0:T(8,128)(2,1)} %up_ref.1, bf16[2,512,512]{2,1,0:T(8,128)(2,1)} %down_ref.1, bf16[128,512]{1,0:T(8,128)(2,1)} %out_w_ref.1, ...), custom_call_target="tpu_custom_call" | custom-call | bytes 6815744 | tf_op jit(solution)/shard_map/split_weights/pallas_call | solution.py:127
  32.2 1.3 collective-permute-start
  33.5 0.0 copy-done.5
  33.5 1.7 fusion.2
  35.2 0.7 compare_select_fusion
  35.9 2.4 %collective-permute-start.1 = (bf16[1664,512]{1,0:T(8,128)(2,1)}, bf16[1664,512]{1,0:T(8,128)(2,1)S(1)}, u32[]{:S(2)}, u32[]{:S(2)}) collective-permute-start(bf16[1664,512]{1,0:T(8,128)(2,1)} %get-tuple-element.25), channel_id=1, source_target_pairs={{0,2},{1,3},{2,0},{3,1},{4,6},{5,7},{6,4},{7,5},{8,10},{9,11},{10,... | collective-permute-start | bytes 5111816 | tf_op jit(solution)/shard_map/ppermute | solution.py:509
  38.3 0.2 collective-permute-start.2
  38.5 7.4 %place_rows.1 = bf16[32,48,512]{2,1,0:T(8,128)(2,1)} custom-call(s32[1,2048]{1,0:T(1,128)} %get-tuple-element.36.spot_ref, bf16[2048,512]{1,0:T(8,128)(2,1)} %x_ref.5), custom_call_target="tpu_custom_call" | custom-call | flops 3221225472 | bytes 4194304 | tf_op jit(solution)/shard_map/place_rows/pallas_call | solution.py:271
  45.9 32.9 %all-to-all-done.1.halo_ref = bf16[64,128,256]{2,1,0:T(8,128)(2,1)} async-done(((bf16[64,128,256]{2,1,0:T(8,128)(2,1)}), bf16[64,128,256]{2,1,0:T(8,128)(2,1)}, u32[]{:S(2)}, u32[]{:S(2)}) %all-to-all-start.1) | async-done | bytes 4194336 | tf_op jit(solution)/shard_map/all_to_all | solution.py:513
  78.8 7.8 %all-to-all-start.2 = ((bf16[32,48,512]{2,1,0:T(8,128)(2,1)}), bf16[32,48,512]{2,1,0:T(8,128)(2,1)}, u32[]{:S(2)}, u32[]{:S(2)}) async-start(bf16[32,48,512]{2,1,0:T(8,128)(2,1)} %place_rows.1), calls=%async_computation.2 | async-start | bytes 3145728 | tf_op jit(solution)/shard_map/all_to_all | solution.py:513
  86.7 1.3 bitcast_convert_fusion.route_ref
  88.0 0.0 collective-permute-done.rest_0_.w1_ref
  88.0 0.0 copy-start
  88.0 1.2 copy-done
  89.2 19.8 %attention.1 = (bf16[2048,128]{1,0:T(8,128)(2,1)}, bf16[32,4,48,128]{3,2,1,0:T(8,128)(2,1)}) custom-call(s32[16,12]{1,0:T(8,128)} %near_ref.3, s32[32,2]{1,0:T(8,128)} %make_requests.1.asked_ref, bf16[2048,128]{1,0:T(8,128)(2,1)} %get-tuple-element.19.q_ref, bf16[16,128,256]{2,1,0:T(8,128)(2,1)} %get-tuple-element.20.kv_ref, ...), custom_call_target="tpu_custom_call" | custom-call | flops 12000000000 | bytes 8388608 | tf_op jit(solution)/shard_map/attention/pallas_call | solution.py:235
  109.0 0.0 all-to-all-done.2.x_ref
  109.0 9.4 %all-to-all-start.3 = ((bf16[128,48,128]{2,1,0:T(8,128)(2,1)}), bf16[128,48,128]{2,1,0:T(8,128)(2,1)S(1)}, u32[]{:S(2)}, u32[]{:S(2)}) async-start(bf16[128,48,128]{2,1,0:T(8,128)(2,1)} %bitcast.36), calls=%async_computation.3 | async-start | bytes 3145728 | tf_op jit(solution)/shard_map/all_to_all | solution.py:513
  118.4 0.0 collective-permute-done.1.rest_1_.w2_ref
  118.4 0.0 copy-start.1
  118.4 0.0 collective-permute-done.2.rest_2_.w3_ref
  118.4 1.2 copy-done.1
  119.6 1.3 hold_route.1.route_ref
  120.9 22.7 %all-to-all-done.3 = bf16[128,48,128]{2,1,0:T(8,128)(2,1)S(1)} async-done(((bf16[128,48,128]{2,1,0:T(8,128)(2,1)}), bf16[128,48,128]{2,1,0:T(8,128)(2,1)S(1)}, u32[]{:S(2)}, u32[]{:S(2)}) %all-to-all-start.3) | async-done | bytes 1572896 | tf_op jit(solution)/shard_map/all_to_all | solution.py:513
  143.6 0.0 copy-start.3
  143.6 0.3 collective-permute-start.3
  143.9 0.4 collective-permute-start.4
  144.3 0.5 copy-done.3
  144.8 15.6 %experts.1 = bf16[32,4,48,128]{3,2,1,0:T(8,128)(2,1)} custom-call(s32[1]{0:T(128)} %bitcast.3.me_ref, f32[1,512]{1,0:T(1,128)} %bitcast.40, f32[1,512]{1,0:T(1,128)} %hold_route.1.route_ref, bf16[32,4,48,128]{3,2,1,0:T(8,128)(2,1)} %bitcast.35, bf16[32,48,512]{2,1,0:T(8,128)(2,1)} %all-to-all-done.2.x_ref, bf16[1664,512]{1,0:T(8,128)(2,1)} %get-tuple-element.21.w0_ref, ...), custom_call_target="tpu_custom_call" | custom-call | flops 10468982784 | bytes 12582912 | tf_op jit(solution)/shard_map/experts/pallas_call | solution.py:369
  160.4 0.0 collective-permute-done.3.h1_ref
  160.5 0.0 collective-permute-done.4.h3_ref
  160.5 5.2 %all-to-all-start.4 = ((bf16[128,48,128]{2,1,0:T(8,128)(2,1)}), bf16[128,48,128]{2,1,0:T(8,128)(2,1)S(1)}, u32[]{:S(2)}, u32[]{:S(2)}) async-start(bf16[128,48,128]{2,1,0:T(8,128)(2,1)} %bitcast.34), calls=%async_computation.4 | async-start | bytes 3145728 | tf_op jit(solution)/shard_map/all_to_all | solution.py:513
  165.7 1.0 slice.6
  166.6 1.5 collective-permute-start.5
  168.1 1.0 slice.7
  169.1 2.1 %collective-permute-start.6 = (bf16[1024,128]{1,0:T(8,128)(2,1)S(1)}, bf16[1024,128]{1,0:T(8,128)(2,1)S(1)}, u32[]{:S(2)}, u32[]{:S(2)}) collective-permute-start(bf16[1024,128]{1,0:T(8,128)(2,1)S(1)} %slice.7), channel_id=1, source_target_pairs={{0,3},{1,2},{2,1},{3,0},{4,7},{5,6},{6,5},{7,4},{8,11},{9,10},{10,... | collective-permute-start | bytes 786440 | tf_op jit(solution)/shard_map/ppermute | solution.py:509
  171.2 3.8 %attention_columns.1 = (f32[2048,128]{1,0:T(8,128)}, bf16[2048,128]{1,0:T(8,128)(2,1)}, bf16[128,128]{1,0:T(8,128)(2,1)}) custom-call(s32[1]{0:T(128)} %bitcast.3.me_ref, bf16[2048,128]{1,0:T(8,128)(2,1)} %get-tuple-element.26.h0_ref, bf16[2048,128]{1,0:T(8,128)(2,1)} %collective-permute-done.3.h1_ref, bf16[2048,128]{1,0:T(8,128)(2,1)} %collective-permute-done.4.h3_ref, ...), custom_call_target="tpu_custom_call" | custom-call | flops 268435456 | bytes 8388608 | tf_op jit(solution)/shard_map/attention_columns/pallas_call | solution.py:407
  175.0 14.7 %collective-permute-done.5.top_hbm = bf16[1024,128]{1,0:T(8,128)(2,1)S(1)} collective-permute-done((bf16[1024,128]{1,0:T(8,128)(2,1)S(1)}, bf16[1024,128]{1,0:T(8,128)(2,1)S(1)}, u32[]{:S(2)}, u32[]{:S(2)}) %collective-permute-start.5) | collective-permute-done | bytes 262176 | tf_op jit(solution)/shard_map/ppermute | solution.py:509
  189.6 0.0 copy-start.6
  189.6 1.2 collective-permute-done.6.bottom_hbm
  190.8 0.0 copy-start.7
  190.8 0.5 all-to-all-done.4
  191.3 0.0 copy-start.2
  191.3 0.0 copy-done.6
  191.3 0.2 copy-done.7
  191.6 0.9 copy-done.2
  192.5 7.1 %combine.1 = (bf16[2048,128]{1,0:T(8,128)(2,1)}, bf16[2048,128]{1,0:T(8,128)(2,1)}) custom-call(s32[1,2048]{1,0:T(1,128)} %get-tuple-element.38.spot_ref, s32[1,2048]{1,0:T(1,128)} %get-tuple-element.37.lane_ref, bf16[128,128]{1,0:T(8,128)(2,1)} %get-tuple-element.32.last_ref, f32[2048,128]{1,0:T(8,128)} %get-tuple-element.33.part_hbm, ...), custom_call_target="tpu_custom_call" | custom-call | flops 3221225472 | bytes 4194304 | tf_op jit(solution)/shard_map/combine/pallas_call | solution.py:488
  (1 shorter events, 0.0 us)
Async XLA Ops:
  2.4 16.5 %all-to-all-start = ((s32[32,1,2]{2,1,0:T(1,128)}), s32[32,1,2]{2,1,0:T(1,128)S(1)}, u32[]{:S(2)}, u32[]{:S(2)}) async-start(s32[32,1,2]{2,1,0:T(1,128)} %bitcast.37), calls=%async_computation | async-start | bytes 32768 | tf_op jit(solution)/shard_map/all_to_all | solution.py:513
  18.9 0.6 copy-start.4
  23.4 55.5 %all-to-all-start.1 = ((bf16[64,128,256]{2,1,0:T(8,128)(2,1)}), bf16[64,128,256]{2,1,0:T(8,128)(2,1)}, u32[]{:S(2)}, u32[]{:S(2)}) async-start(bf16[64,128,256]{2,1,0:T(8,128)(2,1)} %pick_blocks.1._), calls=%async_computation.1 | async-start | bytes 8388608 | tf_op jit(solution)/shard_map/all_to_all | solution.py:513
  28.5 5.0 %copy-start.5 = (s32[2048,1]{0,1:T(1,128)S(1)}, s32[2048,1]{0,1:T(1,128)}, u32[]{:S(2)}) copy-start(s32[2048,1]{0,1:T(1,128)} %param.21) | copy-start | bytes 24580
  32.2 55.8 %collective-permute-start = (bf16[1664,512]{1,0:T(8,128)(2,1)}, bf16[1664,512]{1,0:T(8,128)(2,1)S(1)}, u32[]{:S(2)}, u32[]{:S(2)}) collective-permute-start(bf16[1664,512]{1,0:T(8,128)(2,1)} %get-tuple-element.21.w0_ref), channel_id=1, source_target_pairs={{0,1},{1,0},{2,3},{3,2},{4,5},{5,4},{6,7},{7,6},{8,9},{9,8},{10,11... | collective-permute-start | bytes 5111816 | tf_op jit(solution)/shard_map/ppermute | solution.py:509
  35.9 82.5 %collective-permute-start.1 = (bf16[1664,512]{1,0:T(8,128)(2,1)}, bf16[1664,512]{1,0:T(8,128)(2,1)S(1)}, u32[]{:S(2)}, u32[]{:S(2)}) collective-permute-start(bf16[1664,512]{1,0:T(8,128)(2,1)} %get-tuple-element.25), channel_id=1, source_target_pairs={{0,2},{1,3},{2,0},{3,1},{4,6},{5,7},{6,4},{7,5},{8,10},{9,11},{10,... | collective-permute-start | bytes 5111816 | tf_op jit(solution)/shard_map/ppermute | solution.py:509
  38.3 80.1 %collective-permute-start.2 = (bf16[1664,512]{1,0:T(8,128)(2,1)}, bf16[1664,512]{1,0:T(8,128)(2,1)}, u32[]{:S(2)}, u32[]{:S(2)}) collective-permute-start(bf16[1664,512]{1,0:T(8,128)(2,1)} %get-tuple-element.25), channel_id=1, source_target_pairs={{0,3},{1,2},{2,1},{3,0},{4,7},{5,6},{6,5},{7,4},{8,11},{9,10},{10,... | collective-permute-start | bytes 5111816 | tf_op jit(solution)/shard_map/ppermute | solution.py:509
  78.8 30.2 %all-to-all-start.2 = ((bf16[32,48,512]{2,1,0:T(8,128)(2,1)}), bf16[32,48,512]{2,1,0:T(8,128)(2,1)}, u32[]{:S(2)}, u32[]{:S(2)}) async-start(bf16[32,48,512]{2,1,0:T(8,128)(2,1)} %place_rows.1), calls=%async_computation.2 | async-start | bytes 3145728 | tf_op jit(solution)/shard_map/all_to_all | solution.py:513
  88.0 1.2 copy-start
  109.0 34.6 %all-to-all-start.3 = ((bf16[128,48,128]{2,1,0:T(8,128)(2,1)}), bf16[128,48,128]{2,1,0:T(8,128)(2,1)S(1)}, u32[]{:S(2)}, u32[]{:S(2)}) async-start(bf16[128,48,128]{2,1,0:T(8,128)(2,1)} %bitcast.36), calls=%async_computation.3 | async-start | bytes 3145728 | tf_op jit(solution)/shard_map/all_to_all | solution.py:513
  118.4 1.2 copy-start.1
  143.6 1.2 copy-start.3
  143.6 16.8 %collective-permute-start.3 = (bf16[2048,128]{1,0:T(8,128)(2,1)}, bf16[2048,128]{1,0:T(8,128)(2,1)}, u32[]{:S(2)}, u32[]{:S(2)}) collective-permute-start(bf16[2048,128]{1,0:T(8,128)(2,1)} %get-tuple-element.26.h0_ref), channel_id=1, source_target_pairs={{0,1},{1,0},{2,3},{3,2},{4,5},{5,4},{6,7},{7,6},{8,9},{9,8},{10,11... | collective-permute-start | bytes 1572872 | tf_op jit(solution)/shard_map/ppermute | solution.py:509
  143.9 16.5 %collective-permute-start.4 = (bf16[2048,128]{1,0:T(8,128)(2,1)}, bf16[2048,128]{1,0:T(8,128)(2,1)}, u32[]{:S(2)}, u32[]{:S(2)}) collective-permute-start(bf16[2048,128]{1,0:T(8,128)(2,1)} %get-tuple-element.26.h0_ref), channel_id=1, source_target_pairs={{0,3},{1,2},{2,1},{3,0},{4,7},{5,6},{6,5},{7,4},{8,11},{9,10},{10,... | collective-permute-start | bytes 1572872 | tf_op jit(solution)/shard_map/ppermute | solution.py:509
  160.5 30.9 %all-to-all-start.4 = ((bf16[128,48,128]{2,1,0:T(8,128)(2,1)}), bf16[128,48,128]{2,1,0:T(8,128)(2,1)S(1)}, u32[]{:S(2)}, u32[]{:S(2)}) async-start(bf16[128,48,128]{2,1,0:T(8,128)(2,1)} %bitcast.34), calls=%async_computation.4 | async-start | bytes 3145728 | tf_op jit(solution)/shard_map/all_to_all | solution.py:513
  166.6 23.0 %collective-permute-start.5 = (bf16[1024,128]{1,0:T(8,128)(2,1)S(1)}, bf16[1024,128]{1,0:T(8,128)(2,1)S(1)}, u32[]{:S(2)}, u32[]{:S(2)}) collective-permute-start(bf16[1024,128]{1,0:T(8,128)(2,1)S(1)} %slice.6), channel_id=1, source_target_pairs={{0,1},{1,0},{2,3},{3,2},{4,5},{5,4},{6,7},{7,6},{8,9},{9,8},{10,11... | collective-permute-start | bytes 786440 | tf_op jit(solution)/shard_map/ppermute | solution.py:509
  169.1 21.8 %collective-permute-start.6 = (bf16[1024,128]{1,0:T(8,128)(2,1)S(1)}, bf16[1024,128]{1,0:T(8,128)(2,1)S(1)}, u32[]{:S(2)}, u32[]{:S(2)}) collective-permute-start(bf16[1024,128]{1,0:T(8,128)(2,1)S(1)} %slice.7), channel_id=1, source_target_pairs={{0,3},{1,2},{2,1},{3,0},{4,7},{5,6},{6,5},{7,4},{8,11},{9,10},{10,... | collective-permute-start | bytes 786440 | tf_op jit(solution)/shard_map/ppermute | solution.py:509
  189.6 1.7 copy-start.6
  190.8 0.7 copy-start.7
  191.3 1.2 copy-start.2

commit v9 on v8

--- a/solution.py
+++ b/solution.py
@@ -425,7 +425,7 @@
 
 
 def combine_kernel(
-    spot_ref, lane_ref, last_ref, part_hbm, kept_hbm, top_hbm, bottom_hbm, back_ref, attn_hbm, out_hbm,
+    spot_ref, lane_ref, last_ref, part_hbm, kept_hbm, h2_hbm, back_ref, attn_hbm, out_hbm,
     slots, part_ref, kept_ref, h2_ref, attn_ref, out_ref, sems
 ):
     dests, cap, width = slots.shape
@@ -436,12 +436,10 @@
         )
         for m in range(4)
     ]
-    half = rows // 2
     for source, target in (
         (part_hbm, part_ref),
         (kept_hbm, kept_ref),
-        (top_hbm, h2_ref.at[pl.ds(0, half)]),
-        (bottom_hbm, h2_ref.at[pl.ds(half, half)]),
+        (h2_hbm, h2_ref),
     ):
         copies.append(pltpu.make_async_copy(source, target, sems.at[len(copies)]))
     for copy in copies:
@@ -487,7 +485,7 @@
     out = jax.ShapeDtypeStruct((rows, LANES), BF16)
     return pl.pallas_call(
         combine_kernel,
-        in_specs=[VMEM] * 3 + [HBM] * 5,
+        in_specs=[VMEM] * 3 + [HBM] * 4,
         out_specs=[HBM, HBM],
         out_shape=[out, out],
         scratch_shapes=[
@@ -502,7 +500,7 @@
         compiler_params=params(60),
         cost_estimate=cost(2 * rows * slots * 4 * LANES, 4 * 2**20),
         name="combine",
-    )(spot_row, lane_row, last, part, kept, *relayed, back)
+    )(spot_row, lane_row, last, part, kept, relayed, back)
 
 
 def swap(array, change):
@@ -576,8 +574,7 @@
         (),
     )
     produced, by_one, by_three = lax.optimization_barrier((produced, by_one, by_three))
-    middle = rows // 2
-    relayed = [swap(by_three[:middle], 1), swap(by_one[middle:], 3)]
+    relayed = swap(by_three, 1)
     part, kept_columns, last = attention_columns(
         me_ref, heads, by_one, by_three, weights, node_features
     )

time: 201 us -> 205 us (1.020)
  waiting for transfers between devices: 74.7 us -> 82.5 us
    ppermute x7 -> x6, waiting for transfers between devices: 15.9 us -> 24.1 us  [swap(): return lax.ppermute(array, 'mp', [(i, i ^ change) for i in range(4)])]
    ppermute x7 -> x6, starting transfers between devices: 8.16 us -> 6.29 us  [swap(): return lax.ppermute(array, 'mp', [(i, i ^ change) for i in range(4)])]
    unnamed x16 -> x14, local copies, waits for them, and re-layouts: 4.68 us -> 4.81 us
  transfers between devices with their start and end apart: 12 -> 11, of which waited for: 6 -> 4; matrix products, arithmetic and copies ran while one was open for 3% -> 2% of each run, Pallas kernels for 28% -> 27%
where the time goes in v9:
time: 205 us; the launch traced here: 204 us
  waiting for transfers between devices  82.5 us (40%)
  Pallas kernels  68.6 us (33%)
  starting transfers between devices  43.4 us (21%)
  local copies, waits for them, and re-layouts  4.81 us (2%)
    all_to_all x5, waiting for transfers between devices, exchange(): return lax.all_to_all(array, axes, split_axis=0, concat_axis=0, tiled=True)  58.3 us
    all_to_all x5, starting transfers between devices, exchange(): return lax.all_to_all(array, axes, split_axis=0, concat_axis=0, tiled=True)  37.1 us
    ppermute x6, waiting for transfers between devices, swap(): return lax.ppermute(array, 'mp', [(i, i ^ change) for i in range(4)])  24.1 us
    pallas_call x1, Pallas kernels, attention(): pl.pallas_call(attention_kernel, in_specs=[SMEM, SMEM, VMEM, VMEM, VMEM,...  19.8 us
    pallas_call x1, Pallas kernels, experts(): pl.pallas_call(experts_kernel, in_specs=[SMEM, VMEM, VMEM, HBM, HBM] + [A...  15.6 us
    pallas_call x1, Pallas kernels, place_rows(): pl.pallas_call(place_kernel, in_specs=[VMEM, VMEM], out_specs=VMEM, out_s...  7.4 us
    pallas_call x1, Pallas kernels, combine(): pl.pallas_call(combine_kernel, in_specs=[VMEM] * 3 + [HBM] * 4, out_specs...  7.12 us
    ppermute x6, starting transfers between devices, swap(): return lax.ppermute(array, 'mp', [(i, i ^ change) for i in range(4)])  6.29 us
  transfers between devices with their start and end apart: 11, of which 4 were waited for; matrix products, arithmetic and copies ran while one was open for 2% of the time, Pallas kernels for 27%

profile of v9, /device:TPU:1, one launch (start us, length us, event | category | flops | bytes accessed | tf_op | source)
XLA Modules:
  0.0 203.9 jit_solution(10198925825606657668)
XLA Ops:
  0.6 1.7 make_requests.1.asked_ref
  2.4 9.6 %all-to-all-start = ((s32[32,1,2]{2,1,0:T(1,128)}), s32[32,1,2]{2,1,0:T(1,128)S(1)}, u32[]{:S(2)}, u32[]{:S(2)}) async-start(s32[32,1,2]{2,1,0:T(1,128)} %bitcast.37), calls=%async_computation | async-start | bytes 32768 | tf_op jit(solution)/shard_map/all_to_all | solution.py:511
  12.0 4.3 %qkv.1 = (bf16[2048,128]{1,0:T(8,128)(2,1)}, bf16[16,128,256]{2,1,0:T(8,128)(2,1)}) custom-call(bf16[2048,512]{1,0:T(8,128)(2,1)} %x_ref.5, bf16[3,512,128]{2,1,0:T(8,128)(2,1)} %w_ref.1, f32[2]{0:T(128)} %scale_ref.1), custom_call_target="tpu_custom_call" | custom-call | flops 805306368 | bytes 3670016 | tf_op jit(solution)/shard_map/qkv/pallas_call | solution.py:60
  16.3 2.6 %all-to-all-done.wanted_ref = s32[32,1,2]{2,1,0:T(1,128)S(1)} async-done(((s32[32,1,2]{2,1,0:T(1,128)}), s32[32,1,2]{2,1,0:T(1,128)S(1)}, u32[]{:S(2)}, u32[]{:S(2)}) %all-to-all-start) | async-done | bytes 288 | tf_op jit(solution)/shard_map/all_to_all | solution.py:511
  18.9 0.0 copy-start.4
  18.9 0.6 copy-done.4
  19.5 3.8 %pick_blocks.1._ = bf16[64,128,256]{2,1,0:T(8,128)(2,1)} custom-call(s32[32,1,2]{2,1,0:T(1,128)} %copy-done.4, bf16[16,128,256]{2,1,0:T(8,128)(2,1)} %get-tuple-element.20.kv_ref), custom_call_target="tpu_custom_call" | custom-call | bytes 8388608 | tf_op jit(solution)/shard_map/pick_blocks/pallas_call | solution.py:156
  23.3 5.1 %all-to-all-start.1 = ((bf16[64,128,256]{2,1,0:T(8,128)(2,1)}), bf16[64,128,256]{2,1,0:T(8,128)(2,1)}, u32[]{:S(2)}, u32[]{:S(2)}) async-start(bf16[64,128,256]{2,1,0:T(8,128)(2,1)} %pick_blocks.1._), calls=%async_computation.1 | async-start | bytes 8388608 | tf_op jit(solution)/shard_map/all_to_all | solution.py:511
  28.4 0.0 copy-start.5
  28.5 3.7 %split_weights.1 = (bf16[1664,512]{1,0:T(8,128)(2,1)}, bf16[1664,512]{1,0:T(8,128)(2,1)}) custom-call(s32[1]{0:T(128)} %bitcast.3.me_ref, bf16[2,512,512]{2,1,0:T(8,128)(2,1)} %gate_ref.1, bf16[2,512,512]{2,1,0:T(8,128)(2,1)} %up_ref.1, bf16[2,512,512]{2,1,0:T(8,128)(2,1)} %down_ref.1, bf16[128,512]{1,0:T(8,128)(2,1)} %out_w_ref.1, ...), custom_call_target="tpu_custom_call" | custom-call | bytes 6815744 | tf_op jit(solution)/shard_map/split_weights/pallas_call | solution.py:127
  32.2 1.3 collective-permute-start
  33.5 0.0 copy-done.5
  33.5 1.7 fusion.2
  35.2 0.7 compare_select_fusion
  35.9 2.4 %collective-permute-start.1 = (bf16[1664,512]{1,0:T(8,128)(2,1)}, bf16[1664,512]{1,0:T(8,128)(2,1)S(1)}, u32[]{:S(2)}, u32[]{:S(2)}) collective-permute-start(bf16[1664,512]{1,0:T(8,128)(2,1)} %get-tuple-element.25), channel_id=1, source_target_pairs={{0,2},{1,3},{2,0},{3,1},{4,6},{5,7},{6,4},{7,5},{8,10},{9,11},{10,... | collective-permute-start | bytes 5111816 | tf_op jit(solution)/shard_map/ppermute | solution.py:507
  38.3 0.2 collective-permute-start.2
  38.5 7.4 %place_rows.1 = bf16[32,48,512]{2,1,0:T(8,128)(2,1)} custom-call(s32[1,2048]{1,0:T(1,128)} %get-tuple-element.36.spot_ref, bf16[2048,512]{1,0:T(8,128)(2,1)} %x_ref.5), custom_call_target="tpu_custom_call" | custom-call | flops 3221225472 | bytes 4194304 | tf_op jit(solution)/shard_map/place_rows/pallas_call | solution.py:271
  45.9 32.9 %all-to-all-done.1.halo_ref = bf16[64,128,256]{2,1,0:T(8,128)(2,1)} async-done(((bf16[64,128,256]{2,1,0:T(8,128)(2,1)}), bf16[64,128,256]{2,1,0:T(8,128)(2,1)}, u32[]{:S(2)}, u32[]{:S(2)}) %all-to-all-start.1) | async-done | bytes 4194336 | tf_op jit(solution)/shard_map/all_to_all | solution.py:511
  78.8 7.8 %all-to-all-start.2 = ((bf16[32,48,512]{2,1,0:T(8,128)(2,1)}), bf16[32,48,512]{2,1,0:T(8,128)(2,1)}, u32[]{:S(2)}, u32[]{:S(2)}) async-start(bf16[32,48,512]{2,1,0:T(8,128)(2,1)} %place_rows.1), calls=%async_computation.2 | async-start | bytes 3145728 | tf_op jit(solution)/shard_map/all_to_all | solution.py:511
  86.7 1.3 bitcast_convert_fusion.route_ref
  87.9 0.0 collective-permute-done.rest_0_.w1_ref
  88.0 0.0 copy-start
  88.0 1.2 copy-done
  89.2 19.8 %attention.1 = (bf16[2048,128]{1,0:T(8,128)(2,1)}, bf16[32,4,48,128]{3,2,1,0:T(8,128)(2,1)}) custom-call(s32[16,12]{1,0:T(8,128)} %near_ref.3, s32[32,2]{1,0:T(8,128)} %make_requests.1.asked_ref, bf16[2048,128]{1,0:T(8,128)(2,1)} %get-tuple-element.19.q_ref, bf16[16,128,256]{2,1,0:T(8,128)(2,1)} %get-tuple-element.20.kv_ref, ...), custom_call_target="tpu_custom_call" | custom-call | flops 12000000000 | bytes 8388608 | tf_op jit(solution)/shard_map/attention/pallas_call | solution.py:235
  109.0 0.0 all-to-all-done.2.x_ref
  109.0 9.4 %all-to-all-start.3 = ((bf16[128,48,128]{2,1,0:T(8,128)(2,1)}), bf16[128,48,128]{2,1,0:T(8,128)(2,1)S(1)}, u32[]{:S(2)}, u32[]{:S(2)}) async-start(bf16[128,48,128]{2,1,0:T(8,128)(2,1)} %bitcast.36), calls=%async_computation.3 | async-start | bytes 3145728 | tf_op jit(solution)/shard_map/all_to_all | solution.py:511
  118.4 0.0 collective-permute-done.1.rest_1_.w2_ref
  118.4 0.0 copy-start.1
  118.4 0.0 collective-permute-done.2.rest_2_.w3_ref
  118.4 1.2 copy-done.1
  119.6 1.2 hold_route.1.route_ref
  120.8 22.8 %all-to-all-done.3 = bf16[128,48,128]{2,1,0:T(8,128)(2,1)S(1)} async-done(((bf16[128,48,128]{2,1,0:T(8,128)(2,1)}), bf16[128,48,128]{2,1,0:T(8,128)(2,1)S(1)}, u32[]{:S(2)}, u32[]{:S(2)}) %all-to-all-start.3) | async-done | bytes 1572896 | tf_op jit(solution)/shard_map/all_to_all | solution.py:511
  143.6 0.0 copy-start.3
  143.6 0.3 collective-permute-start.3
  143.9 0.4 collective-permute-start.4
  144.3 0.5 copy-done.3
  144.8 15.6 %experts.1 = bf16[32,4,48,128]{3,2,1,0:T(8,128)(2,1)} custom-call(s32[1]{0:T(128)} %bitcast.3.me_ref, f32[1,512]{1,0:T(1,128)} %bitcast.40, f32[1,512]{1,0:T(1,128)} %hold_route.1.route_ref, bf16[32,4,48,128]{3,2,1,0:T(8,128)(2,1)} %bitcast.35, bf16[32,48,512]{2,1,0:T(8,128)(2,1)} %all-to-all-done.2.x_ref, bf16[1664,512]{1,0:T(8,128)(2,1)} %get-tuple-element.21.w0_ref, ...), custom_call_target="tpu_custom_call" | custom-call | flops 10468982784 | bytes 12582912 | tf_op jit(solution)/shard_map/experts/pallas_call | solution.py:369
  160.4 0.0 collective-permute-done.3.h1_ref
  160.4 0.0 collective-permute-done.4.h3_ref
  160.4 5.2 %all-to-all-start.4 = ((bf16[128,48,128]{2,1,0:T(8,128)(2,1)}), bf16[128,48,128]{2,1,0:T(8,128)(2,1)S(1)}, u32[]{:S(2)}, u32[]{:S(2)}) async-start(bf16[128,48,128]{2,1,0:T(8,128)(2,1)} %bitcast.34), calls=%async_computation.4 | async-start | bytes 3145728 | tf_op jit(solution)/shard_map/all_to_all | solution.py:511
  165.7 1.7 collective-permute-start.5
  167.3 3.8 %attention_columns.1 = (f32[2048,128]{1,0:T(8,128)}, bf16[2048,128]{1,0:T(8,128)(2,1)}, bf16[128,128]{1,0:T(8,128)(2,1)}) custom-call(s32[1]{0:T(128)} %bitcast.3.me_ref, bf16[2048,128]{1,0:T(8,128)(2,1)} %get-tuple-element.26.h0_ref, bf16[2048,128]{1,0:T(8,128)(2,1)} %collective-permute-done.3.h1_ref, bf16[2048,128]{1,0:T(8,128)(2,1)} %collective-permute-done.4.h3_ref, ...), custom_call_target="tpu_custom_call" | custom-call | flops 268435456 | bytes 8388608 | tf_op jit(solution)/shard_map/attention_columns/pallas_call | solution.py:407
  171.1 24.1 %collective-permute-done.5.h2_hbm = bf16[2048,128]{1,0:T(8,128)(2,1)S(1)} collective-permute-done((bf16[2048,128]{1,0:T(8,128)(2,1)}, bf16[2048,128]{1,0:T(8,128)(2,1)S(1)}, u32[]{:S(2)}, u32[]{:S(2)}) %collective-permute-start.5) | collective-permute-done | bytes 524320 | tf_op jit(solution)/shard_map/ppermute | solution.py:507
  195.2 0.0 copy-start.6
  195.2 0.0 all-to-all-done.4
  195.2 0.0 copy-start.2
  195.2 0.8 copy-done.6
  196.1 0.5 copy-done.2
  196.6 7.1 %combine.1 = (bf16[2048,128]{1,0:T(8,128)(2,1)}, bf16[2048,128]{1,0:T(8,128)(2,1)}) custom-call(s32[1,2048]{1,0:T(1,128)} %get-tuple-element.38.spot_ref, s32[1,2048]{1,0:T(1,128)} %get-tuple-element.37.lane_ref, bf16[128,128]{1,0:T(8,128)(2,1)} %get-tuple-element.32.last_ref, f32[2048,128]{1,0:T(8,128)} %get-tuple-element.33.part_hbm, ...), custom_call_target="tpu_custom_call" | custom-call | flops 3221225472 | bytes 4194304 | tf_op jit(solution)/shard_map/combine/pallas_call | solution.py:486
  (1 shorter events, 0.0 us)
Async XLA Ops:
  2.4 16.5 %all-to-all-start = ((s32[32,1,2]{2,1,0:T(1,128)}), s32[32,1,2]{2,1,0:T(1,128)S(1)}, u32[]{:S(2)}, u32[]{:S(2)}) async-start(s32[32,1,2]{2,1,0:T(1,128)} %bitcast.37), calls=%async_computation | async-start | bytes 32768 | tf_op jit(solution)/shard_map/all_to_all | solution.py:511
  18.9 0.6 copy-start.4
  23.3 55.5 %all-to-all-start.1 = ((bf16[64,128,256]{2,1,0:T(8,128)(2,1)}), bf16[64,128,256]{2,1,0:T(8,128)(2,1)}, u32[]{:S(2)}, u32[]{:S(2)}) async-start(bf16[64,128,256]{2,1,0:T(8,128)(2,1)} %pick_blocks.1._), calls=%async_computation.1 | async-start | bytes 8388608 | tf_op jit(solution)/shard_map/all_to_all | solution.py:511
  28.4 5.0 %copy-start.5 = (s32[2048,1]{0,1:T(1,128)S(1)}, s32[2048,1]{0,1:T(1,128)}, u32[]{:S(2)}) copy-start(s32[2048,1]{0,1:T(1,128)} %param.21) | copy-start | bytes 24580
  32.2 55.8 %collective-permute-start = (bf16[1664,512]{1,0:T(8,128)(2,1)}, bf16[1664,512]{1,0:T(8,128)(2,1)S(1)}, u32[]{:S(2)}, u32[]{:S(2)}) collective-permute-start(bf16[1664,512]{1,0:T(8,128)(2,1)} %get-tuple-element.21.w0_ref), channel_id=1, source_target_pairs={{0,1},{1,0},{2,3},{3,2},{4,5},{5,4},{6,7},{7,6},{8,9},{9,8},{10,11... | collective-permute-start | bytes 5111816 | tf_op jit(solution)/shard_map/ppermute | solution.py:507
  35.9 82.5 %collective-permute-start.1 = (bf16[1664,512]{1,0:T(8,128)(2,1)}, bf16[1664,512]{1,0:T(8,128)(2,1)S(1)}, u32[]{:S(2)}, u32[]{:S(2)}) collective-permute-start(bf16[1664,512]{1,0:T(8,128)(2,1)} %get-tuple-element.25), channel_id=1, source_target_pairs={{0,2},{1,3},{2,0},{3,1},{4,6},{5,7},{6,4},{7,5},{8,10},{9,11},{10,... | collective-permute-start | bytes 5111816 | tf_op jit(solution)/shard_map/ppermute | solution.py:507
  38.3 80.1 %collective-permute-start.2 = (bf16[1664,512]{1,0:T(8,128)(2,1)}, bf16[1664,512]{1,0:T(8,128)(2,1)}, u32[]{:S(2)}, u32[]{:S(2)}) collective-permute-start(bf16[1664,512]{1,0:T(8,128)(2,1)} %get-tuple-element.25), channel_id=1, source_target_pairs={{0,3},{1,2},{2,1},{3,0},{4,7},{5,6},{6,5},{7,4},{8,11},{9,10},{10,... | collective-permute-start | bytes 5111816 | tf_op jit(solution)/shard_map/ppermute | solution.py:507
  78.8 30.2 %all-to-all-start.2 = ((bf16[32,48,512]{2,1,0:T(8,128)(2,1)}), bf16[32,48,512]{2,1,0:T(8,128)(2,1)}, u32[]{:S(2)}, u32[]{:S(2)}) async-start(bf16[32,48,512]{2,1,0:T(8,128)(2,1)} %place_rows.1), calls=%async_computation.2 | async-start | bytes 3145728 | tf_op jit(solution)/shard_map/all_to_all | solution.py:511
  88.0 1.2 copy-start
  109.0 34.6 %all-to-all-start.3 = ((bf16[128,48,128]{2,1,0:T(8,128)(2,1)}), bf16[128,48,128]{2,1,0:T(8,128)(2,1)S(1)}, u32[]{:S(2)}, u32[]{:S(2)}) async-start(bf16[128,48,128]{2,1,0:T(8,128)(2,1)} %bitcast.36), calls=%async_computation.3 | async-start | bytes 3145728 | tf_op jit(solution)/shard_map/all_to_all | solution.py:511
  118.4 1.2 copy-start.1
  143.6 1.2 copy-start.3
  143.6 16.8 %collective-permute-start.3 = (bf16[2048,128]{1,0:T(8,128)(2,1)}, bf16[2048,128]{1,0:T(8,128)(2,1)}, u32[]{:S(2)}, u32[]{:S(2)}) collective-permute-start(bf16[2048,128]{1,0:T(8,128)(2,1)} %get-tuple-element.26.h0_ref), channel_id=1, source_target_pairs={{0,1},{1,0},{2,3},{3,2},{4,5},{5,4},{6,7},{7,6},{8,9},{9,8},{10,11... | collective-permute-start | bytes 1572872 | tf_op jit(solution)/shard_map/ppermute | solution.py:507
  143.9 16.5 %collective-permute-start.4 = (bf16[2048,128]{1,0:T(8,128)(2,1)}, bf16[2048,128]{1,0:T(8,128)(2,1)}, u32[]{:S(2)}, u32[]{:S(2)}) collective-permute-start(bf16[2048,128]{1,0:T(8,128)(2,1)} %get-tuple-element.26.h0_ref), channel_id=1, source_target_pairs={{0,3},{1,2},{2,1},{3,0},{4,7},{5,6},{6,5},{7,4},{8,11},{9,10},{10,... | collective-permute-start | bytes 1572872 | tf_op jit(solution)/shard_map/ppermute | solution.py:507
  160.4 34.8 %all-to-all-start.4 = ((bf16[128,48,128]{2,1,0:T(8,128)(2,1)}), bf16[128,48,128]{2,1,0:T(8,128)(2,1)S(1)}, u32[]{:S(2)}, u32[]{:S(2)}) async-start(bf16[128,48,128]{2,1,0:T(8,128)(2,1)} %bitcast.34), calls=%async_computation.4 | async-start | bytes 3145728 | tf_op jit(solution)/shard_map/all_to_all | solution.py:511
  165.7 29.6 %collective-permute-start.5 = (bf16[2048,128]{1,0:T(8,128)(2,1)}, bf16[2048,128]{1,0:T(8,128)(2,1)S(1)}, u32[]{:S(2)}, u32[]{:S(2)}) collective-permute-start(bf16[2048,128]{1,0:T(8,128)(2,1)} %collective-permute-done.4.h3_ref), channel_id=1, source_target_pairs={{0,1},{1,0},{2,3},{3,2},{4,5},{5,4},{6,7},{7,6},{8,9},{9,8},{10,11... | collective-permute-start | bytes 1572872 | tf_op jit(solution)/shard_map/ppermute | solution.py:507
  195.2 0.8 copy-start.6
  195.2 1.3 copy-start.2
